TPU v7x, 32 devices: a whole 2x2x4 slice. The times are simulated.
32 devices in a mesh: seq: 2 (over x), ctx: 4 (over z), mp: 4 (over y, core).
Axes of the slice: x: 2, y: 2, z: 4, core: 2. Of those that a mesh axis runs over, the one named last changes fastest.
Arguments:
- tokens: bfloat16 [5120, 1536], P(('seq', 'ctx')), may hold values from -6 to 6
- norm1_gain: float32 [1536], replicated, may hold values from 0.5 to 1.5
- w_query: bfloat16 [1536, 1536], P(None, 'mp'), may hold values from -0.15625 to 0.15625
- key_weight_matrix: bfloat16 [1536, 512], P(None, 'mp'), may hold values from -0.15625 to 0.15625
- value_weight_matrix: bfloat16 [1536, 512], P(None, 'mp'), may hold values from -0.15625 to 0.15625
- w_out: bfloat16 [1536, 1536], P('mp'), may hold values from -0.625 to 0.625
- norm2_gain: float32 [1536], replicated, may hold values from 0.5 to 1.5
- router: float32 [1536, 8], replicated, may hold values from -0.109375 to 0.109375
- w_gate: bfloat16 [8, 1536, 1024], P('mp'), may hold values from -0.15625 to 0.15625
- w_up: bfloat16 [8, 1536, 1024], P('mp'), may hold values from -0.15625 to 0.15625
- w_down: bfloat16 [8, 1024, 1536], P('mp'), may hold values from -0.1875 to 0.1875
- routes: int32 [5120, 2], P(('seq', 'ctx')), may hold values from 0 to 7, all different within a row; in each aligned block of 160 rows (0 to 159, 160 to 319, ...) at most 50 rows name the same one
- cotangent: bfloat16 [5120, 1536], P(('seq', 'ctx', 'mp')), may hold values from -6 to 6
Outputs:
- output: float32 [5120, 1536], P(('seq', 'ctx', 'mp'))
- grad_tokens: float32 [5120, 1536], P(('seq', 'ctx', 'mp'))
- grad_norm1: float32 [1536], replicated
- grad_query: float32 [1536, 1536], P(('seq', 'ctx'), 'mp')
- grad_key: float32 [1536, 512], P(('seq', 'ctx'), 'mp')
- grad_value: float32 [1536, 512], P(('seq', 'ctx'), 'mp')
- grad_out: float32 [1536, 1536], P('mp', ('seq', 'ctx'))
- grad_norm2: float32 [1536], replicated
- grad_router: float32 [1536, 8], replicated
- grad_gate: float32 [8, 1536, 1024], P('mp', ('seq', 'ctx'))
- grad_up: float32 [8, 1536, 1024], P('mp', ('seq', 'ctx'))
- grad_down: float32 [8, 1024, 1536], P('mp', ('seq', 'ctx'))
Inputs may be any that keep to these rules, and one draw needn't show every extreme that they name: `routes`: the two experts of a row differ. Rows are taken in aligned blocks of 160; within one block no expert is named more than 50 times, a bound that some block reaches.
All inputs are finite; a program needn't handle non-finite values.
Results may differ from a plain program's by a relative error of at most 0.02.
Values may be sent and summed in bfloat16 or wider, within the bound.
A program may use at most 192 MiB of HBM per device.

v0:
```python
import jax
import jax.numpy as jnp
from jax import lax
from jax.sharding import PartitionSpec as P

MODEL_WIDTH = 1536
HEAD_SIZE = 64


EPS = 1e-06


def rms_parts(rows):
    inverse = lax.rsqrt(jnp.mean(rows * rows, axis=-1, keepdims=True) + EPS)
    return (rows * inverse, inverse)


def rms_grad(grad_normed, normed, inverse):
    return inverse * (grad_normed - normed * jnp.mean(grad_normed * normed, axis=-1, keepdims=True))


def key_blocks():
    return 512


def body(
    tokens,
    norm1_gain,
    w_query,
    key_weight_matrix,
    value_weight_matrix,
    w_out,
    norm2_gain,
    router,
    w_gate,
    w_up,
    w_down,
    routes,
    cotangent,
):
    f32 = jnp.float32
    bf16 = jnp.bfloat16
    hp = lax.Precision.HIGHEST
    tok = tokens.shape[0]
    n_mp = lax.axis_size("mp")
    share = tok // n_mp
    mp_index = lax.axis_index("mp")
    ctx_index = lax.axis_index("ctx")
    head_dim = HEAD_SIZE
    kv_heads = key_weight_matrix.shape[1] // head_dim
    query_group = w_query.shape[1] // head_dim // kv_heads
    experts_all = router.shape[1]
    exp_local = w_gate.shape[0]
    top = routes.shape[1]
    cap = share * top * 5 // (4 * experts_all)
    xf = tokens.astype(f32)
    normed_one, inverse_one = rms_parts(xf)
    h_one = (normed_one * norm1_gain).astype(bf16)
    query_rows = jnp.dot(h_one, w_query, preferred_element_type=f32).astype(bf16)
    key_rows = jnp.dot(h_one, key_weight_matrix, preferred_element_type=f32).astype(bf16)
    value_rows = jnp.dot(h_one, value_weight_matrix, preferred_element_type=f32).astype(bf16)
    query4 = query_rows.reshape(tok, kv_heads, query_group, head_dim)
    q_pos = ctx_index * tok + jnp.arange(tok, dtype=jnp.int32)
    start_state = (
        jnp.full((kv_heads, query_group, tok), -1e30, f32),
        jnp.zeros((kv_heads, query_group, tok), f32),
        jnp.zeros((kv_heads, query_group, tok, head_dim), f32),
    )
    piece_k = lax.all_gather(key_rows, "ctx", axis=0, tiled=True)
    piece_v = lax.all_gather(value_rows, "ctx", axis=0, tiled=True)
    count = piece_k.shape[0]
    attend_width = key_blocks()
    k_blocks = piece_k.reshape(count // attend_width, attend_width, kv_heads, head_dim)
    v_blocks = piece_v.reshape(count // attend_width, attend_width, kv_heads, head_dim)
    offsets = jnp.arange(count // attend_width, dtype=jnp.int32) * attend_width

    def step(state, inputs):
        k_block, v_block, offset = inputs
        run_max, run_sum, run_acc = state
        scores = jnp.einsum("qhgd,khd->hgqk", query4, k_block, preferred_element_type=f32) * 0.125
        k_pos = offset + jnp.arange(attend_width, dtype=jnp.int32)
        mask = k_pos[None, :] <= q_pos[:, None]
        new_max = jnp.maximum(run_max, jnp.max(jnp.where(mask, scores, -1e30), axis=-1))
        weights = jnp.where(mask, jnp.exp(scores - new_max[..., None]), 0.0)
        factor = jnp.exp(run_max - new_max)
        run_sum = run_sum * factor + jnp.sum(weights, axis=-1)
        run_acc = run_acc * factor[..., None] + jnp.einsum(
            "hgqk,khd->hgqd", weights.astype(bf16), v_block, preferred_element_type=f32
        )
        return ((new_max, run_sum, run_acc), None)

    state, unused = lax.scan(step, start_state, (k_blocks, v_blocks, offsets))
    run_max, run_sum, run_acc = state
    log_total = run_max + jnp.log(run_sum)
    attended = (run_acc / run_sum[..., None]).transpose(2, 0, 1, 3)
    heads = attended.reshape(tok, kv_heads * query_group * head_dim).astype(bf16)
    branch = lax.psum_scatter(
        jnp.dot(heads, w_out, preferred_element_type=f32).astype(jnp.bfloat16),
        "mp",
        scatter_dimension=0,
        tiled=True,
    ).astype(jnp.float32)
    x_mine = lax.dynamic_slice_in_dim(xf, mp_index * share, share, 0)
    resid = x_mine + branch
    normed_two, inverse_two = rms_parts(resid)
    h_two = (normed_two * norm2_gain).astype(bf16)
    h_two_f = h_two.astype(f32)
    logits = jnp.dot(h_two_f, router, precision=hp)
    my_routes = lax.dynamic_slice_in_dim(routes, mp_index * share, share, 0)
    onehot = (
        my_routes[:, :, None] == jnp.arange(experts_all, dtype=jnp.int32)[None, None, :]
    ).astype(f32)
    chosen = jnp.sum(logits[:, None, :] * onehot, axis=-1)
    gates = jax.nn.softmax(chosen, axis=-1)
    flat = my_routes.reshape(share * top)
    flat_hot = (flat[:, None] == jnp.arange(experts_all, dtype=jnp.int32)[None, :]).astype(
        jnp.int32
    )
    ranks = jnp.sum((jnp.cumsum(flat_hot, axis=0) - 1) * flat_hot, axis=1)
    dest = flat * cap + ranks
    repeated = jnp.repeat(h_two, top, axis=0)
    send_rows = jnp.zeros((experts_all * cap, MODEL_WIDTH), bf16).at[dest].set(repeated)
    send_rows = send_rows.reshape(n_mp, exp_local, cap, MODEL_WIDTH)
    arrived = lax.all_to_all(send_rows, "mp", split_axis=0, concat_axis=2, tiled=True).reshape(
        exp_local, n_mp * cap, MODEL_WIDTH
    )
    gate_pre = jnp.einsum("erd,edf->erf", arrived, w_gate, preferred_element_type=f32)
    up_pre = jnp.einsum("erd,edf->erf", arrived, w_up, preferred_element_type=f32)
    sigma = jax.nn.sigmoid(gate_pre)
    silu_gate = gate_pre * sigma
    hidden = (silu_gate * up_pre).astype(bf16)
    made = jnp.einsum("erf,efd->erd", hidden, w_down, preferred_element_type=f32).astype(bf16)
    returned = lax.all_to_all(
        made.reshape(1, exp_local, n_mp * cap, MODEL_WIDTH),
        "mp",
        split_axis=2,
        concat_axis=0,
        tiled=True,
    )
    returned = returned.reshape(experts_all * cap, MODEL_WIDTH)
    picked = returned[dest].astype(f32).reshape(share, top, MODEL_WIDTH)
    output = resid + jnp.sum(gates[:, :, None] * picked, axis=1)
    grad_out_rows = cotangent.astype(f32)
    grad_gates = jnp.sum(grad_out_rows[:, None, :] * picked, axis=-1)
    grad_picked = (
        (gates[:, :, None] * grad_out_rows[:, None, :])
        .astype(bf16)
        .reshape(share * top, MODEL_WIDTH)
    )
    grad_send = jnp.zeros((experts_all * cap, MODEL_WIDTH), bf16).at[dest].set(grad_picked)
    grad_made = lax.all_to_all(
        grad_send.reshape(n_mp, exp_local, cap, MODEL_WIDTH),
        "mp",
        split_axis=0,
        concat_axis=2,
        tiled=True,
    )
    grad_made = grad_made.reshape(exp_local, n_mp * cap, MODEL_WIDTH)
    grad_hidden = jnp.einsum("erd,efd->erf", grad_made, w_down, preferred_element_type=f32)
    grad_gate_pre = (grad_hidden * up_pre * sigma * (1.0 + gate_pre * (1.0 - sigma))).astype(bf16)
    grad_up_pre = (grad_hidden * silu_gate).astype(bf16)
    grad_w_down = jnp.einsum("erf,erd->efd", hidden, grad_made, preferred_element_type=f32)
    grad_w_gate = jnp.einsum("erd,erf->edf", arrived, grad_gate_pre, preferred_element_type=f32)
    grad_w_up = jnp.einsum("erd,erf->edf", arrived, grad_up_pre, preferred_element_type=f32)
    grad_arrived = jnp.einsum("erf,edf->erd", grad_gate_pre, w_gate, preferred_element_type=f32)
    grad_arrived = grad_arrived + jnp.einsum(
        "erf,edf->erd", grad_up_pre, w_up, preferred_element_type=f32
    )
    grad_arrived = grad_arrived.astype(bf16).reshape(1, exp_local, n_mp * cap, MODEL_WIDTH)
    grad_rows = lax.all_to_all(grad_arrived, "mp", split_axis=2, concat_axis=0, tiled=True).reshape(
        experts_all * cap, MODEL_WIDTH
    )
    grad_rows = grad_rows[dest].astype(f32).reshape(share, top, MODEL_WIDTH)
    grad_chosen = gates * (grad_gates - jnp.sum(gates * grad_gates, axis=-1, keepdims=True))
    grad_logits = jnp.sum(grad_chosen[:, :, None] * onehot, axis=1)
    grad_router = jnp.dot(h_two_f.T, grad_logits, precision=hp)
    grad_h_two = jnp.sum(grad_rows, axis=1) + jnp.dot(grad_logits, router.T, precision=hp)
    grad_norm2 = jnp.sum(grad_h_two * normed_two, axis=0)
    grad_resid = grad_out_rows + rms_grad(grad_h_two * norm2_gain, normed_two, inverse_two)
    resid_grad_all = lax.all_gather(grad_resid.astype(bf16), "mp", axis=0, tiled=True)
    grad_w_out = jnp.einsum("tf,td->fd", heads, resid_grad_all, preferred_element_type=f32)
    grad_heads = jnp.einsum("td,fd->tf", resid_grad_all, w_out, preferred_element_type=f32).astype(
        bf16
    )
    grad_heads4 = grad_heads.reshape(tok, kv_heads, query_group, head_dim)
    delta = jnp.sum(grad_heads4.astype(f32) * attended, axis=-1).transpose(1, 2, 0)
    whole_k, whole_v = (
        lax.all_gather(key_rows, "ctx", axis=0, tiled=True),
        lax.all_gather(value_rows, "ctx", axis=0, tiled=True),
    )
    length = whole_k.shape[0]
    width = key_blocks()
    k_blocks = whole_k.reshape(length // width, width, kv_heads, head_dim)
    v_blocks = whole_v.reshape(length // width, width, kv_heads, head_dim)
    offsets = jnp.arange(length // width, dtype=jnp.int32) * width

    def back_step(grad_query_acc, inputs):
        k_block, v_block, offset = inputs
        scores = jnp.einsum("qhgd,khd->hgqk", query4, k_block, preferred_element_type=f32) * 0.125
        k_pos = offset + jnp.arange(width, dtype=jnp.int32)
        mask = k_pos[None, :] <= q_pos[:, None]
        probs = jnp.where(mask, jnp.exp(scores - log_total[..., None]), 0.0)
        grad_v_block = jnp.einsum(
            "hgqk,qhgd->khd", probs.astype(bf16), grad_heads4, preferred_element_type=f32
        )
        grad_probs = jnp.einsum("qhgd,khd->hgqk", grad_heads4, v_block, preferred_element_type=f32)
        grad_scores = (probs * (grad_probs - delta[..., None])).astype(bf16)
        grad_query_acc = grad_query_acc + jnp.einsum(
            "hgqk,khd->qhgd", grad_scores, k_block, preferred_element_type=f32
        )
        grad_k_block = jnp.einsum("hgqk,qhgd->khd", grad_scores, query4, preferred_element_type=f32)
        return (grad_query_acc, (grad_k_block, grad_v_block))

    grad_query_acc, (grad_k_all, grad_v_all) = lax.scan(
        back_step,
        jnp.zeros((tok, kv_heads, query_group, head_dim), f32),
        (k_blocks, v_blocks, offsets),
    )
    grad_k_all = grad_k_all.reshape(length, kv_heads * head_dim) * 0.125
    grad_v_all = grad_v_all.reshape(length, kv_heads * head_dim)
    grad_k_mine, grad_v_mine = (
        lax.psum_scatter(
            grad_k_all.astype(jnp.bfloat16), "ctx", scatter_dimension=0, tiled=True
        ).astype(jnp.float32),
        lax.psum_scatter(
            grad_v_all.astype(jnp.bfloat16), "ctx", scatter_dimension=0, tiled=True
        ).astype(jnp.float32),
    )
    grad_keys = grad_k_mine.astype(bf16)
    grad_values = grad_v_mine.astype(bf16)
    grad_query = (
        (grad_query_acc * 0.125).reshape(tok, kv_heads * query_group * head_dim).astype(bf16)
    )
    grad_w_query = jnp.einsum("td,tf->df", h_one, grad_query, preferred_element_type=f32)
    grad_w_key = jnp.einsum("td,tf->df", h_one, grad_keys, preferred_element_type=f32)
    grad_w_value = jnp.einsum("td,tf->df", h_one, grad_values, preferred_element_type=f32)
    grad_h_one = jnp.einsum("tf,df->td", grad_query, w_query, preferred_element_type=f32)
    grad_h_one = grad_h_one + jnp.einsum(
        "tf,df->td", grad_keys, key_weight_matrix, preferred_element_type=f32
    )
    grad_h_one = grad_h_one + jnp.einsum(
        "tf,df->td", grad_values, value_weight_matrix, preferred_element_type=f32
    )
    grad_h_mine = lax.psum_scatter(
        grad_h_one.astype(jnp.bfloat16), "mp", scatter_dimension=0, tiled=True
    ).astype(jnp.float32)
    normed_mine = lax.dynamic_slice_in_dim(normed_one, mp_index * share, share, 0)
    inverse_mine = lax.dynamic_slice_in_dim(inverse_one, mp_index * share, share, 0)
    grad_norm1 = jnp.sum(grad_h_mine * normed_mine, axis=0)
    grad_tokens = grad_resid + rms_grad(grad_h_mine * norm1_gain, normed_mine, inverse_mine)
    grad_norm1, grad_norm2, grad_router = lax.psum(
        (grad_norm1, grad_norm2, grad_router), ("seq", "ctx", "mp")
    )
    grad_w_query, grad_w_key, grad_w_value, grad_w_out, grad_w_gate, grad_w_up, grad_w_down = (
        lax.psum_scatter(
            grad_w_query.astype(jnp.bfloat16), ("seq", "ctx"), scatter_dimension=0, tiled=True
        ).astype(jnp.float32),
        lax.psum_scatter(
            grad_w_key.astype(jnp.bfloat16), ("seq", "ctx"), scatter_dimension=0, tiled=True
        ).astype(jnp.float32),
        lax.psum_scatter(
            grad_w_value.astype(jnp.bfloat16), ("seq", "ctx"), scatter_dimension=0, tiled=True
        ).astype(jnp.float32),
        lax.psum_scatter(
            grad_w_out.astype(jnp.bfloat16), ("seq", "ctx"), scatter_dimension=1, tiled=True
        ).astype(jnp.float32),
        lax.psum_scatter(
            grad_w_gate.astype(jnp.bfloat16), ("seq", "ctx"), scatter_dimension=1, tiled=True
        ).astype(jnp.float32),
        lax.psum_scatter(
            grad_w_up.astype(jnp.bfloat16), ("seq", "ctx"), scatter_dimension=1, tiled=True
        ).astype(jnp.float32),
        lax.psum_scatter(
            grad_w_down.astype(jnp.bfloat16), ("seq", "ctx"), scatter_dimension=1, tiled=True
        ).astype(jnp.float32),
    )
    return (
        output,
        grad_tokens,
        grad_norm1,
        grad_w_query,
        grad_w_key,
        grad_w_value,
        grad_w_out,
        grad_norm2,
        grad_router,
        grad_w_gate,
        grad_w_up,
        grad_w_down,
    )


def solution(mesh):
    placed = (
        P(("seq", "ctx"), None),
        P(),
        P(None, "mp"),
        P(None, "mp"),
        P(None, "mp"),
        P("mp", None),
        P(),
        P(),
        P("mp", None, None),
        P("mp", None, None),
        P("mp", None, None),
        P(("seq", "ctx"), None),
        P(("seq", "ctx", "mp"), None),
    )
    return jax.shard_map(
        body,
        mesh=mesh,
        in_specs=placed,
        out_specs=(
            P(("seq", "ctx", "mp"), None),
            P(("seq", "ctx", "mp"), None),
            P(),
            P(("seq", "ctx"), "mp"),
            P(("seq", "ctx"), "mp"),
            P(("seq", "ctx"), "mp"),
            P("mp", ("seq", "ctx")),
            P(),
            P(),
            P("mp", ("seq", "ctx"), None),
            P("mp", ("seq", "ctx"), None),
            P("mp", ("seq", "ctx"), None),
        ),
        check_vma=False,
    )
```

profile of v0, /device:TPU:16, one launch (start us, length us, event | category | flops | bytes accessed | tf_op | source)
XLA Modules:
  0.0 1156.0 jit_solution(9322766775931008272)
XLA Ops:
  11.2 16.4 %all_gather.11 = bf16[2560,128]{1,0:T(8,128)(2,1)S(1)} all-gather(bf16[640,128]{1,0:T(8,128)(2,1)S(1)} %convolution_convert_fusion.12), channel_id=1, replica_groups=mesh['seq'=2,'ctx'=4,'mp'=4] {'ctx'}, dimensions={0}, use_global_device_ids=true | all-gather | bytes 819200 | tf_op jit(solution)/shard_map/all_gather | solution.py:69
  34.0 16.3 %all_gather.12 = bf16[2560,128]{1,0:T(8,128)(2,1)S(1)} all-gather(bf16[640,128]{1,0:T(8,128)(2,1)S(1)} %convolution_convert_fusion.11), channel_id=1, replica_groups=mesh['seq'=2,'ctx'=4,'mp'=4] {'ctx'}, dimensions={0}, use_global_device_ids=true | all-gather | bytes 819200 | tf_op jit(solution)/shard_map/all_gather | solution.py:70
  58.8 77.3 %while.30 = (s32[]{:T(128)}, f32[2,3,640]{2,1,0:T(4,128)S(1)}, f32[2,3,640]{2,1,0:T(4,128)S(1)}, f32[2,3,640,64]{2,3,1,0:T(8,128)}, s32[5]{0:T(128)S(1)}, /*inde...) while((s32[]{:T(128)}, f32[2,3,640]{2,1,0:T(4,128)S(1)}, ...), condition=%wide.region_4.5_spmd.clone, body=%wide.region_1.4_spmd.clone.sunk | while | flops 526028672 | bytes 59336364 | solution.py:92
  147.8 25.1 %reduce-scatter.16.cloned.1.call-done = bf16[160,1536]{1,0:T(8,128)(2,1)} async-done(((bf16[640,1536]{1,0:T(8,128)(2,1)}), bf16[160,1536]{1,0:T(8,128)(2,1)}) %reduce-scatter.16.cloned.1.call-update) | async-done | bytes 491536 | tf_op jit(solution)/shard_map/reduce_scatter | solution.py:97
  233.1 5.6 all-to-all-done.2
  238.8 7.7 multiply_convert_fusion.2
  315.0 23.0 %all-gather.2.cloned.1.call-done = bf16[640,1536]{1,0:T(8,128)(2,1)} async-done(((bf16[160,1536]{1,0:T(8,128)(2,1)}), bf16[640,1536]{1,0:T(8,128)(2,1)}) %all-gather.2.cloned.1.call-update) | async-done | bytes 1966096 | tf_op jit(solution)/shard_map/all_gather | solution.py:180
  341.6 96.2 %while.31 = (s32[]{:T(128)}, f32[640,2,3,64]{0,3,2,1:T(8,128)S(1)}, f32[5,512,2,64]{1,3,2,0:T(8,128)}, bf16[5,512,2,64]{1,3,2,0:T(8,128)(2,1)}, bf16[5,512,2,64]...) while((s32[]{:T(128)}, f32[640,2,3,64]{0,3,2,1:T(8,128)S(1)}, ...), condition=%wide.region_23.24_spmd.clone, body=%wide.region_22.23_spmd.clone.sunk | while | flops 1278772352 | bytes 90431232 | solution.py:214
  355.2 5.6 fusion.175
  374.5 5.6 fusion.175
  393.7 5.6 fusion.175
  412.9 5.6 fusion.175
  444.5 17.9 %reduce-scatter.34.cloned.1.call-done = bf16[640,128]{1,0:T(8,128)(2,1)} async-done(((bf16[2560,128]{1,0:T(8,128)(2,1)}), bf16[640,128]{1,0:T(8,128)(2,1)}) %reduce-scatter.34.cloned.1.call-update) | async-done | bytes 163856
  465.8 20.6 %reduce-scatter.36.cloned.1.call-done = bf16[640,128]{1,0:T(8,128)(2,1)} async-done(((bf16[2560,128]{1,0:T(8,128)(2,1)}), bf16[640,128]{1,0:T(8,128)(2,1)}) %reduce-scatter.36.cloned.1.call-update) | async-done | bytes 163856
  504.8 5.8 convolution_convert_fusion
  526.5 24.9 %reduce-scatter.22.cloned.1.call-done = bf16[192,128]{1,0:T(8,128)(2,1)} async-done(((bf16[1536,128]{1,0:T(8,128)(2,1)}), bf16[192,128]{1,0:T(8,128)(2,1)}) %reduce-scatter.22.cloned.1.call-update) | async-done | bytes 49168 | tf_op jit(solution)/shard_map/reduce_scatter | solution.py:258
  552.9 62.5 %reduce-scatter.24.cloned.1.call-done = bf16[192,128]{1,0:T(8,128)(2,1)} async-done(((bf16[1536,128]{1,0:T(8,128)(2,1)}), bf16[192,128]{1,0:T(8,128)(2,1)}) %reduce-scatter.24.cloned.1.call-update) | async-done | bytes 49168 | tf_op jit(solution)/shard_map/reduce_scatter | solution.py:261
  616.8 65.9 %reduce-scatter.26.cloned.1.call-done = bf16[384,192]{0,1:T(8,128)(2,1)} async-done(((bf16[384,1536]{0,1:T(8,128)(2,1)}), bf16[384,192]{0,1:T(8,128)(2,1)}) %reduce-scatter.26.cloned.1.call-update) | async-done | bytes 147472 | tf_op jit(solution)/shard_map/reduce_scatter | solution.py:264
  684.3 65.7 %reduce-scatter.20.cloned.1.call-done = bf16[192,384]{1,0:T(8,128)(2,1)} async-done(((bf16[1536,384]{1,0:T(8,128)(2,1)}), bf16[192,384]{1,0:T(8,128)(2,1)}) %reduce-scatter.20.cloned.1.call-update) | async-done | bytes 147472 | tf_op jit(solution)/shard_map/reduce_scatter | solution.py:255
  751.7 31.7 %reduce-scatter.18.cloned.1.call-done = bf16[160,1536]{1,0:T(8,128)(2,1)} async-done(((bf16[640,1536]{1,0:T(8,128)(2,1)}), bf16[160,1536]{1,0:T(8,128)(2,1)}) %reduce-scatter.18.cloned.1.call-update) | async-done | bytes 491536 | tf_op jit(solution)/shard_map/reduce_scatter | solution.py:244
  785.1 44.0 %all-reduce.1 = (f32[1536]{0:T(1024)}, f32[1536]{0:T(1024)}, f32[1536,8]{0,1:T(8,128)}) all-reduce(f32[1536]{0:T(1024)S(1)} %get-tuple-element.311, f32[1536]{0:T(1024)S(1)} %copy-done.49, f32[1536,8]{0,1:T(8,128)S(1)} %fusion.88), channel_id=1, replica_groups=mesh['seq'=2,'ctx'=4,'mp'=4] {'seq','ctx','mp'}, use_global_device_ids=true, to_apply=%region_29.30 | all-reduce | flops 15360 | bytes 122880 | tf_op jit(solution)/shard_map/psum | solution.py:251
  832.4 72.6 %reduce-scatter.32.cloned.1.call-done = bf16[2,128,1536]{2,1,0:T(8,128)(2,1)} async-done(((bf16[2,1024,1536]{2,1,0:T(8,128)(2,1)}), bf16[2,128,1536]{2,1,0:T(8,128)(2,1)}) %reduce-scatter.32.cloned.1.call-update) | async-done | bytes 786448 | tf_op jit(solution)/shard_map/reduce_scatter | solution.py:273
  907.5 118.1 %reduce-scatter.28.cloned.1.call-done = bf16[2,192,1024]{2,1,0:T(8,128)(2,1)} async-done(((bf16[2,1536,1024]{2,1,0:T(8,128)(2,1)}), bf16[2,192,1024]{2,1,0:T(8,128)(2,1)}) %reduce-scatter.28.cloned.1.call-update) | async-done | bytes 786448 | tf_op jit(solution)/shard_map/reduce_scatter | solution.py:267
  1028.1 118.1 %reduce-scatter.30.cloned.1.call-done = bf16[2,192,1024]{2,1,0:T(8,128)(2,1)} async-done(((bf16[2,1536,1024]{2,1,0:T(8,128)(2,1)}), bf16[2,192,1024]{2,1,0:T(8,128)(2,1)}) %reduce-scatter.30.cloned.1.call-update) | async-done | bytes 786448 | tf_op jit(solution)/shard_map/reduce_scatter | solution.py:270
  (391 shorter events, 375.7 us)
Async XLA Ops:
  7.2 165.7 %reduce-scatter.16.cloned.1.call-start = ((), (), s32[]{:S(2)}) async-start(), calls=%async_computation.15 | async-start | bytes 2457600 | tf_op jit(solution)/shard_map/reduce_scatter | solution.py:97
  186.1 31.4 %all-to-all-start = ((bf16[4,2,50,1536]{3,1,2,0:T(2,128)(2,1)}), bf16[4,2,50,1536]{3,1,2,0:T(2,128)(2,1)S(1)}, u32[]{:S(2)}, u32[]{:S(2)}) async-start(bf16[4,2,50,1536]{3,1,2,0:T(2,128)(2,1)} %copy.132), calls=%async_computation.1 | async-start | bytes 2457600 | tf_op jit(solution)/shard_map/all_to_all | solution.py:124
  217.6 21.2 %all-to-all-start.2 = ((bf16[4,2,50,1536]{3,1,2,0:T(2,128)(2,1)}), bf16[4,2,50,1536]{3,1,2,0:T(2,128)(2,1)}, u32[]{:S(2)}, u32[]{:S(2)}) async-start(bf16[4,2,50,1536]{3,1,2,0:T(2,128)(2,1)} %copy.138), calls=%async_computation.3 | async-start | bytes 2457600 | tf_op jit(solution)/shard_map/all_to_all | solution.py:151
  253.0 19.9 %all-to-all-start.1 = ((bf16[1,2,200,1536]{3,1,0,2:T(2,128)(2,1)}), bf16[1,2,200,1536]{3,1,0,2:T(2,128)(2,1)S(1)}, u32[]{:S(2)}, u32[]{:S(2)}) async-start(bf16[1,2,200,1536]{3,1,0,2:T(2,128)(2,1)} %copy.135), calls=%async_computation.2 | async-start | bytes 2457600 | tf_op jit(solution)/shard_map/all_to_all | solution.py:133
  272.9 21.2 %all-to-all-start.3 = ((bf16[1,2,200,1536]{3,1,0,2:T(2,128)(2,1)}), bf16[1,2,200,1536]{3,1,0,2:T(2,128)(2,1)}, u32[]{:S(2)}, u32[]{:S(2)}) async-start(bf16[1,2,200,1536]{3,1,0,2:T(2,128)(2,1)} %copy.140), calls=%async_computation.4 | async-start | bytes 2457600 | tf_op jit(solution)/shard_map/all_to_all | solution.py:170
  277.2 60.9 %all-gather.2.cloned.1.call-start = ((), (), s32[]{:S(2)}) async-start(), calls=%async_computation.16 | async-start | bytes 2457600 | tf_op jit(solution)/shard_map/all_gather | solution.py:180
  314.6 147.8 %reduce-scatter.34.cloned.1.call-start = ((), (), s32[]{:S(2)}) async-start(), calls=%async_computation.25 | async-start | bytes 819200
  441.8 44.6 %reduce-scatter.36.cloned.1.call-start = ((), (), s32[]{:S(2)}) async-start(), calls=%async_computation.26 | async-start | bytes 819200
  444.4 107.0 %reduce-scatter.22.cloned.1.call-start = ((), (), s32[]{:S(2)}) async-start(), calls=%async_computation.19 | async-start | bytes 442368 | tf_op jit(solution)/shard_map/reduce_scatter | solution.py:258
  465.7 149.6 %reduce-scatter.24.cloned.1.call-start = ((), (), s32[]{:S(2)}) async-start(), calls=%async_computation.20 | async-start | bytes 442368 | tf_op jit(solution)/shard_map/reduce_scatter | solution.py:261
  489.7 193.0 %reduce-scatter.26.cloned.1.call-start = ((), (), s32[]{:S(2)}) async-start(), calls=%async_computation.21 | async-start | bytes 1327104 | tf_op jit(solution)/shard_map/reduce_scatter | solution.py:264
  493.9 256.1 %reduce-scatter.20.cloned.1.call-start = ((), (), s32[]{:S(2)}) async-start(), calls=%async_computation.18 | async-start | bytes 1327104 | tf_op jit(solution)/shard_map/reduce_scatter | solution.py:255
  498.1 285.3 %reduce-scatter.18.cloned.1.call-start = ((), (), s32[]{:S(2)}) async-start(), calls=%async_computation.17 | async-start | bytes 2457600 | tf_op jit(solution)/shard_map/reduce_scatter | solution.py:244
  503.6 401.3 %reduce-scatter.32.cloned.1.call-start = ((), (), s32[]{:S(2)}) async-start(), calls=%async_computation.24 | async-start | bytes 7077888 | tf_op jit(solution)/shard_map/reduce_scatter | solution.py:273
  510.6 515.1 %reduce-scatter.28.cloned.1.call-start = ((), (), s32[]{:S(2)}) async-start(), calls=%async_computation.22 | async-start | bytes 7077888 | tf_op jit(solution)/shard_map/reduce_scatter | solution.py:267
  516.6 629.6 %reduce-scatter.30.cloned.1.call-start = ((), (), s32[]{:S(2)}) async-start(), calls=%async_computation.23 | async-start | bytes 7077888 | tf_op jit(solution)/shard_map/reduce_scatter | solution.py:270
  526.1 258.9 %copy-start.49 = (f32[1536]{0:T(1024)S(1)}, f32[1536]{0:T(1024)}, u32[]{:S(2)}) copy-start(f32[1536]{0:T(1024)} %get-tuple-element.313) | copy-start | bytes 18436
  526.1 302.9 %copy-start.7 = (f32[160,1536]{1,0:T(8,128)S(1)}, f32[160,1536]{1,0:T(8,128)}, u32[]{:S(2)}) copy-start(f32[160,1536]{1,0:T(8,128)} %copy-done.5) | copy-start | bytes 2949124
  526.1 302.9 %copy-start.12 = (f32[160,1536]{1,0:T(8,128)S(1)}, f32[160,1536]{1,0:T(8,128)}, u32[]{:S(2)}) copy-start(f32[160,1536]{1,0:T(8,128)} %copy-done.11) | copy-start | bytes 2949124
  526.2 302.9 %copy-start.14 = (bf16[160,1536]{1,0:T(8,128)(2,1)S(1)}, bf16[160,1536]{1,0:T(8,128)(2,1)}, u32[]{:S(2)}) copy-start(bf16[160,1536]{1,0:T(8,128)(2,1)} %param.29) | copy-start | bytes 1474564
  526.2 302.9 %copy-start.43 = (f32[1536]{0:T(1024)S(1)}, f32[1536]{0:T(1024)}, u32[]{:S(2)}) copy-start(f32[1536]{0:T(1024)} %param.23) | copy-start | bytes 18436
  526.2 302.9 %copy-start.54 = (f32[160]{0:T(256)S(1)}, f32[160]{0:T(256)}, u32[]{:S(2)}) copy-start(f32[160]{0:T(256)} %copy-done.52) | copy-start | bytes 1924
  526.2 302.9 %copy-start.61 = (f32[160]{0:T(256)S(1)}, f32[160]{0:T(256)}, u32[]{:S(2)}) copy-start(f32[160]{0:T(256)} %copy-done.60) | copy-start | bytes 1924
  905.0 243.7 %copy-start.1 = (bf16[384,1536]{1,0:T(8,128)(2,1)S(1)}, bf16[384,1536]{1,0:T(8,128)(2,1)}, u32[]{:S(2)}) copy-start(bf16[384,1536]{1,0:T(8,128)(2,1)} %param.22) | copy-start | bytes 3538948
  (72 other events, 515.8 us)
Sparse Core Ops, SparseCore 0:
  140.6 32.2 reduce-scatter.15
  314.8 23.2 all-gather.1
  441.9 20.4 reduce-scatter.33
  465.3 21.0 reduce-scatter.35
  490.4 60.9 reduce-scatter.21
  554.9 60.4 reduce-scatter.23
  619.7 62.9 reduce-scatter.25
  687.0 62.9 reduce-scatter.19
  752.8 30.5 reduce-scatter.17
  786.8 118.1 reduce-scatter.31
  908.6 117.0 reduce-scatter.27
  1029.1 117.0 reduce-scatter.29
where the time goes:
time: 1160 us
  waiting for transfers between devices  656 us (57%)
  matrix products  204 us (18%)
  other arithmetic  94.5 us (8%)
  local copies, waits for them, and re-layouts  91.5 us (8%)
  blocking collectives  76.7 us (7%)
  starting transfers between devices  17.2 us (1%)
  between operations  15.5 us (1%)
    reduce_scatter x1, waiting for transfers between devices, body(): lax.psum_scatter(grad_w_up.astype(jnp.bfloat16), ('seq', 'ctx'), scatter_...  118 us
    reduce_scatter x1, waiting for transfers between devices, body(): lax.psum_scatter(grad_w_gate.astype(jnp.bfloat16), ('seq', 'ctx'), scatte...  118 us
    reduce_scatter x1, waiting for transfers between devices, body(): lax.psum_scatter(grad_w_down.astype(jnp.bfloat16), ('seq', 'ctx'), scatte...  72.6 us
    reduce_scatter x1, waiting for transfers between devices, body(): lax.psum_scatter(grad_w_out.astype(jnp.bfloat16), ('seq', 'ctx'), scatter...  65.9 us
    reduce_scatter x1, waiting for transfers between devices, body(): lax.psum_scatter(grad_w_query.astype(jnp.bfloat16), ('seq', 'ctx'), scatt...  65.7 us
    reduce_scatter x1, waiting for transfers between devices, body(): lax.psum_scatter(grad_w_value.astype(jnp.bfloat16), ('seq', 'ctx'), scatt...  62.5 us
    psum x1, blocking collectives, body(): lax.psum((grad_norm1, grad_norm2, grad_router), ('seq', 'ctx', 'mp'))  44 us
    unnamed x14, waiting for transfers between devices  38.8 us
  transfers between devices with their start and end apart: 16, of which 14 were waited for; matrix products, arithmetic and copies ran while one was open for 11% of the time, Pallas kernels for 0%

commit v1 on v0

v1 whole, which is shorter than its diff:
```python
import functools

import jax
import jax.numpy as jnp
from jax import lax
from jax.experimental import pallas as pl
from jax.experimental.pallas import tpu as pltpu
from jax.sharding import PartitionSpec as P

HEAD_SIZE = 64
EPS = 1e-06
MESH = pl.DeviceIdType.MESH
F32 = jnp.float32
BF16 = jnp.bfloat16
VMEM = pl.BlockSpec(memory_space=pltpu.VMEM)
DMA = pltpu.SemaphoreType.DMA
MIB = 2**20


def params(collective_id, mib=56):
    return pltpu.CompilerParams(
        collective_id=collective_id, has_side_effects=True, vmem_limit_bytes=mib * MIB
    )


def nt(a, b):
    return lax.dot_general(a, b, (((1,), (1,)), ((), ())), preferred_element_type=F32)


def nn(a, b):
    return jnp.dot(a, b, preferred_element_type=F32)


def line_barrier(c, n, up, down):
    sem = pltpu.get_barrier_semaphore()

    @pl.when(c > 0)
    def _():
        pl.semaphore_signal(sem, inc=1, device_id=down, device_id_type=MESH)

    @pl.when(c < n - 1)
    def _():
        pl.semaphore_signal(sem, inc=1, device_id=up, device_id_type=MESH)

    pl.semaphore_wait(sem, jnp.where(c > 0, 1, 0) + jnp.where(c < n - 1, 1, 0))


def pad_heads(src, dst, heads, group):
    dst[...] = jnp.zeros_like(dst)
    for h in range(heads):
        g = h // group
        rows = slice(g * HEAD_SIZE, (g + 1) * HEAD_SIZE)
        dst[h, rows, :] = src[h * HEAD_SIZE : (h + 1) * HEAD_SIZE, :]


def causal(t):
    keys = lax.broadcasted_iota(jnp.int32, (t, t), 0)
    queries = lax.broadcasted_iota(jnp.int32, (t, t), 1)
    return keys <= queries


def attend_kernel(n, q_ref, k_ref, v_ref, o_ref, heads_ref, lse_ref, kv_ref, qpad, vt, top, tot, send, recv):
    s, c, m = lax.axis_index("seq"), lax.axis_index("ctx"), lax.axis_index("mp")
    t, kvw = k_ref.shape
    heads = q_ref.shape[0] // HEAD_SIZE
    group = heads // (kvw // HEAD_SIZE)
    up, down = (s, lax.rem(c + 1, n), m), (s, lax.rem(c + n - 1, n), m)
    kv_ref[0, :, :kvw] = k_ref[...]
    kv_ref[0, :, kvw:] = v_ref[...]
    line_barrier(c, n, up, down)

    def pass_up(slot):
        return pltpu.make_async_remote_copy(
            src_ref=kv_ref.at[slot],
            dst_ref=kv_ref.at[slot + 1],
            send_sem=send.at[slot],
            recv_sem=recv.at[slot + 1],
            device_id=up,
            device_id_type=MESH,
        )

    def got(slot):
        return pltpu.make_async_remote_copy(
            src_ref=kv_ref.at[slot],
            dst_ref=kv_ref.at[slot],
            send_sem=send.at[slot],
            recv_sem=recv.at[slot],
            device_id=up,
            device_id_type=MESH,
        )

    @pl.when(c < n - 1)
    def _():
        pass_up(0).start()

    pad_heads(q_ref, qpad, heads, group)
    top[...] = jnp.full_like(top, -1e30)
    tot[...] = jnp.zeros_like(tot)
    o_ref[...] = jnp.zeros_like(o_ref)

    def block(slot, masked):
        vt[...] = kv_ref[slot, :, kvw:].T

        def head(h, carry):
            g = lax.div(h, group)
            scores = nn(kv_ref[slot, :, :kvw], qpad[h])
            if masked:
                scores = jnp.where(causal(t), scores, -1e30)
            old = top[h]
            new = jnp.maximum(old, jnp.max(scores, axis=0, keepdims=True))
            weights = jnp.exp(scores - new)
            factor = jnp.exp(old - new)
            top[h] = new
            tot[h] = tot[h] * factor + jnp.sum(weights, axis=0, keepdims=True)
            rows = pl.ds(pl.multiple_of(h * HEAD_SIZE, HEAD_SIZE), HEAD_SIZE)
            vrows = pl.ds(pl.multiple_of(g * HEAD_SIZE, HEAD_SIZE), HEAD_SIZE)
            o_ref[rows, :] = o_ref[rows, :] * factor + nn(vt[vrows, :], weights.astype(BF16))
            return carry

        lax.fori_loop(0, heads, head, 0)

    block(0, True)

    def earlier(slot, carry):
        got(slot).wait_recv()

        @pl.when(c < n - 1)
        def _():
            pass_up(slot).start()

        block(slot, False)
        return carry

    lax.fori_loop(1, c + 1, earlier, 0)
    for h in range(heads):
        rows = slice(h * HEAD_SIZE, (h + 1) * HEAD_SIZE)
        done = o_ref[rows, :] / tot[h]
        o_ref[rows, :] = done
        heads_ref[rows, :] = done.astype(BF16)
        lse_ref[h] = top[h] + jnp.log(tot[h])

    @pl.when(c < n - 1)
    def _():
        def sent(slot, carry):
            pass_up(slot).wait_send()
            return carry

        lax.fori_loop(0, c + 1, sent, 0)


def attend(n, qt, k, v):
    t, kvw = k.shape
    qw = qt.shape[0]
    heads = qw // HEAD_SIZE
    return pl.pallas_call(
        functools.partial(attend_kernel, n),
        out_shape=(
            jax.ShapeDtypeStruct((qw, t), F32),
            jax.ShapeDtypeStruct((qw, t), BF16),
            jax.ShapeDtypeStruct((heads, 1, t), F32),
            jax.ShapeDtypeStruct((n, t, 2 * kvw), BF16),
        ),
        in_specs=[VMEM] * 3,
        out_specs=(VMEM,) * 4,
        scratch_shapes=[
            pltpu.VMEM((heads, kvw, t), BF16),
            pltpu.VMEM((kvw, t), BF16),
            pltpu.VMEM((heads, 1, t), F32),
            pltpu.VMEM((heads, 1, t), F32),
            DMA((n,)),
            DMA((n,)),
        ],
        compiler_params=params(0),
        name="attend",
    )(qt, k, v)


def attend_back_kernel(
    n, q_ref, do_ref, o_ref, lse_ref, kv_ref, dq_ref, dkv_ref, qpad, dopad, delta, dq, kt, part, passing, send, recv
):
    s, c, m = lax.axis_index("seq"), lax.axis_index("ctx"), lax.axis_index("mp")
    _, t, kvw2 = kv_ref.shape
    kvw = kvw2 // 2
    heads = q_ref.shape[0] // HEAD_SIZE
    group = heads // (kvw // HEAD_SIZE)
    up, down = (s, lax.rem(c + 1, n), m), (s, lax.rem(c + n - 1, n), m)
    line_barrier(c, n, up, down)
    pad_heads(q_ref, qpad, heads, group)
    pad_heads(do_ref, dopad, heads, group)
    for h in range(heads):
        rows = slice(h * HEAD_SIZE, (h + 1) * HEAD_SIZE)
        delta[h] = jnp.sum(do_ref[rows, :].astype(F32) * o_ref[rows, :], axis=0, keepdims=True)
    dq[...] = jnp.zeros_like(dq)

    def block(j, masked):
        slot = c - j
        acc = part.at[lax.rem(j, 2)]
        acc[...] = jnp.zeros(acc.shape, F32)
        kt[...] = kv_ref[slot, :, :kvw].T

        def head(h, carry):
            g = lax.div(h, group)
            scores = nn(kv_ref[slot, :, :kvw], qpad[h])
            probs = jnp.exp(scores - lse_ref[h])
            if masked:
                probs = jnp.where(causal(t), probs, 0.0)
            dprobs = nn(kv_ref[slot, :, kvw:], dopad[h])
            ds = (probs * (dprobs - delta[h])).astype(BF16)
            rows = pl.ds(pl.multiple_of(h * HEAD_SIZE, HEAD_SIZE), HEAD_SIZE)
            krows = pl.ds(pl.multiple_of(g * HEAD_SIZE, HEAD_SIZE), HEAD_SIZE)
            dq[rows, :] = dq[rows, :] + nn(kt[krows, :], ds)
            acc[:, :kvw] = acc[:, :kvw] + nt(ds, qpad[h])
            acc[:, kvw:] = acc[:, kvw:] + nt(probs.astype(BF16), dopad[h])
            return carry

        lax.fori_loop(0, heads, head, 0)

    def pass_down(j):
        return pltpu.make_async_remote_copy(
            src_ref=passing.at[j],
            dst_ref=passing.at[j],
            send_sem=send.at[j],
            recv_sem=recv.at[j],
            device_id=down,
            device_id_type=MESH,
        )

    def gathered(j):
        acc = part.at[lax.rem(j, 2)]

        @pl.when(c < n - 1)
        def _():
            pass_down(j).wait_recv()
            acc[...] = acc[...] + passing[j].astype(F32)

        return acc

    def forward(j):
        acc = gathered(j)
        passing[j] = acc[...].astype(BF16)
        pass_down(j).start()

    def step(j, carry):
        block(j, False)

        @pl.when(jnp.logical_and(j > 0, c < n - 1))
        def _():
            forward(j - 1)

        @pl.when(c == n - 1)
        def _():
            forward(j)

        return carry

    lax.fori_loop(0, c, step, 0)
    block(c, True)

    @pl.when(jnp.logical_and(c > 0, c < n - 1))
    def _():
        forward(c - 1)

    dq_ref[...] = (dq[...] * 0.125).astype(BF16)
    acc = gathered(c)
    dkv_ref[...] = acc[...].astype(BF16)

    def sent(j, carry):
        pass_down(j).wait_send()
        return carry

    lax.fori_loop(0, c, sent, 0)


def attend_back(n, qt, dot, o, lse, kv):
    qw, t = qt.shape
    heads = qw // HEAD_SIZE
    kvw = kv.shape[2] // 2
    return pl.pallas_call(
        functools.partial(attend_back_kernel, n),
        out_shape=(
            jax.ShapeDtypeStruct((qw, t), BF16),
            jax.ShapeDtypeStruct((t, 2 * kvw), BF16),
        ),
        in_specs=[VMEM] * 5,
        out_specs=(VMEM,) * 2,
        scratch_shapes=[
            pltpu.VMEM((heads, kvw, t), BF16),
            pltpu.VMEM((heads, kvw, t), BF16),
            pltpu.VMEM((heads, 1, t), F32),
            pltpu.VMEM((qw, t), F32),
            pltpu.VMEM((kvw, t), BF16),
            pltpu.VMEM((2, t, 2 * kvw), F32),
            pltpu.VMEM((n, t, 2 * kvw), BF16),
            DMA((n,)),
            DMA((n,)),
        ],
        compiler_params=params(1),
        name="attend_back",
    )(qt, dot, o, lse, kv)


class Mp:
    def __init__(self, part, core_in, y_out, y_in, full, sems, chunks):
        self.part, self.core_in, self.y_out, self.y_in, self.full = part, core_in, y_out, y_in, full
        self.sems, self.chunks = sems, chunks
        s, c, m = lax.axis_index("seq"), lax.axis_index("ctx"), lax.axis_index("mp")
        self.m = m
        self.sib = m + 1 - 2 * lax.rem(m, 2)
        self.opp = lax.rem(m + 2, 4)
        self.diag = lax.rem(self.sib + 2, 4)
        self.sib_id, self.opp_id = (s, c, self.sib), (s, c, self.opp)
        share = (part if part is not None else full).shape[1]
        self.rows = share // chunks

    def barrier(self):
        sem = pltpu.get_barrier_semaphore()
        for d in (self.sib_id, self.opp_id):
            pl.semaphore_signal(sem, inc=1, device_id=d, device_id_type=MESH)
        pl.semaphore_wait(sem, 2)

    def copy(self, src, dst, i, dev):
        return pltpu.make_async_remote_copy(
            src_ref=src,
            dst_ref=dst,
            send_sem=self.sems.at[0, i],
            recv_sem=self.sems.at[1, i],
            device_id=dev,
            device_id_type=MESH,
        )

    def cut(self, i):
        return pl.ds(i * self.rows, self.rows)

    def rs_core(self, i):
        src = self.part.at[self.diag] if i == 0 else self.part.at[self.sib]
        return self.copy(src, self.core_in.at[i], i, self.sib_id)

    def rs_y(self, i):
        return self.copy(self.y_out.at[self.cut(i)], self.y_in.at[self.cut(i)], 2 + i, self.opp_id)

    def rs_begin(self):
        self.rs_core(0).start()
        self.rs_core(1).start()
        self.rs_core(0).wait_recv()
        for i in range(self.chunks):
            cut = self.cut(i)
            self.y_out[cut, :] = (
                self.part[self.opp, cut, :].astype(F32) + self.core_in[0, cut, :].astype(F32)
            ).astype(BF16)
            self.rs_y(i).start()
        self.rs_core(1).wait_recv()

    def rs_chunk(self, i):
        cut = self.cut(i)
        self.rs_y(i).wait_recv()
        return (
            self.part[self.m, cut, :].astype(F32) + self.core_in[1, cut, :].astype(F32)
        ) + self.y_in[cut, :].astype(F32)

    def rs_end(self):
        self.rs_core(0).wait_send()
        self.rs_core(1).wait_send()
        for i in range(self.chunks):
            self.rs_y(i).wait_send()

    def ag(self, kind, i, whose):
        block = self.full.at[whose, self.cut(i)]
        base = 2 + self.chunks
        dev = self.opp_id if kind == 0 else self.sib_id
        return self.copy(block, block, base + kind * self.chunks + i, dev)

    def ag_send(self, i):
        self.ag(0, i, self.m).start()
        self.ag(1, i, self.m).start()

    def ag_end(self):
        for i in range(self.chunks):
            self.ag(0, i, self.opp).wait_recv()
            self.ag(2, i, self.opp).start()
        for i in range(self.chunks):
            self.ag(1, i, self.sib).wait_recv()
            self.ag(2, i, self.diag).wait_recv()
            self.ag(0, i, self.m).wait_send()
            self.ag(1, i, self.m).wait_send()
            self.ag(2, i, self.opp).wait_send()


def mp_scratch(share, width, chunks):
    return [
        pltpu.VMEM((2, share, width), BF16),
        pltpu.VMEM((share, width), BF16),
        pltpu.VMEM((share, width), BF16),
        DMA((2, 2 + 4 * chunks)),
    ]


def rms_parts(rows):
    inverse = lax.rsqrt(jnp.mean(rows * rows, axis=-1, keepdims=True) + EPS)
    return rows * inverse, inverse


def rms_grad(grad_normed, normed, inverse):
    return inverse * (grad_normed - normed * jnp.mean(grad_normed * normed, axis=-1, keepdims=True))


def mid_forward_kernel(chunks, part, x_ref, gain, resid_ref, h_ref, core_in, y_out, y_in, sems):
    mp = Mp(part, core_in, y_out, y_in, h_ref, sems, chunks)
    mp.barrier()
    mp.rs_begin()
    for i in range(chunks):
        cut = mp.cut(i)
        resid = x_ref[cut, :].astype(F32) + mp.rs_chunk(i)
        resid_ref[cut, :] = resid
        normed, _ = rms_parts(resid)
        h_ref[mp.m, cut, :] = (normed * gain[...]).astype(BF16)
        mp.ag_send(i)
    mp.ag_end()
    mp.rs_end()


def mid_forward(part, x_mine, gain, chunks=2):
    _, share, width = part.shape
    return pl.pallas_call(
        functools.partial(mid_forward_kernel, chunks),
        out_shape=(jax.ShapeDtypeStruct((share, width), F32), jax.ShapeDtypeStruct(part.shape, BF16)),
        in_specs=[VMEM] * 3,
        out_specs=(VMEM,) * 2,
        scratch_shapes=mp_scratch(share, width, chunks),
        compiler_params=params(2),
        name="mid_forward",
    )(part, x_mine, gain)


def mid_back_kernel(
    chunks, part, resid_ref, gain, cot, gate_ref, router_ref, dresid_ref, db_ref, dlog_ref, gnorm_ref, core_in, y_out, y_in, sems
):
    mp = Mp(part, core_in, y_out, y_in, db_ref, sems, chunks)
    width = gain.shape[1]
    ex = gate_ref.shape[1]
    mp.barrier()
    mp.rs_begin()
    gnorm_ref[...] = jnp.zeros_like(gnorm_ref)
    for i in range(chunks):
        cut = mp.cut(i)
        both = mp.rs_chunk(i)
        dgate = both[:, width : width + ex] + both[:, width + ex :]
        gate = gate_ref[cut, :]
        dlog = gate * (dgate - jnp.sum(gate * dgate, axis=-1, keepdims=True))
        dlog_ref[cut, :] = dlog
        dh = both[:, :width] + jnp.dot(
            dlog, router_ref[...], precision=lax.Precision.HIGHEST, preferred_element_type=F32
        )
        normed, inverse = rms_parts(resid_ref[cut, :])
        gnorm_ref[0:1, :] = gnorm_ref[0:1, :] + jnp.sum(dh * normed, axis=0, keepdims=True)
        dresid = cot[cut, :].astype(F32) + rms_grad(dh * gain[...], normed, inverse)
        dresid_ref[cut, :] = dresid
        db_ref[mp.m, cut, :] = dresid.astype(BF16)
        mp.ag_send(i)
    mp.ag_end()
    mp.rs_end()


def mid_back(part, resid, gain, cot, gate, router_t, chunks=2):
    n, share, wide = part.shape
    width = gain.shape[1]
    return pl.pallas_call(
        functools.partial(mid_back_kernel, chunks),
        out_shape=(
            jax.ShapeDtypeStruct((share, width), F32),
            jax.ShapeDtypeStruct((n, share, width), BF16),
            jax.ShapeDtypeStruct(gate.shape, F32),
            jax.ShapeDtypeStruct((8, width), F32),
        ),
        in_specs=[VMEM] * 6,
        out_specs=(VMEM,) * 4,
        scratch_shapes=mp_scratch(share, wide, chunks),
        compiler_params=params(3),
        name="mid_back",
    )(part, resid, gain, cot, gate, router_t)


def last_kernel(chunks, part, x_ref, gain, dresid_ref, out_ref, core_in, y_out, y_in, sems):
    mp = Mp(part, core_in, y_out, y_in, None, sems, chunks)
    mp.barrier()
    mp.rs_begin()
    for i in range(chunks):
        cut = mp.cut(i)
        dh = mp.rs_chunk(i)
        normed, inverse = rms_parts(x_ref[cut, :].astype(F32))
        out_ref[cut, :] = dresid_ref[cut, :] + rms_grad(dh * gain[...], normed, inverse)
    mp.rs_end()


def last(part, x_mine, gain, dresid, chunks=2):
    _, share, width = part.shape
    return pl.pallas_call(
        functools.partial(last_kernel, chunks),
        out_shape=jax.ShapeDtypeStruct((share, width), F32),
        in_specs=[VMEM] * 4,
        out_specs=VMEM,
        scratch_shapes=mp_scratch(share, width, chunks),
        compiler_params=params(4),
        name="last",
    )(part, x_mine, gain, dresid)


def small_sum_kernel(sizes, x_ref, out_ref, *rest):
    bufs, sems = rest[:3], rest[3]
    axes = ("seq", "ctx", "mp")
    me = [lax.axis_index(a) for a in axes]

    def peer(axis, d):
        ids = list(me)
        ids[axis] = lax.rem(me[axis] + d, sizes[axis])
        return tuple(ids)

    bar = pltpu.get_barrier_semaphore()
    for axis in range(3):
        for d in range(1, sizes[axis]):
            pl.semaphore_signal(bar, inc=1, device_id=peer(axis, d), device_id_type=MESH)
    pl.semaphore_wait(bar, sum(sizes) - 3)
    out_ref[...] = x_ref[...]
    base = 0
    for axis in (2, 0, 1):
        n, buf = sizes[axis], bufs[axis]
        buf[0] = out_ref[...]
        copies = []
        for d in range(1, n):
            copy = pltpu.make_async_remote_copy(
                src_ref=buf.at[0],
                dst_ref=buf.at[d],
                send_sem=sems.at[0, base + d],
                recv_sem=sems.at[1, base + d],
                device_id=peer(axis, d),
                device_id_type=MESH,
            )
            copy.start()
            copies.append(copy)
        for copy in copies:
            copy.wait()
        total = jnp.zeros(out_ref.shape, F32)
        for i in range(n):
            total = total + buf[lax.rem(me[axis] - i + n, n)]
        out_ref[...] = total
        base += n


def small_sum(sizes, x):
    rows, width = x.shape
    return pl.pallas_call(
        functools.partial(small_sum_kernel, sizes),
        out_shape=jax.ShapeDtypeStruct(x.shape, F32),
        in_specs=[VMEM],
        out_specs=VMEM,
        scratch_shapes=[pltpu.VMEM((n, rows, width), F32) for n in sizes] + [DMA((2, sum(sizes)))],
        compiler_params=params(5),
        name="small_sum",
    )(x)


def line_sum(parts, n, dim):
    c = lax.axis_index("ctx")
    size = parts.shape[dim] // n

    def chunk(k):
        return lax.dynamic_slice_in_dim(parts, jnp.clip(k, 0, n - 1) * size, size, dim)

    total = chunk(c).astype(F32)
    for way in (1, -1):
        moving = None
        for t in range(1, n):
            mine = chunk(n - t + c if way == 1 else c - n + t)
            if moving is not None:
                mine = (mine.astype(F32) + moving.astype(F32)).astype(BF16)
            if way == 1:
                pairs = [(i, i + 1) for i in range(t)]
            else:
                pairs = [(i, i - 1) for i in range(n - t, n)]
            moving = lax.ppermute(mine, "ctx", pairs)
        total = total + moving.astype(F32)
    return total


def half(x, s, dim):
    size = x.shape[dim] // 2
    return lax.dynamic_slice_in_dim(x, s * size, size, dim)


SWAP = [(0, 1), (1, 0)]


def body(
    tokens,
    norm1_gain,
    w_query,
    key_weight_matrix,
    value_weight_matrix,
    w_out,
    norm2_gain,
    router,
    w_gate,
    w_up,
    w_down,
    routes,
    cotangent,
):
    n_seq, n_ctx, n_mp = (lax.axis_size(a) for a in ("seq", "ctx", "mp"))
    s, m = lax.axis_index("seq"), lax.axis_index("mp")
    tok, width = tokens.shape
    share = tok // n_mp
    experts_all = router.shape[1]
    exp_local = w_gate.shape[0]
    top = routes.shape[1]
    cap = share * top * 5 // (4 * experts_all)
    slots = n_mp * cap
    gain1 = norm1_gain.reshape(1, width)
    gain2 = norm2_gain.reshape(1, width)

    cot_all = lax.all_gather(cotangent, "mp", axis=0, tiled=True)
    x_mine = lax.dynamic_slice_in_dim(tokens, m * share, share, 0)

    normed_one, _ = rms_parts(tokens.astype(F32))
    h_one = (normed_one * gain1).astype(BF16)
    qt = (jnp.einsum("df,td->ft", w_query, h_one, preferred_element_type=F32).astype(BF16)) * BF16(0.125)
    k = nn(h_one, key_weight_matrix).astype(BF16)
    v = nn(h_one, value_weight_matrix).astype(BF16)
    o, heads_t, lse, kv = attend(n_ctx, qt, k, v)

    experts = jnp.arange(experts_all, dtype=jnp.int32)
    chosen = (routes[:, :, None] == experts[None, None, :]).any(axis=1)
    low = (jnp.arange(tok)[:, None] >= jnp.arange(tok)[None, :]).astype(BF16)
    rank = (nn(low, chosen.astype(BF16)) - 1.0).astype(jnp.int32)
    first = m * exp_local
    rank_t = lax.dynamic_slice_in_dim(rank.T, first, exp_local, 0)
    chosen_t = lax.dynamic_slice_in_dim(chosen.T, first, exp_local, 0)
    place = (
        (rank_t[:, None, :] == jnp.arange(slots, dtype=jnp.int32)[None, :, None]) & chosen_t[:, None, :]
    ).astype(BF16)
    dout_rows = jnp.einsum("ert,td->erd", place, cot_all, preferred_element_type=F32)
    dout_rows = dout_rows.astype(BF16).astype(F32)
    r_hi = router.astype(BF16)
    r_rest = router - r_hi.astype(F32)
    r_mid = r_rest.astype(BF16)
    r_low = (r_rest - r_mid.astype(F32)).astype(BF16)
    router3 = jnp.concatenate([r_hi, r_mid, r_low], axis=1)

    part = jnp.einsum("ft,fd->td", heads_t, w_out, preferred_element_type=F32).astype(BF16)
    resid, h_two = mid_forward(part.reshape(n_mp, share, width), x_mine, gain2)
    h_two = h_two.reshape(tok, width)

    logits3 = nn(h_two, router3)
    logits = (
        logits3[:, :experts_all]
        + logits3[:, experts_all : 2 * experts_all]
        + logits3[:, 2 * experts_all :]
    )
    peak = jnp.max(jnp.where(chosen, logits, -jnp.inf), axis=-1, keepdims=True)
    raised = jnp.where(chosen, jnp.exp(jnp.where(chosen, logits - peak, 0.0)), 0.0)
    gates = raised / jnp.sum(raised, axis=-1, keepdims=True)
    gates_mine = lax.dynamic_slice_in_dim(gates.T, first, exp_local, 0)
    gate_rows = jnp.sum(place.astype(F32) * gates_mine[:, None, :], axis=-1)[..., None]
    arrived = jnp.einsum("ert,td->erd", place, h_two, preferred_element_type=F32).astype(BF16)
    gate_pre = jnp.einsum("erd,edf->erf", arrived, w_gate, preferred_element_type=F32)
    up_pre = jnp.einsum("erd,edf->erf", arrived, w_up, preferred_element_type=F32)
    sigma = jax.nn.sigmoid(gate_pre)
    silu_gate = gate_pre * sigma
    hidden = (silu_gate * up_pre).astype(BF16)
    grad_made = (gate_rows * dout_rows).astype(BF16)
    grad_hidden = jnp.einsum("erd,efd->erf", grad_made, w_down, preferred_element_type=F32)
    grad_gate_pre = (grad_hidden * up_pre * sigma * (1.0 + gate_pre * (1.0 - sigma))).astype(BF16)
    grad_up_pre = (grad_hidden * silu_gate).astype(BF16)
    grad_arrived = jnp.einsum("erf,edf->erd", grad_gate_pre, w_gate, preferred_element_type=F32)
    grad_arrived = grad_arrived + jnp.einsum("erf,edf->erd", grad_up_pre, w_up, preferred_element_type=F32)
    grad_arrived = grad_arrived.astype(BF16)
    made = jnp.einsum("erf,efd->erd", hidden, w_down, preferred_element_type=F32).astype(BF16)
    made_f = made.astype(F32)
    gate_grads = jnp.sum(dout_rows * made_f, axis=-1)
    ex_pad = 64
    local_hot = (experts[None, :] == (first + jnp.arange(exp_local, dtype=jnp.int32))[:, None]).astype(F32)
    gate_grads = gate_grads[..., None] * local_hot[:, None, :]
    gate_grads = jnp.pad(gate_grads, ((0, 0), (0, 0), (0, ex_pad - experts_all)))
    gg_hi = gate_grads.astype(BF16)
    gg_low = (gate_grads - gg_hi.astype(F32)).astype(BF16)
    flat = place.reshape(exp_local * slots, tok)
    back_rows = jnp.concatenate([grad_arrived, gg_hi, gg_low], axis=-1).reshape(exp_local * slots, -1)
    back = jnp.einsum("rt,rd->td", flat, back_rows, preferred_element_type=F32).astype(BF16)
    comb_rows = (gate_rows * made_f).astype(BF16).reshape(exp_local * slots, width)
    comb = jnp.einsum("rt,rd->td", flat, comb_rows, preferred_element_type=F32).astype(BF16)
    output = resid + lax.psum_scatter(comb, "mp", scatter_dimension=0, tiled=True).astype(F32)

    gates_pad = jnp.pad(
        lax.dynamic_slice_in_dim(gates, m * share, share, 0), ((0, 0), (0, ex_pad - experts_all))
    )
    router_t = jnp.pad(router.T, ((0, ex_pad - experts_all), (0, 0)))
    dresid, db, dlog, gnorm2 = mid_back(
        back.reshape(n_mp, share, -1), resid, gain2, cotangent, gates_pad, router_t
    )
    db = db.reshape(tok, width)
    h_two_mine = lax.dynamic_slice_in_dim(h_two, m * share, share, 0).astype(F32)
    g_router = jnp.einsum("te,td->ed", dlog[:, :experts_all], h_two_mine, precision=lax.Precision.HIGHEST)

    def joined(x):
        return jnp.concatenate([x, lax.ppermute(x, "seq", SWAP)], axis=1)

    def joined_half(x):
        return jnp.concatenate([half(x, s, 2), lax.ppermute(half(x, 1 - s, 2), "seq", SWAP)], axis=1)

    arrived2 = joined_half(arrived)
    dg2, du2 = joined(grad_gate_pre), joined(grad_up_pre)
    g_gate = jnp.einsum("erd,erf->edf", arrived2, dg2, preferred_element_type=F32).astype(BF16)
    g_up = jnp.einsum("erd,erf->edf", arrived2, du2, preferred_element_type=F32).astype(BF16)
    hid2, dy2 = joined_half(hidden), joined(grad_made)
    g_down = jnp.einsum("erf,erd->efd", hid2, dy2, preferred_element_type=F32).astype(BF16)
    g_gate, g_up, g_down = (line_sum(g, n_ctx, 1) for g in (g_gate, g_up, g_down))

    dheads = jnp.einsum("fd,td->ft", w_out, db, preferred_element_type=F32).astype(BF16)
    g_out = jnp.einsum("td,ft->df", db, heads_t, preferred_element_type=F32).astype(BF16)

    def seq_half_sum(g):
        return (
            half(g, s, 0).astype(F32) + lax.ppermute(half(g, 1 - s, 0), "seq", SWAP).astype(F32)
        ).astype(BF16)

    g_out = line_sum(seq_half_sum(g_out), n_ctx, 0).T
    dq, dkv = attend_back(n_ctx, qt, dheads, o, lse, kv)
    kvw = dkv.shape[1] // 2
    dk, dv = dkv[:, :kvw], dkv[:, kvw:]
    dh = jnp.einsum("ft,df->td", dq, w_query, preferred_element_type=F32)
    dh = dh + jnp.einsum("tf,df->td", dk, key_weight_matrix, preferred_element_type=F32)
    dh = dh + jnp.einsum("tf,df->td", dv, value_weight_matrix, preferred_element_type=F32)
    gnorm1 = jnp.sum(dh * normed_one, axis=0, keepdims=True)
    grad_tokens = last(dh.astype(BF16).reshape(n_mp, share, width), x_mine, gain1, dresid)
    g_q = jnp.einsum("td,ft->df", h_one, dq, preferred_element_type=F32)
    g_kv = jnp.einsum("td,tf->df", h_one, dkv, preferred_element_type=F32)
    g_qkv = jnp.concatenate([g_q, g_kv], axis=1).astype(BF16)
    g_qkv = line_sum(seq_half_sum(g_qkv), n_ctx, 0)
    qw = w_query.shape[1]

    rows = 2 + experts_all
    small = jnp.concatenate(
        [gnorm1, gnorm2[:1], g_router, jnp.zeros((-rows % 8, width), F32)], axis=0
    )
    small = small_sum((n_seq, n_ctx, n_mp), small)
    return (
        output,
        grad_tokens,
        small[0],
        g_qkv[:, :qw],
        g_qkv[:, qw : qw + kvw],
        g_qkv[:, qw + kvw :],
        g_out,
        small[1],
        small[2:rows].T,
        g_gate,
        g_up,
        g_down,
    )


def solution(mesh):
    placed = (
        P(("seq", "ctx"), None),
        P(),
        P(None, "mp"),
        P(None, "mp"),
        P(None, "mp"),
        P("mp", None),
        P(),
        P(),
        P("mp", None, None),
        P("mp", None, None),
        P("mp", None, None),
        P(("seq", "ctx"), None),
        P(("seq", "ctx", "mp"), None),
    )
    return jax.shard_map(
        body,
        mesh=mesh,
        in_specs=placed,
        out_specs=(
            P(("seq", "ctx", "mp"), None),
            P(("seq", "ctx", "mp"), None),
            P(),
            P(("seq", "ctx"), "mp"),
            P(("seq", "ctx"), "mp"),
            P(("seq", "ctx"), "mp"),
            P("mp", ("seq", "ctx")),
            P(),
            P(),
            P("mp", ("seq", "ctx"), None),
            P("mp", ("seq", "ctx"), None),
            P("mp", ("seq", "ctx"), None),
        ),
        check_vma=False,
    )
```

time: 1160 us -> 539 us (0.46)
  waiting for transfers between devices: 656 us -> 117 us
  Pallas kernels: 0 us -> 174 us
  matrix products: 204 us -> 86 us
  blocking collectives: 76.7 us -> 0 us
  local copies, waits for them, and re-layouts: 91.5 us -> 19.6 us
  starting transfers between devices: 17.2 us -> 88 us
  other arithmetic: 94.5 us -> 32.3 us
    reduce_scatter x9 -> x1, waiting for transfers between devices: 585 us -> 0.02 us  [body(): lax.psum_scatter(comb, 'mp', scatter_dimension=0, tiled=True).astype(F32)]
    pallas_call x0 -> x6, Pallas kernels: none -> 174 us  [the longest x1 42.4 us: attend_back(): pl.pallas_call(functools.partial(attend_back_kernel, n), out_shape=(jax.S...]
    ppermute x0 -> x37, waiting for transfers between devices: none -> 116 us  [the longest x30 98.8 us: line_sum(): moving = lax.ppermute(mine, 'ctx', pairs)]
    dot_general x58 -> x26, matrix products: 199 us -> 82.5 us  [the longest x1 7.02 us: body(): jnp.einsum('erd,efd->erf', grad_made, w_down, preferred_element_type=F32)]
    ppermute x0 -> x37, starting transfers between devices: none -> 87.9 us  [the longest x30 80.2 us: line_sum(): moving = lax.ppermute(mine, 'ctx', pairs)]
    psum x1 -> x0, blocking collectives: 44 us -> none  [body(): lax.psum((grad_norm1, grad_norm2, grad_router), ('seq', 'ctx', 'mp'))]
    reduce_sum x14 -> x2, other arithmetic: 40.1 us -> 1.14 us  [the longest x1 0.96 us: body(): jnp.sum(place.astype(F32) * gates_mine[:, None, :], axis=-1)[..., None]]
    unnamed x14 -> x2, waiting for transfers between devices: 38.8 us -> 0.7 us
  transfers between devices with their start and end apart: 16 -> 39, of which waited for: 14 -> 15; matrix products, arithmetic and copies ran while one was open for 11% -> 25% of each run, Pallas kernels for 0% -> 33%
where the time goes in v1:
time: 539 us; the launch traced here: 533 us
  Pallas kernels  174 us (32%)
  waiting for transfers between devices  117 us (22%)
  starting transfers between devices  88 us (16%)
  matrix products  86 us (16%)
  other arithmetic  32.3 us (6%)
  local copies, waits for them, and re-layouts  19.6 us (4%)
  between operations  15.7 us (3%)
    ppermute x30, waiting for transfers between devices, line_sum(): moving = lax.ppermute(mine, 'ctx', pairs)  98.8 us
    ppermute x30, starting transfers between devices, line_sum(): moving = lax.ppermute(mine, 'ctx', pairs)  80.2 us
    pallas_call x1, Pallas kernels, attend_back(): pl.pallas_call(functools.partial(attend_back_kernel, n), out_shape=(jax.S...  42.4 us
    pallas_call x1, Pallas kernels, mid_back(): pl.pallas_call(functools.partial(mid_back_kernel, chunks), out_shape=(jax...  31.6 us
    pallas_call x1, Pallas kernels, mid_forward(): pl.pallas_call(functools.partial(mid_forward_kernel, chunks), out_shape=(...  30.5 us
    pallas_call x1, Pallas kernels, attend(): pl.pallas_call(functools.partial(attend_kernel, n), out_shape=(jax.ShapeD...  26.4 us
    pallas_call x1, Pallas kernels, small_sum(): pl.pallas_call(functools.partial(small_sum_kernel, sizes), out_shape=jax....  25 us
    pallas_call x1, Pallas kernels, last(): pl.pallas_call(functools.partial(last_kernel, chunks), out_shape=jax.Shap...  18.6 us
  transfers between devices with their start and end apart: 39, of which 15 were waited for; matrix products, arithmetic and copies ran while one was open for 25% of the time, Pallas kernels for 33%

profile of v1, /device:TPU:16, one launch (start us, length us, event | category | flops | bytes accessed | tf_op | source)
XLA Modules:
  0.0 533.0 jit_solution(1803923327684597680)
XLA Ops:
  19.0 26.4 %attend.1 = (f32[384,640]{1,0:T(8,128)}, bf16[384,640]{1,0:T(8,128)(2,1)}, f32[6,1,640]{2,1,0:T(1,128)}, bf16[4,640,256]{2,1,0:T(8,128)(2,1)}) custom-call(bf16[384,640]{1,0:T(8,128)(2,1)} %fusion.25.q_ref, bf16[640,128]{1,0:T(8,128)(2,1)} %convolution_convert_fusion.13.k_ref, bf16[640,128]{1,0:T(8,128)(2,1)} %convolution_convert_fusion.12.v_ref), custom_call_target="tpu_custom_call" | custom-call | tf_op jit(solution)/shard_map/attend/pallas_call | solution.py:155
  49.0 30.5 %mid_forward.1 = (f32[160,1536]{1,0:T(8,128)}, bf16[4,160,1536]{2,1,0:T(8,128)(2,1)}) custom-call(bf16[4,160,1536]{2,1,0:T(8,128)(2,1)} %bitcast.68, bf16[160,1536]{1,0:T(8,128)(2,1)} %constant_dynamic-slice_fusion.18.x_ref, f32[1,1536]{1,0:T(1,128)} %reshape.88.gain), custom_call_target="tpu_custom_call" | custom-call | tf_op jit(solution)/shard_map/mid_forward/pallas_call | solution.py:423
  93.2 5.4 %fusion.77 = f32[2,200,1024]{2,1,0:T(8,128)} fusion(bf16[2,200,1536]{2,1,0:T(8,128)(2,1)S(1)} %convolution_convert_fusion.4, bf16[2,1536,1024]{2,1,0:T(8,128)(2,1)} %param.22), kind=kOutput, calls=%fused_computation.169 | convolution fusion | flops 1258291200 | bytes 9158656 | tf_op jit(solution)/shard_map/erd,edf->erf/dot_general | solution.py:664
  98.6 5.4 %fusion.76 = f32[2,200,1024]{2,1,0:T(8,128)} fusion(bf16[2,200,1536]{2,1,0:T(8,128)(2,1)S(1)} %convolution_convert_fusion.4, bf16[2,1536,1024]{2,1,0:T(8,128)(2,1)} %param.21), kind=kOutput, calls=%fused_computation.168 | convolution fusion | flops 1258291200 | bytes 9158656 | tf_op jit(solution)/shard_map/erd,edf->erf/dot_general | solution.py:663
  108.5 7.0 %multiply_convert_fusion = (bf16[2,200,1024]{2,1,0:T(8,128)(2,1)}, bf16[2,200,1024]{2,1,0:T(8,128)(2,1)}, bf16[2,200,1024]{2,1,0:T(8,128)(2,1)S(1)}) fusion(f32[2,200,1024]{2,1,0:T(8,128)S(1)} %copy-done.8, f32[2,200,1024]{2,1,0:T(8,128)S(1)} %copy-done.7, bf16[2,200,1536]{2,1,0:T(8,128)(2,1)} %get-tuple-element.110, bf16[2,1024,1536]{2,1,0:T(8,128)(2,1)} %param.23), kind=kOutput, calls=%fused_computation.43 | convolution fusion | flops 1264435200 | bytes 13254656 | tf_op jit(solution)/shard_map/erd,efd->erf/dot_general | solution.py:669
  133.8 31.6 %mid_back.1 = (f32[160,1536]{1,0:T(8,128)}, bf16[4,160,1536]{2,1,0:T(8,128)(2,1)}, f32[160,64]{1,0:T(8,128)}, f32[8,1536]{1,0:T(8,128)}) custom-call(bf16[4,160,1664]{2,1,0:T(8,128)(2,1)} %bitcast.67, f32[160,1536]{1,0:T(8,128)} %get-tuple-element.25.resid_ref, f32[1,1536]{1,0:T(1,128)} %reshape.88.gain, bf16[160,1536]{1,0:T(8,128)(2,1)} %cot.1, ...), custom_call_target="tpu_custom_call" | custom-call | tf_op jit(solution)/shard_map/mid_back/pallas_call | solution.py:466
  171.4 42.4 %attend_back.1 = (bf16[384,640]{1,0:T(8,128)(2,1)}, bf16[640,256]{1,0:T(8,128)(2,1)}) custom-call(bf16[384,640]{1,0:T(8,128)(2,1)} %fusion.25.q_ref, bf16[384,640]{1,0:T(8,128)(2,1)} %fusion.23.do_ref, f32[384,640]{1,0:T(8,128)} %get-tuple-element.28.o_ref, f32[6,1,640]{2,1,0:T(1,128)} %get-tuple-element.29.lse_ref, ...), custom_call_target="tpu_custom_call" | custom-call | tf_op jit(solution)/shard_map/attend_back/pallas_call | solution.py:278
  230.7 6.0 %fusion.3 = (f32[1536]{0:T(1024)S(1)}, bf16[640,1536]{1,0:T(8,128)(2,1)}) fusion(bf16[640,1536]{1,0:T(8,128)(2,1)S(1)} %copy-done.3, f32[640]{0:T(1024)S(1)} %copy-done.28, bf16[1536,128]{1,0:T(8,128)(2,1)S(1)} %copy-done.23, bf16[640,256]{1,0:T(8,128)(2,1)} %get-tuple-element.32, f32[640,1536]{1,0:T(8,128)} %fusion.79, f32[640,1536]{1,0:T(8,128)} %fusion.48), kind=kOutput, calls=%fused_computation.6 | convolution fusion | flops 258537984 | bytes 12362240 | tf_op jit(solution)/shard_map/tf,df->td/dot_general | solution.py:730
  237.4 25.0 %small_sum.1 = f32[16,1536]{1,0:T(8,128)} custom-call(f32[16,1536]{1,0:T(8,128)} %maximum_maximum_fusion.x_ref), custom_call_target="tpu_custom_call" | custom-call | tf_op jit(solution)/shard_map/small_sum/pallas_call | solution.py:550
  266.4 18.6 %last.1 = f32[160,1536]{1,0:T(8,128)} custom-call(bf16[4,160,1536]{2,1,0:T(8,128)(2,1)} %bitcast.66, bf16[160,1536]{1,0:T(8,128)(2,1)} %constant_dynamic-slice_fusion.18.x_ref, f32[1,1536]{1,0:T(1,128)} %reshape.93.gain, f32[160,1536]{1,0:T(8,128)} %get-tuple-element.33.dresid_ref), custom_call_target="tpu_custom_call" | custom-call | tf_op jit(solution)/shard_map/last/pallas_call | solution.py:496
  300.3 17.5 %collective-permute-done = bf16[768,640]{0,1:T(8,128)(2,1)S(1)} collective-permute-done((bf16[768,640]{0,1:T(8,128)(2,1)S(1)}, bf16[768,640]{0,1:T(8,128)(2,1)S(1)}, u32[]{:S(2)}, u32[]{:S(2)}) %collective-permute-start) | collective-permute-done | bytes 983072 | tf_op jit(solution)/shard_map/ppermute | solution.py:721
  333.4 16.3 %collective-permute-start.13 = (bf16[192,384]{1,0:T(8,128)(2,1)S(1)}, bf16[192,384]{1,0:T(8,128)(2,1)S(1)}, u32[]{:S(2)}, u32[]{:S(2)}) collective-permute-start(bf16[192,384]{1,0:T(8,128)(2,1)S(1)} %add_convert_fusion.18), channel_id=1, source_target_pairs={{4,0},{8,4},{12,8},{5,1},{9,5},{13,9},{6,2},{10,6},{14,10},{7,3},{... | collective-permute-start | bytes 442376 | tf_op jit(solution)/shard_map/ppermute | solution.py:579
  355.1 4.3 collective-permute-done.2
  361.2 4.3 collective-permute-start.5
  368.9 7.2 %collective-permute-done.26 = bf16[2,192,1024]{2,1,0:T(8,128)(2,1)S(1)} collective-permute-done((bf16[2,192,1024]{2,1,0:T(8,128)(2,1)S(1)}, bf16[2,192,1024]{2,1,0:T(8,128)(2,1)S(1)}, u32[]{:S(2)}, u32[]{:S(2)}) %collective-permute-start.26) | collective-permute-done | bytes 786464 | tf_op jit(solution)/shard_map/ppermute | solution.py:579
  377.5 22.6 %collective-permute-done.5 = bf16[192,640]{0,1:T(8,128)(2,1)S(1)} collective-permute-done((bf16[192,640]{0,1:T(8,128)(2,1)S(1)}, bf16[192,640]{0,1:T(8,128)(2,1)S(1)}, u32[]{:S(2)}, u32[]{:S(2)}) %collective-permute-start.5) | collective-permute-done | bytes 245792 | tf_op jit(solution)/shard_map/ppermute | solution.py:579
  405.1 4.5 collective-permute-start.6
  409.6 5.3 collective-permute-start.27
  420.7 12.6 %collective-permute-start.35 = (bf16[2,128,1536]{2,1,0:T(8,128)(2,1)}, bf16[2,128,1536]{2,1,0:T(8,128)(2,1)}, u32[]{:S(2)}, u32[]{:S(2)}) collective-permute-start(bf16[2,128,1536]{2,1,0:T(8,128)(2,1)} %get-tuple-element.82), channel_id=1, source_target_pairs={{8,4},{12,8},{9,5},{13,9},{10,6},{14,10},{11,7},{15,11},{24,20},{2... | collective-permute-start | bytes 2359304 | tf_op jit(solution)/shard_map/ppermute | solution.py:579
  445.4 12.4 %collective-permute-done.20 = bf16[2,192,1024]{2,1,0:T(8,128)(2,1)} collective-permute-done((bf16[2,192,1024]{2,1,0:T(8,128)(2,1)}, bf16[2,192,1024]{2,1,0:T(8,128)(2,1)}, u32[]{:S(2)}, u32[]{:S(2)}) %collective-permute-start.20) | collective-permute-done | bytes 786464 | tf_op jit(solution)/shard_map/ppermute | solution.py:579
  462.2 12.4 %collective-permute-done.35 = bf16[2,128,1536]{2,1,0:T(8,128)(2,1)} collective-permute-done((bf16[2,128,1536]{2,1,0:T(8,128)(2,1)}, bf16[2,128,1536]{2,1,0:T(8,128)(2,1)}, u32[]{:S(2)}, u32[]{:S(2)}) %collective-permute-start.35) | collective-permute-done | bytes 786464 | tf_op jit(solution)/shard_map/ppermute | solution.py:579
  484.0 7.4 %collective-permute-done.28 = bf16[2,192,1024]{2,1,0:T(8,128)(2,1)} collective-permute-done((bf16[2,192,1024]{2,1,0:T(8,128)(2,1)}, bf16[2,192,1024]{2,1,0:T(8,128)(2,1)}, u32[]{:S(2)}, u32[]{:S(2)}) %collective-permute-start.28) | collective-permute-done | bytes 786464 | tf_op jit(solution)/shard_map/ppermute | solution.py:579
  494.4 13.9 %collective-permute-done.21 = bf16[2,192,1024]{2,1,0:T(8,128)(2,1)} collective-permute-done((bf16[2,192,1024]{2,1,0:T(8,128)(2,1)}, bf16[2,192,1024]{2,1,0:T(8,128)(2,1)}, u32[]{:S(2)}, u32[]{:S(2)}) %collective-permute-start.21) | collective-permute-done | bytes 786464 | tf_op jit(solution)/shard_map/ppermute | solution.py:579
  511.5 10.2 %collective-permute-done.36 = bf16[2,128,1536]{2,1,0:T(8,128)(2,1)} collective-permute-done((bf16[2,128,1536]{2,1,0:T(8,128)(2,1)}, bf16[2,128,1536]{2,1,0:T(8,128)(2,1)}, u32[]{:S(2)}, u32[]{:S(2)}) %collective-permute-start.36) | collective-permute-done | bytes 786464 | tf_op jit(solution)/shard_map/ppermute | solution.py:579
  (261 shorter events, 168.2 us)
Async XLA Ops:
  7.2 96.8 %all-gather.2.cloned.1.call-start = ((), (), s32[]{:S(2)}) async-start(), calls=%async_computation.2 | async-start | bytes 2457600 | tf_op jit(solution)/shard_map/all_gather | solution.py:619
  8.0 473.9 %reduce-scatter.2.cloned.1.call-start = ((), (), s32[]{:S(2)}) async-start(), calls=%async_computation.1 | async-start | bytes 2457600 | tf_op jit(solution)/shard_map/reduce_scatter | solution.py:689
  83.4 201.9 %collective-permute-start.14 = (bf16[2,200,768]{2,1,0:T(8,128)(2,1)}, bf16[2,200,768]{2,1,0:T(8,128)(2,1)}, u32[]{:S(2)}, u32[]{:S(2)}) collective-permute-start(bf16[2,200,768]{2,1,0:T(8,128)(2,1)} %get-tuple-element.94), channel_id=1, source_target_pairs={{0,16},{16,0},{1,17},{17,1},{2,18},{18,2},{3,19},{19,3},{4,20},{20... | collective-permute-start | bytes 1843208 | tf_op jit(solution)/shard_map/ppermute | solution.py:706
  107.9 220.7 %collective-permute-start.30 = (bf16[2,200,1536]{2,1,0:T(8,128)(2,1)}, bf16[2,200,1536]{2,1,0:T(8,128)(2,1)}, u32[]{:S(2)}, u32[]{:S(2)}) collective-permute-start(bf16[2,200,1536]{2,1,0:T(8,128)(2,1)} %get-tuple-element.110), channel_id=1, source_target_pairs={{0,16},{16,0},{1,17},{17,1},{2,18},{18,2},{3,19},{19,3},{4,20},{20... | collective-permute-start | bytes 3686408 | tf_op jit(solution)/shard_map/ppermute | solution.py:703
  118.3 174.0 %collective-permute-start.15 = (bf16[2,200,1024]{2,1,0:T(8,128)(2,1)}, bf16[2,200,1024]{2,1,0:T(8,128)(2,1)}, u32[]{:S(2)}, u32[]{:S(2)}) collective-permute-start(bf16[2,200,1024]{2,1,0:T(8,128)(2,1)} %get-tuple-element.79), channel_id=1, source_target_pairs={{0,16},{16,0},{1,17},{17,1},{2,18},{18,2},{3,19},{19,3},{4,20},{20... | collective-permute-start | bytes 2457608 | tf_op jit(solution)/shard_map/ppermute | solution.py:703
  123.5 163.9 %collective-permute-start.22 = (bf16[2,200,1024]{2,1,0:T(8,128)(2,1)}, bf16[2,200,1024]{2,1,0:T(8,128)(2,1)}, u32[]{:S(2)}, u32[]{:S(2)}) collective-permute-start(bf16[2,200,1024]{2,1,0:T(8,128)(2,1)} %get-tuple-element.78), channel_id=1, source_target_pairs={{0,16},{16,0},{1,17},{17,1},{2,18},{18,2},{3,19},{19,3},{4,20},{20... | collective-permute-start | bytes 2457608 | tf_op jit(solution)/shard_map/ppermute | solution.py:703
  229.8 35.6 %collective-permute-start.7 = (bf16[768,384]{1,0:T(8,128)(2,1)S(1)}, bf16[768,384]{1,0:T(8,128)(2,1)S(1)}, u32[]{:S(2)}, u32[]{:S(2)}) collective-permute-start(bf16[768,384]{1,0:T(8,128)(2,1)S(1)} %constant_dynamic-slice_fusion.12), channel_id=1, source_target_pairs={{0,16},{16,0},{1,17},{17,1},{2,18},{18,2},{3,19},{19,3},{4,20},{20... | collective-permute-start | bytes 1769480 | tf_op jit(solution)/shard_map/ppermute | solution.py:721
  285.1 42.7 %collective-permute-start.29 = (bf16[2,200,512]{2,1,0:T(8,128)(2,1)S(1)}, bf16[2,200,512]{2,1,0:T(8,128)(2,1)S(1)}, u32[]{:S(2)}, u32[]{:S(2)}) collective-permute-start(bf16[2,200,512]{2,1,0:T(8,128)(2,1)S(1)} %get-tuple-element.100), channel_id=1, source_target_pairs={{0,16},{16,0},{1,17},{17,1},{2,18},{18,2},{3,19},{19,3},{4,20},{20... | collective-permute-start | bytes 1228808 | tf_op jit(solution)/shard_map/ppermute | solution.py:706
  285.3 32.5 %collective-permute-start = (bf16[768,640]{0,1:T(8,128)(2,1)S(1)}, bf16[768,640]{0,1:T(8,128)(2,1)S(1)}, u32[]{:S(2)}, u32[]{:S(2)}) collective-permute-start(bf16[768,640]{0,1:T(8,128)(2,1)S(1)} %fusion.32), channel_id=1, source_target_pairs={{0,16},{16,0},{1,17},{17,1},{2,18},{18,2},{3,19},{19,3},{4,20},{20... | collective-permute-start | bytes 2949128 | tf_op jit(solution)/shard_map/ppermute | solution.py:721
  297.2 64.0 %collective-permute-start.23 = (bf16[2,192,1024]{2,1,0:T(8,128)(2,1)S(1)}, bf16[2,192,1024]{2,1,0:T(8,128)(2,1)S(1)}, u32[]{:S(2)}, u32[]{:S(2)}) collective-permute-start(bf16[2,192,1024]{2,1,0:T(8,128)(2,1)S(1)} %get-tuple-element.87), channel_id=1, source_target_pairs={{0,4},{1,5},{2,6},{3,7},{16,20},{17,21},{18,22},{19,23}} | collective-permute-start | bytes 2359304 | tf_op jit(solution)/shard_map/ppermute | solution.py:579
  299.5 66.3 %collective-permute-start.16 = (bf16[2,192,1024]{2,1,0:T(8,128)(2,1)S(1)}, bf16[2,192,1024]{2,1,0:T(8,128)(2,1)S(1)}, u32[]{:S(2)}, u32[]{:S(2)}) collective-permute-start(bf16[2,192,1024]{2,1,0:T(8,128)(2,1)S(1)} %get-tuple-element.91), channel_id=1, source_target_pairs={{0,4},{1,5},{2,6},{3,7},{16,20},{17,21},{18,22},{19,23}} | collective-permute-start | bytes 2359304 | tf_op jit(solution)/shard_map/ppermute | solution.py:579
  359.4 45.6 %collective-permute-start.19 = (bf16[2,192,1024]{2,1,0:T(8,128)(2,1)S(1)}, bf16[2,192,1024]{2,1,0:T(8,128)(2,1)S(1)}, u32[]{:S(2)}, u32[]{:S(2)}) collective-permute-start(bf16[2,192,1024]{2,1,0:T(8,128)(2,1)S(1)} %get-tuple-element.92), channel_id=1, source_target_pairs={{12,8},{13,9},{14,10},{15,11},{28,24},{29,25},{30,26},{31,27}} | collective-permute-start | bytes 2359304 | tf_op jit(solution)/shard_map/ppermute | solution.py:579
  361.2 38.9 %collective-permute-start.5 = (bf16[192,640]{0,1:T(8,128)(2,1)S(1)}, bf16[192,640]{0,1:T(8,128)(2,1)S(1)}, u32[]{:S(2)}, u32[]{:S(2)}) collective-permute-start(bf16[192,640]{0,1:T(8,128)(2,1)S(1)} %get-tuple-element.96), channel_id=1, source_target_pairs={{8,4},{12,8},{9,5},{13,9},{10,6},{14,10},{11,7},{15,11},{24,20},{2... | collective-permute-start | bytes 737288 | tf_op jit(solution)/shard_map/ppermute | solution.py:579
  365.8 35.7 %collective-permute-start.24 = (bf16[2,192,1024]{2,1,0:T(8,128)(2,1)S(1)}, bf16[2,192,1024]{2,1,0:T(8,128)(2,1)S(1)}, u32[]{:S(2)}, u32[]{:S(2)}) collective-permute-start(bf16[2,192,1024]{2,1,0:T(8,128)(2,1)S(1)} %add_convert_fusion.8), channel_id=1, source_target_pairs={{0,4},{4,8},{1,5},{5,9},{2,6},{6,10},{3,7},{7,11},{16,20},{20,24},... | collective-permute-start | bytes 2359304 | tf_op jit(solution)/shard_map/ppermute | solution.py:579
  367.4 42.2 %collective-permute-start.17 = (bf16[2,192,1024]{2,1,0:T(8,128)(2,1)S(1)}, bf16[2,192,1024]{2,1,0:T(8,128)(2,1)S(1)}, u32[]{:S(2)}, u32[]{:S(2)}) collective-permute-start(bf16[2,192,1024]{2,1,0:T(8,128)(2,1)S(1)} %add_convert_fusion.12), channel_id=1, source_target_pairs={{0,4},{4,8},{1,5},{5,9},{2,6},{6,10},{3,7},{7,11},{16,20},{20,24},... | collective-permute-start | bytes 2359304 | tf_op jit(solution)/shard_map/ppermute | solution.py:579
  376.2 40.7 %collective-permute-start.34 = (bf16[2,128,1536]{2,1,0:T(8,128)(2,1)S(1)}, bf16[2,128,1536]{2,1,0:T(8,128)(2,1)S(1)}, u32[]{:S(2)}, u32[]{:S(2)}) collective-permute-start(bf16[2,128,1536]{2,1,0:T(8,128)(2,1)S(1)} %get-tuple-element.84), channel_id=1, source_target_pairs={{12,8},{13,9},{14,10},{15,11},{28,24},{29,25},{30,26},{31,27}} | collective-permute-start | bytes 2359304 | tf_op jit(solution)/shard_map/ppermute | solution.py:579
  416.9 40.8 %collective-permute-start.20 = (bf16[2,192,1024]{2,1,0:T(8,128)(2,1)}, bf16[2,192,1024]{2,1,0:T(8,128)(2,1)}, u32[]{:S(2)}, u32[]{:S(2)}) collective-permute-start(bf16[2,192,1024]{2,1,0:T(8,128)(2,1)} %get-tuple-element.90), channel_id=1, source_target_pairs={{8,4},{12,8},{9,5},{13,9},{10,6},{14,10},{11,7},{15,11},{24,20},{2... | collective-permute-start | bytes 2359304 | tf_op jit(solution)/shard_map/ppermute | solution.py:579
  420.7 53.9 %collective-permute-start.35 = (bf16[2,128,1536]{2,1,0:T(8,128)(2,1)}, bf16[2,128,1536]{2,1,0:T(8,128)(2,1)}, u32[]{:S(2)}, u32[]{:S(2)}) collective-permute-start(bf16[2,128,1536]{2,1,0:T(8,128)(2,1)} %get-tuple-element.82), channel_id=1, source_target_pairs={{8,4},{12,8},{9,5},{13,9},{10,6},{14,10},{11,7},{15,11},{24,20},{2... | collective-permute-start | bytes 2359304 | tf_op jit(solution)/shard_map/ppermute | solution.py:579
  435.9 43.1 %collective-permute-start.25 = (bf16[2,192,1024]{2,1,0:T(8,128)(2,1)S(1)}, bf16[2,192,1024]{2,1,0:T(8,128)(2,1)S(1)}, u32[]{:S(2)}, u32[]{:S(2)}) collective-permute-start(bf16[2,192,1024]{2,1,0:T(8,128)(2,1)S(1)} %get-tuple-element.85), channel_id=1, source_target_pairs={{0,4},{4,8},{8,12},{1,5},{5,9},{9,13},{2,6},{6,10},{10,14},{3,7},{... | collective-permute-start | bytes 2359304 | tf_op jit(solution)/shard_map/ppermute | solution.py:579
  437.8 56.6 %collective-permute-start.18 = (bf16[2,192,1024]{2,1,0:T(8,128)(2,1)S(1)}, bf16[2,192,1024]{2,1,0:T(8,128)(2,1)}, u32[]{:S(2)}, u32[]{:S(2)}) collective-permute-start(bf16[2,192,1024]{2,1,0:T(8,128)(2,1)S(1)} %get-tuple-element.89), channel_id=1, source_target_pairs={{0,4},{4,8},{8,12},{1,5},{5,9},{9,13},{2,6},{6,10},{10,14},{3,7},{... | collective-permute-start | bytes 2359304 | tf_op jit(solution)/shard_map/ppermute | solution.py:579
  440.9 70.6 %collective-permute-start.33 = (bf16[2,128,1536]{2,1,0:T(8,128)(2,1)}, bf16[2,128,1536]{2,1,0:T(8,128)(2,1)}, u32[]{:S(2)}, u32[]{:S(2)}) collective-permute-start(bf16[2,128,1536]{2,1,0:T(8,128)(2,1)} %get-tuple-element.81), channel_id=1, source_target_pairs={{0,4},{4,8},{8,12},{1,5},{5,9},{9,13},{2,6},{6,10},{10,14},{3,7},{... | collective-permute-start | bytes 2359304 | tf_op jit(solution)/shard_map/ppermute | solution.py:579
  457.7 33.7 %collective-permute-start.28 = (bf16[2,192,1024]{2,1,0:T(8,128)(2,1)}, bf16[2,192,1024]{2,1,0:T(8,128)(2,1)}, u32[]{:S(2)}, u32[]{:S(2)}) collective-permute-start(bf16[2,192,1024]{2,1,0:T(8,128)(2,1)} %add_convert_fusion.5), channel_id=1, source_target_pairs={{4,0},{8,4},{12,8},{5,1},{9,5},{13,9},{6,2},{10,6},{14,10},{7,3},{... | collective-permute-start | bytes 2359304 | tf_op jit(solution)/shard_map/ppermute | solution.py:579
  474.6 33.7 %collective-permute-start.21 = (bf16[2,192,1024]{2,1,0:T(8,128)(2,1)}, bf16[2,192,1024]{2,1,0:T(8,128)(2,1)}, u32[]{:S(2)}, u32[]{:S(2)}) collective-permute-start(bf16[2,192,1024]{2,1,0:T(8,128)(2,1)} %add_convert_fusion.9), channel_id=1, source_target_pairs={{4,0},{8,4},{12,8},{5,1},{9,5},{13,9},{6,2},{10,6},{14,10},{7,3},{... | collective-permute-start | bytes 2359304 | tf_op jit(solution)/shard_map/ppermute | solution.py:579
  479.9 41.7 %collective-permute-start.36 = (bf16[2,128,1536]{2,1,0:T(8,128)(2,1)}, bf16[2,128,1536]{2,1,0:T(8,128)(2,1)}, u32[]{:S(2)}, u32[]{:S(2)}) collective-permute-start(bf16[2,128,1536]{2,1,0:T(8,128)(2,1)} %add_convert_fusion.1), channel_id=1, source_target_pairs={{4,0},{8,4},{12,8},{5,1},{9,5},{13,9},{6,2},{10,6},{14,10},{7,3},{... | collective-permute-start | bytes 2359304 | tf_op jit(solution)/shard_map/ppermute | solution.py:579
  (63 other events, 1164.4 us)
Sparse Core Ops, SparseCore 0:
  9.6 22.9 all-gather.1
  226.5 32.0 reduce-scatter.1

commit v2 on v1

--- a/solution.py
+++ b/solution.py
@@ -17,6 +17,10 @@
 MIB = 2**20
 
 
+def cost(us):
+    return pl.CostEstimate(flops=0, bytes_accessed=int(us * 3.6e6), transcendentals=0)
+
+
 def params(collective_id, mib=56):
     return pltpu.CompilerParams(
         collective_id=collective_id, has_side_effects=True, vmem_limit_bytes=mib * MIB
@@ -31,18 +35,179 @@
     return jnp.dot(a, b, preferred_element_type=F32)
 
 
-def line_barrier(c, n, up, down):
-    sem = pltpu.get_barrier_semaphore()
+class Spread:
+    def __init__(self, n, own, below, above, all_ref, send, recv, local):
+        self.n, self.own, self.below, self.above, self.all = n, own, below, above, all_ref
+        self.send, self.recv, self.local = send, recv, local
+        s, self.c, m = lax.axis_index("seq"), lax.axis_index("ctx"), lax.axis_index("mp")
+        self.lower, self.upper = lax.rem(self.c + n - 1, n), lax.rem(self.c + 1, n)
+        self.up, self.down = (s, self.upper, m), (s, self.lower, m)
+        self.inner = jnp.logical_and(self.c > 0, self.c < n - 1)
+
+    def move(self, b, src, device):
+        return pltpu.make_async_remote_copy(
+            src_ref=src,
+            dst_ref=self.all.at[b],
+            send_sem=self.send.at[b],
+            recv_sem=self.recv.at[b],
+            device_id=device,
+            device_id_type=MESH,
+        )
+
+    def keep(self, i, src, b):
+        return pltpu.make_async_copy(src, self.all.at[b], self.local.at[i])
+
+    def start(self):
+        @pl.when(self.inner)
+        def _():
+            self.move(self.lower, self.below, self.up).start()
+            self.move(self.upper, self.above, self.down).start()
+
+        self.keep(0, self.own, self.c).start()
+
+        @pl.when(self.c > 0)
+        def _():
+            self.keep(1, self.below, self.lower).start()
+
+        @pl.when(self.c < self.n - 1)
+        def _():
+            self.keep(2, self.above, self.upper).start()
+
+    def tick(self, i):
+        c, n = self.c, self.n
+
+        @pl.when(c - 1 - i >= 0)
+        def _():
+            b = jnp.maximum(c - 1 - i, 0)
+            self.move(b, self.all.at[b], self.up).wait_recv()
+
+            @pl.when(c < n - 1)
+            def _():
+                self.move(b, self.all.at[b], self.up).start()
+
+        @pl.when(c + 1 + i <= n - 1)
+        def _():
+            b = jnp.minimum(c + 1 + i, n - 1)
+            self.move(b, self.all.at[b], self.down).wait_recv()
+
+            @pl.when(c > 0)
+            def _():
+                self.move(b, self.all.at[b], self.down).start()
+
+    def ticks(self, first):
+        def later(i, carry):
+            self.tick(i)
+            return carry
+
+        lax.fori_loop(first, self.n - 1, later, 0)
+
+    def finish(self):
+        self.keep(0, self.own, self.c).wait()
+
+        @pl.when(self.c > 0)
+        def _():
+            self.keep(1, self.below, self.lower).wait()
+
+        @pl.when(self.c < self.n - 1)
+        def _():
+            self.keep(2, self.above, self.upper).wait()
+
+        @pl.when(self.inner)
+        def _():
+            def sent(b, carry):
+                @pl.when(b != self.c)
+                def _():
+                    self.move(b, self.all.at[b], self.up).wait_send()
+
+                return carry
+
+            lax.fori_loop(0, self.n, sent, 0)
+
+
+class Neighbours:
+    def __init__(self, n, own, below, above, send, recv):
+        self.n, self.own, self.below, self.above, self.send, self.recv = n, own, below, above, send, recv
+        s, self.c, m = lax.axis_index("seq"), lax.axis_index("ctx"), lax.axis_index("mp")
+        self.up, self.down = (s, lax.rem(self.c + 1, n), m), (s, lax.rem(self.c + n - 1, n), m)
+
+    def move(self, way):
+        return pltpu.make_async_remote_copy(
+            src_ref=self.own,
+            dst_ref=self.below if way == 0 else self.above,
+            send_sem=self.send.at[way],
+            recv_sem=self.recv.at[way],
+            device_id=self.up if way == 0 else self.down,
+            device_id_type=MESH,
+        )
+
+    def start_up(self):
+        @pl.when(self.c < self.n - 1)
+        def _():
+            self.move(0).start()
+
+    def start_down(self):
+        @pl.when(self.c > 0)
+        def _():
+            self.move(1).start()
+
+    def finish(self):
+        @pl.when(self.c > 0)
+        def _():
+            self.move(0).wait_recv()
+            self.move(1).wait_send()
+
+        @pl.when(self.c < self.n - 1)
+        def _():
+            self.move(1).wait_recv()
+            self.move(0).wait_send()
+
+
+class Peers:
+    def __init__(self, n, src_of, dst_of, send, recv):
+        self.n, self.src_of, self.dst_of, self.send, self.recv = n, src_of, dst_of, send, recv
+        self.s, self.c, self.m = lax.axis_index("seq"), lax.axis_index("ctx"), lax.axis_index("mp")
+
+    def move(self, d):
+        peer = lax.rem(self.c + d, self.n)
+        return pltpu.make_async_remote_copy(
+            src_ref=self.src_of(peer),
+            dst_ref=self.dst_of(self.c),
+            send_sem=self.send.at[d],
+            recv_sem=self.recv.at[d],
+            device_id=(self.s, peer, self.m),
+            device_id_type=MESH,
+        )
+
+    def signal(self, sem):
+        for d in range(1, self.n):
+            pl.semaphore_signal(
+                sem, inc=1, device_id=(self.s, lax.rem(self.c + d, self.n), self.m), device_id_type=MESH
+            )
+
+    def start(self):
+        for d in range(1, self.n):
+            self.move(d).start()
+
+    def finish(self):
+        for d in range(1, self.n):
+            self.move(d).wait()
+
+
+def signal_line(n, sem):
+    s, c, m = lax.axis_index("seq"), lax.axis_index("ctx"), lax.axis_index("mp")
 
     @pl.when(c > 0)
     def _():
-        pl.semaphore_signal(sem, inc=1, device_id=down, device_id_type=MESH)
+        pl.semaphore_signal(sem, inc=1, device_id=(s, lax.rem(c + n - 1, n), m), device_id_type=MESH)
 
     @pl.when(c < n - 1)
     def _():
-        pl.semaphore_signal(sem, inc=1, device_id=up, device_id_type=MESH)
-
-    pl.semaphore_wait(sem, jnp.where(c > 0, 1, 0) + jnp.where(c < n - 1, 1, 0))
+        pl.semaphore_signal(sem, inc=1, device_id=(s, lax.rem(c + 1, n), m), device_id_type=MESH)
+
+
+def line_degree(n):
+    c = lax.axis_index("ctx")
+    return jnp.where(c > 0, 1, 0) + jnp.where(c < n - 1, 1, 0)
 
 
 def pad_heads(src, dst, heads, group):
@@ -59,7 +224,29 @@
     return keys <= queries
 
 
-def attend_kernel(n, q_ref, k_ref, v_ref, o_ref, heads_ref, lse_ref, kv_ref, qpad, vt, top, tot, send, recv):
+def attend_kernel(
+    n,
+    q_ref,
+    k_ref,
+    v_ref,
+    cot_ref,
+    routes_ref,
+    o_ref,
+    heads_ref,
+    lse_ref,
+    kv_ref,
+    below_ref,
+    above_ref,
+    line_ref,
+    qpad,
+    vt,
+    top,
+    tot,
+    send,
+    recv,
+    side,
+    peers_sem,
+):
     s, c, m = lax.axis_index("seq"), lax.axis_index("ctx"), lax.axis_index("mp")
     t, kvw = k_ref.shape
     heads = q_ref.shape[0] // HEAD_SIZE
@@ -67,7 +254,12 @@
     up, down = (s, lax.rem(c + 1, n), m), (s, lax.rem(c + n - 1, n), m)
     kv_ref[0, :, :kvw] = k_ref[...]
     kv_ref[0, :, kvw:] = v_ref[...]
-    line_barrier(c, n, up, down)
+    line_ref[c] = routes_ref[...]
+    peers = Peers(n, lambda p: routes_ref, lambda i: line_ref.at[i], peers_sem.at[0], peers_sem.at[1])
+    beside = Neighbours(n, cot_ref, below_ref, above_ref, side.at[0], side.at[1])
+    sem = pltpu.get_barrier_semaphore()
+    peers.signal(sem)
+    pl.semaphore_wait(sem, n - 1)
 
     def pass_up(slot):
         return pltpu.make_async_remote_copy(
@@ -93,6 +285,8 @@
     def _():
         pass_up(0).start()
 
+    peers.start()
+    beside.start_down()
     pad_heads(q_ref, qpad, heads, group)
     top[...] = jnp.full_like(top, -1e30)
     tot[...] = jnp.zeros_like(tot)
@@ -132,6 +326,7 @@
         return carry
 
     lax.fori_loop(1, c + 1, earlier, 0)
+    beside.start_up()
     for h in range(heads):
         rows = slice(h * HEAD_SIZE, (h + 1) * HEAD_SIZE)
         done = o_ref[rows, :] / tot[h]
@@ -147,8 +342,11 @@
 
         lax.fori_loop(0, c + 1, sent, 0)
 
-
-def attend(n, qt, k, v):
+    peers.finish()
+    beside.finish()
+
+
+def attend(n, qt, k, v, cot, routes):
     t, kvw = k.shape
     qw = qt.shape[0]
     heads = qw // HEAD_SIZE
@@ -159,9 +357,12 @@
             jax.ShapeDtypeStruct((qw, t), BF16),
             jax.ShapeDtypeStruct((heads, 1, t), F32),
             jax.ShapeDtypeStruct((n, t, 2 * kvw), BF16),
+            jax.ShapeDtypeStruct(cot.shape, BF16),
+            jax.ShapeDtypeStruct(cot.shape, BF16),
+            jax.ShapeDtypeStruct((n,) + routes.shape, jnp.int32),
         ),
-        in_specs=[VMEM] * 3,
-        out_specs=(VMEM,) * 4,
+        in_specs=[VMEM] * 5,
+        out_specs=(VMEM,) * 7,
         scratch_shapes=[
             pltpu.VMEM((heads, kvw, t), BF16),
             pltpu.VMEM((kvw, t), BF16),
@@ -169,22 +370,140 @@
             pltpu.VMEM((heads, 1, t), F32),
             DMA((n,)),
             DMA((n,)),
+            DMA((2, 2)),
+            DMA((2, n)),
         ],
         compiler_params=params(0),
         name="attend",
-    )(qt, k, v)
+        cost_estimate=cost(30),
+    )(qt, k, v, cot, routes)
 
 
 def attend_back_kernel(
-    n, q_ref, do_ref, o_ref, lse_ref, kv_ref, dq_ref, dkv_ref, qpad, dopad, delta, dq, kt, part, passing, send, recv
+    n,
+    q_ref,
+    do_ref,
+    o_ref,
+    lse_ref,
+    kv_ref,
+    sum_ref,
+    own_ref,
+    below_ref,
+    above_ref,
+    dq_ref,
+    dkv_ref,
+    summed_ref,
+    all_ref,
+    qpad,
+    dopad,
+    delta,
+    dq,
+    kt,
+    part,
+    passing,
+    from_below,
+    from_above,
+    send,
+    recv,
+    spread_sem,
+    local,
 ):
     s, c, m = lax.axis_index("seq"), lax.axis_index("ctx"), lax.axis_index("mp")
     _, t, kvw2 = kv_ref.shape
     kvw = kvw2 // 2
     heads = q_ref.shape[0] // HEAD_SIZE
     group = heads // (kvw // HEAD_SIZE)
+    ex = sum_ref.shape[0]
+    chunk_rows = sum_ref.shape[1] // n
     up, down = (s, lax.rem(c + 1, n), m), (s, lax.rem(c + n - 1, n), m)
-    line_barrier(c, n, up, down)
+    spread = Spread(n, own_ref, below_ref, above_ref, all_ref, spread_sem.at[0], spread_sem.at[1], local)
+    sem = pltpu.get_barrier_semaphore()
+    signal_line(n, sem)
+    pl.semaphore_wait(sem, line_degree(n))
+
+    def remote(kind, i, src, dst, device):
+        return pltpu.make_async_remote_copy(
+            src_ref=src,
+            dst_ref=dst,
+            send_sem=send.at[kind, i],
+            recv_sem=recv.at[kind, i],
+            device_id=device,
+            device_id_type=MESH,
+        )
+
+    def own_unit(k, e):
+        return sum_ref.at[e, pl.ds(pl.multiple_of(k * chunk_rows, 16), chunk_rows), :]
+
+    def sum_up(k, e, first=False):
+        there = from_below.at[k, e]
+        return remote(1, k * ex + e, own_unit(k, e) if first else there, there, up)
+
+    def sum_down(k, e, first=False):
+        there = from_above.at[k, e]
+        return remote(2, k * ex + e, own_unit(k, e) if first else there, there, down)
+
+    units = (n - 1) * ex
+    ahead = 2
+
+    def first_up(u):
+        @pl.when(jnp.logical_and(c == 0, u < units))
+        def _():
+            @pl.when(u >= ahead)
+            def _():
+                v = jnp.maximum(u - ahead, 0)
+                sum_up(n - 1 - lax.div(v, ex), lax.rem(v, ex), True).wait_send()
+
+            w = jnp.minimum(u, units - 1)
+            sum_up(n - 1 - lax.div(w, ex), lax.rem(w, ex), True).start()
+
+    def first_down(u):
+        @pl.when(jnp.logical_and(c == n - 1, u < units))
+        def _():
+            @pl.when(u >= ahead)
+            def _():
+                v = jnp.maximum(u - ahead, 0)
+                sum_down(lax.div(v, ex), lax.rem(v, ex), True).wait_send()
+
+            w = jnp.minimum(u, units - 1)
+            sum_down(lax.div(w, ex), lax.rem(w, ex), True).start()
+
+    first_up(0)
+    first_down(0)
+    spread.start()
+
+    def tick(i):
+        first_up(i + 1)
+        first_down(i + 1)
+        for hop in range(1, n - 1):
+
+            @pl.when(i == hop * ex)
+            def _():
+                spread.tick(hop)
+
+        u = i - c
+        k = n - 1 - lax.div(jnp.maximum(u, 0), ex)
+        e = lax.rem(jnp.maximum(u, 0), ex)
+
+        @pl.when(jnp.logical_and(c > 0, jnp.logical_and(u >= 0, k > c)))
+        def _():
+            there = jnp.maximum(k, 0)
+            sum_up(there, e).wait_recv()
+            from_below[there, e] = (own_unit(there, e)[...].astype(F32) + from_below[there, e].astype(F32)).astype(BF16)
+            sum_up(there, e).start()
+
+        v = i - (n - 1 - c)
+        kd = lax.div(jnp.maximum(v, 0), ex)
+        ed = lax.rem(jnp.maximum(v, 0), ex)
+
+        @pl.when(jnp.logical_and(c < n - 1, jnp.logical_and(v >= 0, kd < c)))
+        def _():
+            there = jnp.minimum(kd, n - 1)
+            sum_down(there, ed).wait_recv()
+            from_above[there, ed] = (own_unit(there, ed)[...].astype(F32) + from_above[there, ed].astype(F32)).astype(BF16)
+            sum_down(there, ed).start()
+
+    last_tick = units + n
+
     pad_heads(q_ref, qpad, heads, group)
     pad_heads(do_ref, dopad, heads, group)
     for h in range(heads):
@@ -216,14 +535,7 @@
         lax.fori_loop(0, heads, head, 0)
 
     def pass_down(j):
-        return pltpu.make_async_remote_copy(
-            src_ref=passing.at[j],
-            dst_ref=passing.at[j],
-            send_sem=send.at[j],
-            recv_sem=recv.at[j],
-            device_id=down,
-            device_id_type=MESH,
-        )
+        return remote(0, j, passing.at[j], passing.at[j], down)
 
     def gathered(j):
         acc = part.at[lax.rem(j, 2)]
@@ -251,38 +563,83 @@
         def _():
             forward(j)
 
+        tick(j)
         return carry
 
     lax.fori_loop(0, c, step, 0)
     block(c, True)
 
-    @pl.when(jnp.logical_and(c > 0, c < n - 1))
+    @pl.when(spread.inner)
     def _():
         forward(c - 1)
 
     dq_ref[...] = (dq[...] * 0.125).astype(BF16)
+
+    def later(i, carry):
+        tick(i)
+        return carry
+
+    lax.fori_loop(c, last_tick, later, 0)
     acc = gathered(c)
     dkv_ref[...] = acc[...].astype(BF16)
-
-    def sent(j, carry):
+    for e in range(ex):
+        summed_ref[e] = own_unit(c, e)[...].astype(F32)
+
+        @pl.when(c > 0)
+        def _():
+            sum_up(c, e).wait_recv()
+            summed_ref[e] = summed_ref[e] + from_below[c, e].astype(F32)
+
+        @pl.when(c < n - 1)
+        def _():
+            sum_down(c, e).wait_recv()
+            summed_ref[e] = summed_ref[e] + from_above[c, e].astype(F32)
+
+    spread.finish()
+
+    def sent_kv(j, carry):
         pass_down(j).wait_send()
         return carry
 
-    lax.fori_loop(0, c, sent, 0)
-
-
-def attend_back(n, qt, dot, o, lse, kv):
+    lax.fori_loop(0, c, sent_kv, 0)
+
+    done = jnp.where(c == 0, units - ahead, 0)
+
+    @pl.when(c < n - 1)
+    def _():
+        def sent(u, carry):
+            sum_up(n - 1 - lax.div(u, ex), lax.rem(u, ex)).wait_send()
+            return carry
+
+        lax.fori_loop(done, (n - 1 - c) * ex, sent, 0)
+
+    done_down = jnp.where(c == n - 1, units - ahead, 0)
+
+    @pl.when(c > 0)
+    def _():
+        def sent(u, carry):
+            sum_down(lax.div(u, ex), lax.rem(u, ex)).wait_send()
+            return carry
+
+        lax.fori_loop(done_down, c * ex, sent, 0)
+
+
+def attend_back(n, qt, dot, o, lse, kv, sums, own, below, above):
     qw, t = qt.shape
     heads = qw // HEAD_SIZE
     kvw = kv.shape[2] // 2
+    ex, rows, cols = sums.shape
+    chunk = (ex, rows // n, cols)
     return pl.pallas_call(
         functools.partial(attend_back_kernel, n),
         out_shape=(
             jax.ShapeDtypeStruct((qw, t), BF16),
             jax.ShapeDtypeStruct((t, 2 * kvw), BF16),
+            jax.ShapeDtypeStruct(chunk, F32),
+            jax.ShapeDtypeStruct((n,) + own.shape, BF16),
         ),
-        in_specs=[VMEM] * 5,
-        out_specs=(VMEM,) * 2,
+        in_specs=[VMEM] * 9,
+        out_specs=(VMEM,) * 4,
         scratch_shapes=[
             pltpu.VMEM((heads, kvw, t), BF16),
             pltpu.VMEM((heads, kvw, t), BF16),
@@ -291,12 +648,17 @@
             pltpu.VMEM((kvw, t), BF16),
             pltpu.VMEM((2, t, 2 * kvw), F32),
             pltpu.VMEM((n, t, 2 * kvw), BF16),
-            DMA((n,)),
-            DMA((n,)),
+            pltpu.VMEM((n,) + chunk, BF16),
+            pltpu.VMEM((n,) + chunk, BF16),
+            DMA((3, n * ex)),
+            DMA((3, n * ex)),
+            DMA((2, n)),
+            DMA((3,)),
         ],
         compiler_params=params(1),
         name="attend_back",
-    )(qt, dot, o, lse, kv)
+        cost_estimate=cost(75),
+    )(qt, dot, o, lse, kv, sums, own, below, above)
 
 
 class Mp:
@@ -312,11 +674,9 @@
         share = (part if part is not None else full).shape[1]
         self.rows = share // chunks
 
-    def barrier(self):
-        sem = pltpu.get_barrier_semaphore()
+    def signal(self, sem):
         for d in (self.sib_id, self.opp_id):
             pl.semaphore_signal(sem, inc=1, device_id=d, device_id_type=MESH)
-        pl.semaphore_wait(sem, 2)
 
     def copy(self, src, dst, i, dev):
         return pltpu.make_async_remote_copy(
@@ -341,6 +701,9 @@
     def rs_begin(self):
         self.rs_core(0).start()
         self.rs_core(1).start()
+        self.rs_forward()
+
+    def rs_forward(self):
         self.rs_core(0).wait_recv()
         for i in range(self.chunks):
             cut = self.cut(i)
@@ -403,10 +766,17 @@
     return inverse * (grad_normed - normed * jnp.mean(grad_normed * normed, axis=-1, keepdims=True))
 
 
-def mid_forward_kernel(chunks, part, x_ref, gain, resid_ref, h_ref, core_in, y_out, y_in, sems):
+def mid_forward_kernel(
+    chunks, n, part, x_ref, gain, own, below, above, resid_ref, h_ref, line_ref, core_in, y_out, y_in, sems, send, recv, local
+):
     mp = Mp(part, core_in, y_out, y_in, h_ref, sems, chunks)
-    mp.barrier()
+    spread = Spread(n, own, below, above, line_ref, send, recv, local)
+    sem = pltpu.get_barrier_semaphore()
+    mp.signal(sem)
+    signal_line(n, sem)
+    pl.semaphore_wait(sem, 2 + line_degree(n))
     mp.rs_begin()
+    spread.start()
     for i in range(chunks):
         cut = mp.cut(i)
         resid = x_ref[cut, :].astype(F32) + mp.rs_chunk(i)
@@ -414,31 +784,80 @@
         normed, _ = rms_parts(resid)
         h_ref[mp.m, cut, :] = (normed * gain[...]).astype(BF16)
         mp.ag_send(i)
+    if n > 2:
+        spread.tick(1)
     mp.ag_end()
     mp.rs_end()
-
-
-def mid_forward(part, x_mine, gain, chunks=2):
+    spread.ticks(2)
+    spread.finish()
+
+
+def mid_forward(n, part, x_mine, gain, own, below, above, chunks=2):
     _, share, width = part.shape
     return pl.pallas_call(
-        functools.partial(mid_forward_kernel, chunks),
-        out_shape=(jax.ShapeDtypeStruct((share, width), F32), jax.ShapeDtypeStruct(part.shape, BF16)),
-        in_specs=[VMEM] * 3,
-        out_specs=(VMEM,) * 2,
-        scratch_shapes=mp_scratch(share, width, chunks),
-        compiler_params=params(2),
+        functools.partial(mid_forward_kernel, chunks, n),
+        out_shape=(
+            jax.ShapeDtypeStruct((share, width), F32),
+            jax.ShapeDtypeStruct(part.shape, BF16),
+            jax.ShapeDtypeStruct((n,) + own.shape, BF16),
+        ),
+        in_specs=[VMEM] * 6,
+        out_specs=(VMEM,) * 3,
+        scratch_shapes=mp_scratch(share, width, chunks) + [DMA((n,)), DMA((n,)), DMA((3,))],
+        compiler_params=params(2, 30),
         name="mid_forward",
-    )(part, x_mine, gain)
+        cost_estimate=cost(30),
+    )(part, x_mine, gain, own, below, above)
 
 
 def mid_back_kernel(
-    chunks, part, resid_ref, gain, cot, gate_ref, router_ref, dresid_ref, db_ref, dlog_ref, gnorm_ref, core_in, y_out, y_in, sems
+    chunks,
+    n,
+    part,
+    resid_ref,
+    gain,
+    cot,
+    gate_ref,
+    router_ref,
+    rows_ref,
+    hid_ref,
+    du_ref,
+    dresid_ref,
+    db_ref,
+    dlog_ref,
+    gnorm_ref,
+    rows_line,
+    hid_line,
+    below_ref,
+    above_ref,
+    core_in,
+    y_out,
+    y_in,
+    sems,
+    side,
+    peers_sem,
+    local,
 ):
+    c = lax.axis_index("ctx")
     mp = Mp(part, core_in, y_out, y_in, db_ref, sems, chunks)
+    rows_peers = Peers(n, lambda p: rows_ref, lambda i: rows_line.at[i], peers_sem.at[0], peers_sem.at[1])
+    hid_peers = Peers(n, lambda p: hid_ref.at[p], lambda i: hid_line.at[i], peers_sem.at[2], peers_sem.at[3])
+    beside = Neighbours(n, du_ref, below_ref, above_ref, side.at[0], side.at[1])
     width = gain.shape[1]
     ex = gate_ref.shape[1]
-    mp.barrier()
+    sem = pltpu.get_barrier_semaphore()
+    mp.signal(sem)
+    rows_peers.signal(sem)
+    pl.semaphore_wait(sem, 2 + n - 1)
     mp.rs_begin()
+    beside.start_up()
+    beside.start_down()
+    rows_peers.start()
+    hid_peers.start()
+    own_rows = pltpu.make_async_copy(rows_ref, rows_line.at[c], local.at[0])
+    own_hid = pltpu.make_async_copy(hid_ref.at[c], hid_line.at[c], local.at[1])
+    own_rows.start()
+    own_hid.start()
     gnorm_ref[...] = jnp.zeros_like(gnorm_ref)
     for i in range(chunks):
         cut = mp.cut(i)
@@ -458,104 +877,118 @@
         mp.ag_send(i)
     mp.ag_end()
     mp.rs_end()
-
-
-def mid_back(part, resid, gain, cot, gate, router_t, chunks=2):
-    n, share, wide = part.shape
+    own_rows.wait()
+    own_hid.wait()
+    rows_peers.finish()
+    hid_peers.finish()
+    beside.finish()
+
+
+def mid_back(n, part, resid, gain, cot, gate, router_t, rows, hid, du, chunks=2):
+    k, share, wide = part.shape
     width = gain.shape[1]
     return pl.pallas_call(
-        functools.partial(mid_back_kernel, chunks),
+        functools.partial(mid_back_kernel, chunks, n),
         out_shape=(
             jax.ShapeDtypeStruct((share, width), F32),
-            jax.ShapeDtypeStruct((n, share, width), BF16),
+            jax.ShapeDtypeStruct((k, share, width), BF16),
             jax.ShapeDtypeStruct(gate.shape, F32),
             jax.ShapeDtypeStruct((8, width), F32),
+            jax.ShapeDtypeStruct((n,) + rows.shape, F32),
+            jax.ShapeDtypeStruct(hid.shape, BF16),
+            jax.ShapeDtypeStruct(du.shape, BF16),
+            jax.ShapeDtypeStruct(du.shape, BF16),
         ),
-        in_specs=[VMEM] * 6,
-        out_specs=(VMEM,) * 4,
-        scratch_shapes=mp_scratch(share, wide, chunks),
-        compiler_params=params(3),
+        in_specs=[VMEM] * 9,
+        out_specs=(VMEM,) * 8,
+        scratch_shapes=mp_scratch(share, wide, chunks) + [DMA((2, 2)), DMA((4, n)), DMA((2,))],
+        compiler_params=params(3, 36),
         name="mid_back",
-    )(part, resid, gain, cot, gate, router_t)
-
-
-def last_kernel(chunks, part, x_ref, gain, dresid_ref, out_ref, core_in, y_out, y_in, sems):
+        cost_estimate=cost(32),
+    )(part, resid, gain, cot, gate, router_t, rows, hid, du)
+
+
+class SmallSum:
+    def __init__(self, sizes, x_ref, out_ref, bufs, sems):
+        self.sizes, self.x, self.out, self.bufs, self.sems = sizes, x_ref, out_ref, bufs, sems
+        self.me = [lax.axis_index(a) for a in ("seq", "ctx", "mp")]
+
+    def peer(self, axis, d):
+        ids = list(self.me)
+        ids[axis] = lax.rem(self.me[axis] + d, self.sizes[axis])
+        return tuple(ids)
+
+    def signal(self, sem):
+        for axis in range(3):
+            for d in range(1, self.sizes[axis]):
+                pl.semaphore_signal(sem, inc=1, device_id=self.peer(axis, d), device_id_type=MESH)
+        return sum(self.sizes) - 3
+
+    def move(self, axis, d):
+        base = sum(self.sizes[:axis])
+        buf = self.bufs[axis]
+        return pltpu.make_async_remote_copy(
+            src_ref=buf.at[0],
+            dst_ref=buf.at[d],
+            send_sem=self.sems.at[0, base + d],
+            recv_sem=self.sems.at[1, base + d],
+            device_id=self.peer(axis, d),
+            device_id_type=MESH,
+        )
+
+    def begin(self, axis, value):
+        self.bufs[axis][0] = value
+        for d in range(1, self.sizes[axis]):
+            self.move(axis, d).start()
+
+    def end(self, axis):
+        n = self.sizes[axis]
+        for d in range(1, n):
+            self.move(axis, d).wait()
+        total = jnp.zeros(self.out.shape, F32)
+        for i in range(n):
+            total = total + self.bufs[axis][lax.rem(self.me[axis] - i + n, n)]
+        return total
+
+
+def last_kernel(
+    chunks, sizes, part, x_ref, gain, dresid_ref, small_ref, out_ref, total_ref, core_in, y_out, y_in, sems, *rest
+):
     mp = Mp(part, core_in, y_out, y_in, None, sems, chunks)
-    mp.barrier()
-    mp.rs_begin()
+    small = SmallSum(sizes, small_ref, total_ref, rest[:3], rest[3])
+    sem = pltpu.get_barrier_semaphore()
+    pl.semaphore_wait(sem, small.signal(sem))
+    mp.rs_core(0).start()
+    mp.rs_core(1).start()
+    small.begin(2, small_ref[...])
+    mp.rs_forward()
+    small.begin(0, small.end(2))
+    order = (lambda: small.begin(1, small.end(0)),)
     for i in range(chunks):
         cut = mp.cut(i)
+        if i < len(order):
+            order[i]()
         dh = mp.rs_chunk(i)
         normed, inverse = rms_parts(x_ref[cut, :].astype(F32))
         out_ref[cut, :] = dresid_ref[cut, :] + rms_grad(dh * gain[...], normed, inverse)
+    total_ref[...] = small.end(1)
     mp.rs_end()
 
 
-def last(part, x_mine, gain, dresid, chunks=2):
+def last(sizes, part, x_mine, gain, dresid, small, chunks=2):
     _, share, width = part.shape
     return pl.pallas_call(
-        functools.partial(last_kernel, chunks),
-        out_shape=jax.ShapeDtypeStruct((share, width), F32),
-        in_specs=[VMEM] * 4,
-        out_specs=VMEM,
-        scratch_shapes=mp_scratch(share, width, chunks),
-        compiler_params=params(4),
+        functools.partial(last_kernel, chunks, sizes),
+        out_shape=(jax.ShapeDtypeStruct((share, width), F32), jax.ShapeDtypeStruct(small.shape, F32)),
+        in_specs=[VMEM] * 5,
+        out_specs=(VMEM,) * 2,
+        scratch_shapes=mp_scratch(share, width, chunks)
+        + [pltpu.VMEM((n,) + small.shape, F32) for n in sizes]
+        + [DMA((2, sum(sizes)))],
+        compiler_params=params(4, 20),
         name="last",
-    )(part, x_mine, gain, dresid)
-
-
-def small_sum_kernel(sizes, x_ref, out_ref, *rest):
-    bufs, sems = rest[:3], rest[3]
-    axes = ("seq", "ctx", "mp")
-    me = [lax.axis_index(a) for a in axes]
-
-    def peer(axis, d):
-        ids = list(me)
-        ids[axis] = lax.rem(me[axis] + d, sizes[axis])
-        return tuple(ids)
-
-    bar = pltpu.get_barrier_semaphore()
-    for axis in range(3):
-        for d in range(1, sizes[axis]):
-            pl.semaphore_signal(bar, inc=1, device_id=peer(axis, d), device_id_type=MESH)
-    pl.semaphore_wait(bar, sum(sizes) - 3)
-    out_ref[...] = x_ref[...]
-    base = 0
-    for axis in (2, 0, 1):
-        n, buf = sizes[axis], bufs[axis]
-        buf[0] = out_ref[...]
-        copies = []
-        for d in range(1, n):
-            copy = pltpu.make_async_remote_copy(
-                src_ref=buf.at[0],
-                dst_ref=buf.at[d],
-                send_sem=sems.at[0, base + d],
-                recv_sem=sems.at[1, base + d],
-                device_id=peer(axis, d),
-                device_id_type=MESH,
-            )
-            copy.start()
-            copies.append(copy)
-        for copy in copies:
-            copy.wait()
-        total = jnp.zeros(out_ref.shape, F32)
-        for i in range(n):
-            total = total + buf[lax.rem(me[axis] - i + n, n)]
-        out_ref[...] = total
-        base += n
-
-
-def small_sum(sizes, x):
-    rows, width = x.shape
-    return pl.pallas_call(
-        functools.partial(small_sum_kernel, sizes),
-        out_shape=jax.ShapeDtypeStruct(x.shape, F32),
-        in_specs=[VMEM],
-        out_specs=VMEM,
-        scratch_shapes=[pltpu.VMEM((n, rows, width), F32) for n in sizes] + [DMA((2, sum(sizes)))],
-        compiler_params=params(5),
-        name="small_sum",
-    )(x)
+        cost_estimate=cost(20),
+    )(part, x_mine, gain, dresid, small)
 
 
 def line_sum(parts, n, dim):
@@ -587,6 +1020,13 @@
 
 
 SWAP = [(0, 1), (1, 0)]
+
+
+def columns(x):
+    n_seq, n_ctx = lax.axis_size("seq"), lax.axis_size("ctx")
+    size = x.shape[2] // (n_seq * n_ctx)
+    part = lambda i, j: x[:, :, (j * n_ctx + i) * size : (j * n_ctx + i + 1) * size]
+    return jnp.stack([jnp.stack([part(i, j) for j in range(n_seq)]) for i in range(n_ctx)])
 
 
 def body(
@@ -605,7 +1045,7 @@
     cotangent,
 ):
     n_seq, n_ctx, n_mp = (lax.axis_size(a) for a in ("seq", "ctx", "mp"))
-    s, m = lax.axis_index("seq"), lax.axis_index("mp")
+    s, c, m = (lax.axis_index(a) for a in ("seq", "ctx", "mp"))
     tok, width = tokens.shape
     share = tok // n_mp
     experts_all = router.shape[1]
@@ -624,18 +1064,22 @@
     qt = (jnp.einsum("df,td->ft", w_query, h_one, preferred_element_type=F32).astype(BF16)) * BF16(0.125)
     k = nn(h_one, key_weight_matrix).astype(BF16)
     v = nn(h_one, value_weight_matrix).astype(BF16)
-    o, heads_t, lse, kv = attend(n_ctx, qt, k, v)
+    o, heads_t, lse, kv, cot_below, cot_above, routes_line = attend(n_ctx, qt, k, v, cotangent, routes.T)
 
     experts = jnp.arange(experts_all, dtype=jnp.int32)
+    first = m * exp_local
+    local = first + jnp.arange(exp_local, dtype=jnp.int32)
+    chosen_line = (routes_line[:, None, :, :] == local[None, :, None, None]).any(axis=2)
+    low = (jnp.arange(tok)[:, None] <= jnp.arange(tok)[None, :]).astype(BF16)
+    rank_line = (
+        jnp.einsum("cet,tu->ceu", chosen_line.astype(BF16), low, preferred_element_type=F32) - 1.0
+    ).astype(jnp.int32)
+    place_line = (
+        (rank_line[:, :, None, :] == jnp.arange(slots, dtype=jnp.int32)[None, None, :, None])
+        & chosen_line[:, :, None, :]
+    ).astype(BF16)
     chosen = (routes[:, :, None] == experts[None, None, :]).any(axis=1)
-    low = (jnp.arange(tok)[:, None] >= jnp.arange(tok)[None, :]).astype(BF16)
-    rank = (nn(low, chosen.astype(BF16)) - 1.0).astype(jnp.int32)
-    first = m * exp_local
-    rank_t = lax.dynamic_slice_in_dim(rank.T, first, exp_local, 0)
-    chosen_t = lax.dynamic_slice_in_dim(chosen.T, first, exp_local, 0)
-    place = (
-        (rank_t[:, None, :] == jnp.arange(slots, dtype=jnp.int32)[None, :, None]) & chosen_t[:, None, :]
-    ).astype(BF16)
+    place = lax.dynamic_index_in_dim(place_line, c, 0, keepdims=False)
     dout_rows = jnp.einsum("ert,td->erd", place, cot_all, preferred_element_type=F32)
     dout_rows = dout_rows.astype(BF16).astype(F32)
     r_hi = router.astype(BF16)
@@ -645,7 +1089,9 @@
     router3 = jnp.concatenate([r_hi, r_mid, r_low], axis=1)
 
     part = jnp.einsum("ft,fd->td", heads_t, w_out, preferred_element_type=F32).astype(BF16)
-    resid, h_two = mid_forward(part.reshape(n_mp, share, width), x_mine, gain2)
+    resid, h_two, cot_mine = mid_forward(
+        n_ctx, part.reshape(n_mp, share, width), x_mine, gain2, cotangent, cot_below, cot_above
+    )
     h_two = h_two.reshape(tok, width)
 
     logits3 = nn(h_two, router3)
@@ -692,26 +1138,44 @@
         lax.dynamic_slice_in_dim(gates, m * share, share, 0), ((0, 0), (0, ex_pad - experts_all))
     )
     router_t = jnp.pad(router.T, ((0, ex_pad - experts_all), (0, 0)))
-    dresid, db, dlog, gnorm2 = mid_back(
-        back.reshape(n_mp, share, -1), resid, gain2, cotangent, gates_pad, router_t
+    hidden_parts = columns(hidden)
+    dresid, db, dlog, gnorm2, gate_rows_line, hidden_line, du_below, du_above = mid_back(
+        n_ctx,
+        back.reshape(n_mp, share, -1),
+        resid,
+        gain2,
+        cotangent,
+        gates_pad,
+        router_t,
+        gate_rows[..., 0],
+        hidden_parts,
+        grad_up_pre,
     )
     db = db.reshape(tok, width)
     h_two_mine = lax.dynamic_slice_in_dim(h_two, m * share, share, 0).astype(F32)
     g_router = jnp.einsum("te,td->ed", dlog[:, :experts_all], h_two_mine, precision=lax.Precision.HIGHEST)
 
-    def joined(x):
-        return jnp.concatenate([x, lax.ppermute(x, "seq", SWAP)], axis=1)
-
-    def joined_half(x):
-        return jnp.concatenate([half(x, s, 2), lax.ppermute(half(x, 1 - s, 2), "seq", SWAP)], axis=1)
-
-    arrived2 = joined_half(arrived)
-    dg2, du2 = joined(grad_gate_pre), joined(grad_up_pre)
+    arrived2 = jnp.concatenate([half(arrived, s, 2), lax.ppermute(half(arrived, 1 - s, 2), "seq", SWAP)], axis=1)
+    dg2 = jnp.concatenate([grad_gate_pre, lax.ppermute(grad_gate_pre, "seq", SWAP)], axis=1)
     g_gate = jnp.einsum("erd,erf->edf", arrived2, dg2, preferred_element_type=F32).astype(BF16)
-    g_up = jnp.einsum("erd,erf->edf", arrived2, du2, preferred_element_type=F32).astype(BF16)
-    hid2, dy2 = joined_half(hidden), joined(grad_made)
-    g_down = jnp.einsum("erf,erd->efd", hid2, dy2, preferred_element_type=F32).astype(BF16)
-    g_gate, g_up, g_down = (line_sum(g, n_ctx, 1) for g in (g_gate, g_up, g_down))
+    arrived_line = lax.all_to_all(columns(arrived), "ctx", split_axis=0, concat_axis=0, tiled=True)
+    opp = [(i, (i + n_mp // 2) % n_mp) for i in range(n_mp)]
+    sib = [(i, i + 1 - 2 * (i % 2)) for i in range(n_mp)]
+    cot_opp = lax.ppermute(cot_mine, "mp", opp)
+    cot_sib, cot_diag = lax.ppermute(cot_mine, "mp", sib), lax.ppermute(cot_opp, "mp", sib)
+    by_mp = jnp.stack([cot_mine, cot_sib, cot_opp, cot_diag])
+    where = jnp.arange(n_mp)
+    flip = (where & 1) ^ (m & 1) | (where & 2) ^ (m & 2)
+    cot_line = by_mp[flip].transpose(1, 0, 2, 3).reshape(n_ctx, tok, width)
+    dout_line = jnp.einsum("cert,ctd->cerd", place_line, cot_line, preferred_element_type=F32)
+    dy_line = (gate_rows_line[..., None] * dout_line.astype(BF16).astype(F32)).astype(BF16)
+
+    def seq_sum(g):
+        mine = lax.dynamic_index_in_dim(g, s, 0, keepdims=False)
+        theirs = lax.dynamic_index_in_dim(g, 1 - s, 0, keepdims=False).astype(BF16)
+        return mine.astype(F32) + lax.ppermute(theirs, "seq", SWAP).astype(F32)
+
+    g_down = seq_sum(jnp.einsum("csera,cerd->sead", hidden_line, dy_line, preferred_element_type=F32))
 
     dheads = jnp.einsum("fd,td->ft", w_out, db, preferred_element_type=F32).astype(BF16)
     g_out = jnp.einsum("td,ft->df", db, heads_t, preferred_element_type=F32).astype(BF16)
@@ -722,25 +1186,27 @@
         ).astype(BF16)
 
     g_out = line_sum(seq_half_sum(g_out), n_ctx, 0).T
-    dq, dkv = attend_back(n_ctx, qt, dheads, o, lse, kv)
+    dq, dkv, g_gate, du_line = attend_back(
+        n_ctx, qt, dheads, o, lse, kv, g_gate, grad_up_pre, du_below, du_above
+    )
+    g_up = seq_sum(jnp.einsum("csera,cerf->seaf", arrived_line, du_line, preferred_element_type=F32))
     kvw = dkv.shape[1] // 2
     dk, dv = dkv[:, :kvw], dkv[:, kvw:]
     dh = jnp.einsum("ft,df->td", dq, w_query, preferred_element_type=F32)
     dh = dh + jnp.einsum("tf,df->td", dk, key_weight_matrix, preferred_element_type=F32)
     dh = dh + jnp.einsum("tf,df->td", dv, value_weight_matrix, preferred_element_type=F32)
     gnorm1 = jnp.sum(dh * normed_one, axis=0, keepdims=True)
-    grad_tokens = last(dh.astype(BF16).reshape(n_mp, share, width), x_mine, gain1, dresid)
+    rows = 2 + experts_all
+    small = jnp.concatenate([gnorm1, gnorm2[:1], g_router, jnp.zeros((-rows % 8, width), F32)], axis=0)
+    grad_tokens, small = last(
+        (n_seq, n_ctx, n_mp), dh.astype(BF16).reshape(n_mp, share, width), x_mine, gain1, dresid, small
+    )
     g_q = jnp.einsum("td,ft->df", h_one, dq, preferred_element_type=F32)
     g_kv = jnp.einsum("td,tf->df", h_one, dkv, preferred_element_type=F32)
     g_qkv = jnp.concatenate([g_q, g_kv], axis=1).astype(BF16)
     g_qkv = line_sum(seq_half_sum(g_qkv), n_ctx, 0)
     qw = w_query.shape[1]
 
-    rows = 2 + experts_all
-    small = jnp.concatenate(
-        [gnorm1, gnorm2[:1], g_router, jnp.zeros((-rows % 8, width), F32)], axis=0
-    )
-    small = small_sum((n_seq, n_ctx, n_mp), small)
     return (
         output,
         grad_tokens,

time: 539 us -> 463 us (0.86)
  waiting for transfers between devices: 117 us -> 22 us
  starting transfers between devices: 88 us -> 37.8 us
  Pallas kernels: 174 us -> 219 us
  local copies, waits for them, and re-layouts: 19.6 us -> 47.8 us
  matrix products: 86 us -> 78.3 us
    ppermute x30 -> x12, waiting for transfers between devices: 98.8 us -> 8.48 us  [line_sum(): moving = lax.ppermute(mine, 'ctx', pairs)]
    ppermute x30 -> x12, starting transfers between devices: 80.2 us -> 24.7 us  [line_sum(): moving = lax.ppermute(mine, 'ctx', pairs)]
    pallas_call x1, Pallas kernels: 42.4 us -> 82.4 us  [attend_back(): pl.pallas_call(functools.partial(attend_back_kernel, n), out_shape=(jax.S...]
    pallas_call x1, Pallas kernels: 26.4 us -> 39.2 us  [attend(): pl.pallas_call(functools.partial(attend_kernel, n), out_shape=(jax.ShapeD...]
    ppermute x2, waiting for transfers between devices: 17.5 us -> 6.96 us  [seq_half_sum(): lax.ppermute(half(g, 1 - s, 0), 'seq', SWAP).astype(F32)]
    another operation x0 -> x7, other arithmetic: none -> 9.34 us  [the longest x1 7.27 us: body(): by_mp = jnp.stack([cot_mine, cot_sib, cot_opp, cot_diag])]
    convert_element_type x15 -> x6, other arithmetic: 14.1 us -> 5.17 us  [line_sum(): mine = (mine.astype(F32) + moving.astype(F32)).astype(BF16)]
    pallas_call x4 -> x3, Pallas kernels: 106 us -> 97.7 us  [the longest x1 41 us: mid_back(): pl.pallas_call(functools.partial(mid_back_kernel, chunks, n), out_shape=(...]
  transfers between devices with their start and end apart: 39 -> 24, of which waited for: 15 -> 7; matrix products, arithmetic and copies ran while one was open for 25% -> 33% of each run, Pallas kernels for 33% -> 48%
where the time goes in v2:
time: 463 us; the launch traced here: 454 us
  Pallas kernels  219 us (47%)
  matrix products  78.3 us (17%)
  local copies, waits for them, and re-layouts  47.8 us (10%)
  starting transfers between devices  37.8 us (8%)
  other arithmetic  32.7 us (7%)
  waiting for transfers between devices  22 us (5%)
  between operations  15.9 us (3%)
    pallas_call x1, Pallas kernels, attend_back(): pl.pallas_call(functools.partial(attend_back_kernel, n), out_shape=(jax.S...  82.4 us
    pallas_call x1, Pallas kernels, mid_back(): pl.pallas_call(functools.partial(mid_back_kernel, chunks, n), out_shape=(...  41 us
    pallas_call x1, Pallas kernels, attend(): pl.pallas_call(functools.partial(attend_kernel, n), out_shape=(jax.ShapeD...  39.2 us
    pallas_call x1, Pallas kernels, mid_forward(): pl.pallas_call(functools.partial(mid_forward_kernel, chunks, n), out_shap...  29.5 us
    pallas_call x1, Pallas kernels, last(): pl.pallas_call(functools.partial(last_kernel, chunks, sizes), out_shape=(...  27.2 us
    ppermute x12, starting transfers between devices, line_sum(): moving = lax.ppermute(mine, 'ctx', pairs)  24.7 us
    unnamed x178, local copies, waits for them, and re-layouts  12.3 us
  transfers between devices with their start and end apart: 24, of which 7 were waited for; matrix products, arithmetic and copies ran while one was open for 33% of the time, Pallas kernels for 48%

profile of v2, /device:TPU:16, one launch (start us, length us, event | category | flops | bytes accessed | tf_op | source)
XLA Modules:
  0.0 454.0 jit_solution(4206365734646887386)
XLA Ops:
  16.2 39.2 %attend.1 = (f32[384,640]{1,0:T(8,128)}, bf16[384,640]{1,0:T(8,128)(2,1)}, f32[6,1,640]{2,1,0:T(1,128)}, bf16[4,640,256]{2,1,0:T(8,128)(2,1)}, bf16[160,1536]{1,...) custom-call(bf16[384,640]{1,0:T(8,128)(2,1)} %fusion.40.q_ref, ...), custom_call_target="tpu_custom_call" | custom-call | bytes 108000000 | tf_op jit(solution)/shard_map/attend/pallas_call | solution.py:353
  57.9 29.5 %mid_forward.1 = (f32[160,1536]{1,0:T(8,128)S(1)}, bf16[4,160,1536]{2,1,0:T(8,128)(2,1)S(1)}, bf16[4,160,1536]{2,1,0:T(8,128)(2,1)}) custom-call(bf16[4,160,1536]{2,1,0:T(8,128)(2,1)S(1)} %bitcast.171, bf16[160,1536]{1,0:T(8,128)(2,1)S(1)} %constant_dynamic-slice_fusion.9.x_ref, f32[1,1536]{1,0:T(1,128)S(1)} %reshape.139.gain, ...), custom_call_target="tpu_custom_call" | custom-call | bytes 108000000 | tf_op jit(solution)/shard_map/mid_forward/pallas_call | solution.py:797
  105.0 3.9 copy.120
  109.0 5.8 %all-to-all-start = ((bf16[4,2,2,200,192]{3,4,2,1,0:T(8,128)(2,1)}), bf16[4,2,2,200,192]{3,4,2,1,0:T(8,128)(2,1)}, u32[]{:S(2)}, u32[]{:S(2)}) async-start(bf16[4,2,2,200,192]{3,4,2,1,0:T(8,128)(2,1)} %copy.120), calls=%async_computation.1 | async-start | bytes 3145728 | tf_op jit(solution)/shard_map/all_to_all | solution.py:1161
  117.7 5.9 %fusion.86 = f32[2,200,1024]{2,1,0:T(8,128)} fusion(bf16[2,200,1536]{2,1,0:T(8,128)(2,1)} %copy-done.22, bf16[2,1536,1024]{2,1,0:T(8,128)(2,1)} %param.22), kind=kOutput, calls=%fused_computation.178 | convolution fusion | flops 1258291200 | bytes 9158656 | tf_op jit(solution)/shard_map/erd,edf->erf/dot_general | solution.py:1110
  123.6 5.4 %fusion.85 = f32[2,200,1024]{2,1,0:T(8,128)} fusion(bf16[2,200,1536]{2,1,0:T(8,128)(2,1)S(1)} %copy-done.23, bf16[2,1536,1024]{2,1,0:T(8,128)(2,1)} %param.21), kind=kOutput, calls=%fused_computation.177 | convolution fusion | flops 1258291200 | bytes 9158656 | tf_op jit(solution)/shard_map/erd,edf->erf/dot_general | solution.py:1109
  129.0 5.8 %collective-permute-done.18 = bf16[4,160,1536]{2,1,0:T(8,128)(2,1)} collective-permute-done((bf16[4,160,1536]{2,1,0:T(8,128)(2,1)}, bf16[4,160,1536]{2,1,0:T(8,128)(2,1)}, u32[]{:S(2)}, u32[]{:S(2)}) %collective-permute-start.18) | collective-permute-done | bytes 1966112 | tf_op jit(solution)/shard_map/ppermute | solution.py:1164
  137.7 6.3 %multiply_convert_fusion.1 = (bf16[2,200,1024]{2,1,0:T(8,128)(2,1)S(1)}, bf16[2,200,1024]{2,1,0:T(8,128)(2,1)}, bf16[2,200,1024]{2,1,0:T(8,128)(2,1)S(1)}) fusion(f32[2,200,1024]{2,1,0:T(8,128)S(1)} %copy-done.29, f32[2,200,1024]{2,1,0:T(8,128)S(1)} %copy-done.28, bf16[2,1024,1536]{2,1,0:T(8,128)(2,1)} %param.23, ...), kind=kOutput, calls=%fused_computation.49 | convolution fusion | flops 1266278400 | bytes 13256256 | tf_op jit(solution)/shard_map/erd,efd->erf/dot_general | solution.py:1115
  157.1 3.4 concatenate.20
  164.7 41.0 %mid_back.1 = (f32[160,1536]{1,0:T(8,128)S(1)}, bf16[4,160,1536]{2,1,0:T(8,128)(2,1)S(1)}, f32[160,64]{1,0:T(8,128)S(1)}, f32[8,1536]{1,0:T(8,128)S(1)}, f32[4,2...) custom-call(bf16[4,160,1664]{2,1,0:T(8,128)(2,1)S(1)} %bitcast.170, ...), custom_call_target="tpu_custom_call" | custom-call | bytes 115200000 | tf_op jit(solution)/shard_map/mid_back/pallas_call | solution.py:890
  212.5 3.5 fusion.38.do_ref
  216.0 7.0 %collective-permute-done.9 = bf16[768,384]{1,0:T(8,128)(2,1)} collective-permute-done((bf16[768,384]{1,0:T(8,128)(2,1)S(1)}, bf16[768,384]{1,0:T(8,128)(2,1)}, u32[]{:S(2)}, u32[]{:S(2)}) %collective-permute-start.9) | collective-permute-done | bytes 589856 | tf_op jit(solution)/shard_map/ppermute | solution.py:1185
  229.7 5.2 %convolution_convert_fusion.9.sum_ref = bf16[2,768,1024]{2,1,0:T(8,128)(2,1)} fusion(bf16[2,200,1024]{2,1,0:T(8,128)(2,1)} %collective-permute-done.1, bf16[2,200,1024]{2,1,0:T(8,128)(2,1)} %get-tuple-element.129, bf16[2,200,768]{2,1,0:T(8,128)(2,1)} %collective-permute-done, bf16[2,200,768]{2,1,0:T(8,128)(2,1)S(1)} %copy-done.44), kind=kOutput, calls=%fused_computation.39 | convolution fusion | flops 1265598464 | bytes 6012928 | tf_op jit(solution)/shard_map/erd,erf->edf/dot_general | solution.py:1160
  234.9 82.4 %attend_back.1 = (bf16[384,640]{1,0:T(8,128)(2,1)}, bf16[640,256]{1,0:T(8,128)(2,1)}, f32[2,192,1024]{2,1,0:T(8,128)}, bf16[4,2,200,1024]{3,2,1,0:T(8,128)(2,1)}) custom-call(bf16[384,640]{1,0:T(8,128)(2,1)} %fusion.40.q_ref, bf16[384,640]{1,0:T(8,128)(2,1)} %fusion.38.do_ref, f32[384,640]{1,0:T(8,128)} %get-tuple-element.43.o_ref, ...), custom_call_target="tpu_custom_call" | custom-call | bytes 270000000 | tf_op jit(solution)/shard_map/attend_back/pallas_call | solution.py:633
  325.4 27.2 %last.1 = (f32[160,1536]{1,0:T(8,128)S(1)}, f32[16,1536]{1,0:T(8,128)S(1)}) custom-call(bf16[4,160,1536]{2,1,0:T(8,128)(2,1)S(1)} %bitcast.169, bf16[160,1536]{1,0:T(8,128)(2,1)S(1)} %constant_dynamic-slice_fusion.9.x_ref, f32[1,1536]{1,0:T(1,128)S(1)} %reshape.147.gain, f32[160,1536]{1,0:T(8,128)S(1)} %copy-done.8, f32[16,1536]{1,0:T(8,128)S(1)} %maximum_maximum_fusion.small_ref), custom_call_target="tpu_custom_call" | custom-call | bytes 72000000 | tf_op jit(solution)/shard_map/last/pallas_call | solution.py:980
  353.2 4.2 fusion.21
  364.2 4.4 collective-permute-start.14
  368.6 7.3 %pad_maximum_fusion = bf16[4,4,160,1536]{3,2,1,0:T(8,128)(2,1)} fusion(bf16[1,4,160,1536]{3,2,1,0:T(8,128)(2,1)} %bitcast.54, bf16[1,4,160,1536]{3,2,1,0:T(8,128)(2,1)} %bitcast.53, bf16[1,4,160,1536]{3,2,1,0:T(8,128)(2,1)} %bitcast.52, bf16[1,4,160,1536]{3,2,1,0:T(8,128)(2,1)} %bitcast.51), kind=kLoop, calls=%fused_computation.2 | loop fusion | flops 11796480 | bytes 15728640 | tf_op jit(solution)/shard_map/stack | solution.py:1166
  375.9 7.8 %gather_fusion = bf16[4,4,160,1536]{3,2,1,0:T(8,128)(2,1)} fusion(bf16[4,4,160,1536]{3,2,1,0:T(8,128)(2,1)} %pad_maximum_fusion, s32[1024]{0:T(1024)} %pad_clamp_fusion), kind=kCustom, calls=%fused_computation | custom fusion | bytes 15728656 | tf_op jit(solution)/shard_map/gather | solution.py:1169
  383.7 7.2 %copy.125 = bf16[4,4,160,1536]{3,2,1,0:T(8,128)(2,1)} copy(bf16[4,4,160,1536]{3,2,0,1:T(8,128)(2,1)} %bitcast.181) | data formatting | bytes 15728640 | tf_op jit(solution)/shard_map/transpose | solution.py:1169
  395.3 9.1 %fusion.13 = f32[2,1536,2,128]{3,1,2,0:T(8,128)} fusion(f32[4,2,200]{2,0,1:T(4,128)S(1)} %copy-done.74, bf16[4,640,1536,1]{2,1,0,3:T(8,128)(2,1)} %bitcast.182, bf16[4,2,2,200,128]{4,3,2,1,0:T(8,128)(2,1)S(1)} %copy-done.21, s32[4,2,640]{2,0,1:T(4,128)S(1)} %copy-done.66, pred[4,2,640]{2,0,1:T(4,128)(4,1)S(1)} %copy-done.63), kind=kOutput, calls=%fused_computation.19 | convolution fusion | flops 4415897600 | bytes 11861248 | tf_op jit(solution)/shard_map/csera,cerd->sead/dot_general | solution.py:1178
  415.4 3.3 collective-permute-done.6
  420.1 3.9 collective-permute-start.7
  429.5 3.6 collective-permute-start.8
  (312 shorter events, 115.3 us)
Async XLA Ops:
  7.2 127.6 %all-gather.2.cloned.1.call-start = ((), (), s32[]{:S(2)}) async-start(), calls=%async_computation.3 | async-start | bytes 2457600 | tf_op jit(solution)/shard_map/all_gather | solution.py:1059
  89.7 45.2 %collective-permute-start.18 = (bf16[4,160,1536]{2,1,0:T(8,128)(2,1)}, bf16[4,160,1536]{2,1,0:T(8,128)(2,1)}, u32[]{:S(2)}, u32[]{:S(2)}) collective-permute-start(bf16[4,160,1536]{2,1,0:T(8,128)(2,1)} %get-tuple-element.58), channel_id=1, source_target_pairs={{0,2},{1,3},{2,0},{3,1},{4,6},{5,7},{6,4},{7,5},{8,10},{9,11},{10,... | collective-permute-start | bytes 5898248 | tf_op jit(solution)/shard_map/ppermute | solution.py:1164
  90.2 274.0 %collective-permute-start.17 = (bf16[4,160,1536]{2,1,0:T(8,128)(2,1)}, bf16[4,160,1536]{2,1,0:T(8,128)(2,1)}, u32[]{:S(2)}, u32[]{:S(2)}) collective-permute-start(bf16[4,160,1536]{2,1,0:T(8,128)(2,1)} %get-tuple-element.58), channel_id=1, source_target_pairs={{0,1},{1,0},{2,3},{3,2},{4,5},{5,4},{6,7},{7,6},{8,9},{9,8},{10,11... | collective-permute-start | bytes 5898248 | tf_op jit(solution)/shard_map/ppermute | solution.py:1165
  101.3 127.1 %collective-permute-start = (bf16[2,200,768]{2,1,0:T(8,128)(2,1)}, bf16[2,200,768]{2,1,0:T(8,128)(2,1)}, u32[]{:S(2)}, u32[]{:S(2)}) collective-permute-start(bf16[2,200,768]{2,1,0:T(8,128)(2,1)} %get-tuple-element.140), channel_id=1, source_target_pairs={{0,16},{16,0},{1,17},{17,1},{2,18},{18,2},{3,19},{19,3},{4,20},{20... | collective-permute-start | bytes 1843208 | tf_op jit(solution)/shard_map/ppermute | solution.py:1158
  109.0 244.2 %all-to-all-start = ((bf16[4,2,2,200,192]{3,4,2,1,0:T(8,128)(2,1)}), bf16[4,2,2,200,192]{3,4,2,1,0:T(8,128)(2,1)}, u32[]{:S(2)}, u32[]{:S(2)}) async-start(bf16[4,2,2,200,192]{3,4,2,1,0:T(8,128)(2,1)} %copy.120), calls=%async_computation.1 | async-start | bytes 3145728 | tf_op jit(solution)/shard_map/all_to_all | solution.py:1161
  114.8 327.6 %reduce-scatter.2.cloned.1.call-start = ((), (), s32[]{:S(2)}) async-start(), calls=%async_computation.2 | async-start | bytes 2457600 | tf_op jit(solution)/shard_map/reduce_scatter | solution.py:1135
  134.8 233.8 %collective-permute-start.19 = (bf16[4,160,1536]{2,1,0:T(8,128)(2,1)}, bf16[4,160,1536]{2,1,0:T(8,128)(2,1)}, u32[]{:S(2)}, u32[]{:S(2)}) collective-permute-start(bf16[4,160,1536]{2,1,0:T(8,128)(2,1)} %collective-permute-done.18), channel_id=1, source_target_pairs={{0,1},{1,0},{2,3},{3,2},{4,5},{5,4},{6,7},{7,6},{8,9},{9,8},{10,11... | collective-permute-start | bytes 5898248 | tf_op jit(solution)/shard_map/ppermute | solution.py:1165
  149.0 80.6 %collective-permute-start.1 = (bf16[2,200,1024]{2,1,0:T(8,128)(2,1)}, bf16[2,200,1024]{2,1,0:T(8,128)(2,1)}, u32[]{:S(2)}, u32[]{:S(2)}) collective-permute-start(bf16[2,200,1024]{2,1,0:T(8,128)(2,1)} %get-tuple-element.129), channel_id=1, source_target_pairs={{0,16},{16,0},{1,17},{17,1},{2,18},{18,2},{3,19},{19,3},{4,20},{20... | collective-permute-start | bytes 2457608 | tf_op jit(solution)/shard_map/ppermute | solution.py:1159
  207.6 15.4 %collective-permute-start.9 = (bf16[768,384]{1,0:T(8,128)(2,1)S(1)}, bf16[768,384]{1,0:T(8,128)(2,1)}, u32[]{:S(2)}, u32[]{:S(2)}) collective-permute-start(bf16[768,384]{1,0:T(8,128)(2,1)S(1)} %constant_dynamic-slice_fusion.2), channel_id=1, source_target_pairs={{0,16},{16,0},{1,17},{17,1},{2,18},{18,2},{3,19},{19,3},{4,20},{20... | collective-permute-start | bytes 1769480 | tf_op jit(solution)/shard_map/ppermute | solution.py:1185
  224.3 2.1 collective-permute-start.10
  226.3 133.8 %collective-permute-start.13 = (bf16[192,384]{1,0:T(8,128)(2,1)S(1)}, bf16[192,384]{1,0:T(8,128)(2,1)}, u32[]{:S(2)}, u32[]{:S(2)}) collective-permute-start(bf16[192,384]{1,0:T(8,128)(2,1)S(1)} %get-tuple-element.160), channel_id=1, source_target_pairs={{12,8},{13,9},{14,10},{15,11},{28,24},{29,25},{30,26},{31,27}} | collective-permute-start | bytes 442376 | tf_op jit(solution)/shard_map/ppermute | solution.py:1012
  228.3 132.2 %collective-permute-start.11 = (bf16[192,384]{1,0:T(8,128)(2,1)}, bf16[192,384]{1,0:T(8,128)(2,1)}, u32[]{:S(2)}, u32[]{:S(2)}) collective-permute-start(bf16[192,384]{1,0:T(8,128)(2,1)} %add_convert_fusion.9), channel_id=1, source_target_pairs={{0,4},{4,8},{1,5},{5,9},{2,6},{6,10},{3,7},{7,11},{16,20},{20,24},... | collective-permute-start | bytes 442376 | tf_op jit(solution)/shard_map/ppermute | solution.py:1012
  321.6 69.4 %collective-permute-start.2 = (bf16[768,640]{0,1:T(8,128)(2,1)}, bf16[768,640]{0,1:T(8,128)(2,1)}, u32[]{:S(2)}, u32[]{:S(2)}) collective-permute-start(bf16[768,640]{0,1:T(8,128)(2,1)} %fusion.52), channel_id=1, source_target_pairs={{0,16},{16,0},{1,17},{17,1},{2,18},{18,2},{3,19},{19,3},{4,20},{20... | collective-permute-start | bytes 2949128 | tf_op jit(solution)/shard_map/ppermute | solution.py:1185
  360.1 63.9 %collective-permute-start.16 = (bf16[2,192,1024]{2,1,0:T(8,128)(2,1)}, bf16[2,192,1024]{2,1,0:T(8,128)(2,1)}, u32[]{:S(2)}, u32[]{:S(2)}) collective-permute-start(bf16[2,192,1024]{2,1,0:T(8,128)(2,1)} %fusion.55), channel_id=1, source_target_pairs={{0,16},{16,0},{1,17},{17,1},{2,18},{18,2},{3,19},{19,3},{4,20},{20... | collective-permute-start | bytes 2359304 | tf_op jit(solution)/shard_map/ppermute | solution.py:1176
  362.3 50.7 %collective-permute-start.12 = (bf16[192,384]{1,0:T(8,128)(2,1)S(1)}, bf16[192,384]{1,0:T(8,128)(2,1)S(1)}, u32[]{:S(2)}, u32[]{:S(2)}) collective-permute-start(bf16[192,384]{1,0:T(8,128)(2,1)S(1)} %get-tuple-element.157), channel_id=1, source_target_pairs={{0,4},{4,8},{8,12},{1,5},{5,9},{9,13},{2,6},{6,10},{10,14},{3,7},{... | collective-permute-start | bytes 442376 | tf_op jit(solution)/shard_map/ppermute | solution.py:1012
  364.2 40.2 %collective-permute-start.14 = (bf16[192,384]{1,0:T(8,128)(2,1)}, bf16[192,384]{1,0:T(8,128)(2,1)}, u32[]{:S(2)}, u32[]{:S(2)}) collective-permute-start(bf16[192,384]{1,0:T(8,128)(2,1)} %get-tuple-element.158), channel_id=1, source_target_pairs={{8,4},{12,8},{9,5},{13,9},{10,6},{14,10},{11,7},{15,11},{24,20},{2... | collective-permute-start | bytes 442376 | tf_op jit(solution)/shard_map/ppermute | solution.py:1012
  394.6 14.1 %collective-permute-start.3 = (bf16[192,640]{0,1:T(8,128)(2,1)}, bf16[192,640]{0,1:T(8,128)(2,1)S(1)}, u32[]{:S(2)}, u32[]{:S(2)}) collective-permute-start(bf16[192,640]{0,1:T(8,128)(2,1)} %get-tuple-element.145), channel_id=1, source_target_pairs={{0,4},{1,5},{2,6},{3,7},{16,20},{17,21},{18,22},{19,23}} | collective-permute-start | bytes 737288 | tf_op jit(solution)/shard_map/ppermute | solution.py:1012
  405.5 9.2 %collective-permute-start.15 = (bf16[192,384]{1,0:T(8,128)(2,1)S(1)}, bf16[192,384]{1,0:T(8,128)(2,1)S(1)}, u32[]{:S(2)}, u32[]{:S(2)}) collective-permute-start(bf16[192,384]{1,0:T(8,128)(2,1)S(1)} %add_convert_fusion.6), channel_id=1, source_target_pairs={{4,0},{8,4},{12,8},{5,1},{9,5},{13,9},{6,2},{10,6},{14,10},{7,3},{... | collective-permute-start | bytes 442376 | tf_op jit(solution)/shard_map/ppermute | solution.py:1012
  407.4 11.3 %collective-permute-start.6 = (bf16[192,640]{0,1:T(8,128)(2,1)}, bf16[192,640]{0,1:T(8,128)(2,1)S(1)}, u32[]{:S(2)}, u32[]{:S(2)}) collective-permute-start(bf16[192,640]{0,1:T(8,128)(2,1)} %get-tuple-element.146), channel_id=1, source_target_pairs={{12,8},{13,9},{14,10},{15,11},{28,24},{29,25},{30,26},{31,27}} | collective-permute-start | bytes 737288 | tf_op jit(solution)/shard_map/ppermute | solution.py:1012
  409.9 9.8 %collective-permute-start.4 = (bf16[192,640]{0,1:T(8,128)(2,1)S(1)}, bf16[192,640]{0,1:T(8,128)(2,1)S(1)}, u32[]{:S(2)}, u32[]{:S(2)}) collective-permute-start(bf16[192,640]{0,1:T(8,128)(2,1)S(1)} %add_convert_fusion.5), channel_id=1, source_target_pairs={{0,4},{4,8},{1,5},{5,9},{2,6},{6,10},{3,7},{7,11},{16,20},{20,24},... | collective-permute-start | bytes 737288 | tf_op jit(solution)/shard_map/ppermute | solution.py:1012
  413.0 20.2 %collective-permute-start.20 = (bf16[2,128,1536]{1,2,0:T(8,128)(2,1)S(1)}, bf16[2,128,1536]{1,2,0:T(8,128)(2,1)S(1)}, u32[]{:S(2)}, u32[]{:S(2)}) collective-permute-start(bf16[2,128,1536]{1,2,0:T(8,128)(2,1)S(1)} %fusion.56), channel_id=1, source_target_pairs={{0,16},{16,0},{1,17},{17,1},{2,18},{18,2},{3,19},{19,3},{4,20},{20... | collective-permute-start | bytes 2359304 | tf_op jit(solution)/shard_map/ppermute | solution.py:1176
  420.1 9.2 %collective-permute-start.7 = (bf16[192,640]{0,1:T(8,128)(2,1)S(1)}, bf16[192,640]{0,1:T(8,128)(2,1)S(1)}, u32[]{:S(2)}, u32[]{:S(2)}) collective-permute-start(bf16[192,640]{0,1:T(8,128)(2,1)S(1)} %get-tuple-element.144), channel_id=1, source_target_pairs={{8,4},{12,8},{9,5},{13,9},{10,6},{14,10},{11,7},{15,11},{24,20},{2... | collective-permute-start | bytes 737288 | tf_op jit(solution)/shard_map/ppermute | solution.py:1012
  426.6 9.1 %collective-permute-start.5 = (bf16[192,640]{0,1:T(8,128)(2,1)S(1)}, bf16[192,640]{0,1:T(8,128)(2,1)}, u32[]{:S(2)}, u32[]{:S(2)}) collective-permute-start(bf16[192,640]{0,1:T(8,128)(2,1)S(1)} %get-tuple-element.143), channel_id=1, source_target_pairs={{0,4},{4,8},{8,12},{1,5},{5,9},{9,13},{2,6},{6,10},{10,14},{3,7},{... | collective-permute-start | bytes 737288 | tf_op jit(solution)/shard_map/ppermute | solution.py:1012
  429.5 9.1 %collective-permute-start.8 = (bf16[192,640]{0,1:T(8,128)(2,1)S(1)}, bf16[192,640]{0,1:T(8,128)(2,1)}, u32[]{:S(2)}, u32[]{:S(2)}) collective-permute-start(bf16[192,640]{0,1:T(8,128)(2,1)S(1)} %add_convert_fusion.2), channel_id=1, source_target_pairs={{4,0},{8,4},{12,8},{5,1},{9,5},{13,9},{6,2},{10,6},{14,10},{7,3},{... | collective-permute-start | bytes 737288 | tf_op jit(solution)/shard_map/ppermute | solution.py:1012
  (86 other events, 798.4 us)
Sparse Core Ops, SparseCore 0:
  9.6 22.9 all-gather.1
  211.2 32.1 reduce-scatter.1

commit v3 on v2

--- a/solution.py
+++ b/solution.py
@@ -191,6 +191,56 @@
     def finish(self):
         for d in range(1, self.n):
             self.move(d).wait()
+
+
+class CotExchange:
+    def __init__(self, line_ref, full, first, count, sems, local):
+        self.line, self.full, self.first, self.count, self.sems, self.local = line_ref, full, first, count, sems, local
+        s, c, m = lax.axis_index("seq"), lax.axis_index("ctx"), lax.axis_index("mp")
+        self.m = m
+        self.share = line_ref.shape[1]
+        self.sib = m + 1 - 2 * lax.rem(m, 2)
+        self.opp = lax.rem(m + 2, 4)
+        self.sib_id, self.opp_id = (s, c, self.sib), (s, c, self.opp)
+
+    def signal(self, sem):
+        for d in (self.sib_id, self.opp_id):
+            pl.semaphore_signal(sem, inc=1, device_id=d, device_id_type=MESH)
+
+    def place(self, who):
+        return self.full.at[:, pl.ds(pl.multiple_of(who * self.share, 16), self.share), :]
+
+    def move(self, i):
+        mine = self.line.at[pl.ds(self.first, self.count)]
+        src = self.place(self.opp) if i == 2 else mine
+        whose = self.opp if i == 2 else self.m
+        return pltpu.make_async_remote_copy(
+            src_ref=src,
+            dst_ref=self.place(whose),
+            send_sem=self.sems.at[0, i],
+            recv_sem=self.sems.at[1, i],
+            device_id=self.opp_id if i == 0 else self.sib_id,
+            device_id_type=MESH,
+        )
+
+    def own(self):
+        return pltpu.make_async_copy(
+            self.line.at[pl.ds(self.first, self.count)], self.place(self.m), self.local.at[0]
+        )
+
+    def start(self):
+        self.move(0).start()
+        self.move(1).start()
+        self.own().start()
+
+    def finish(self):
+        self.move(0).wait_recv()
+        self.move(2).start()
+        self.own().wait()
+        self.move(1).wait_recv()
+        self.move(2).wait_recv()
+        for i in range(3):
+            self.move(i).wait_send()
 
 
 def signal_line(n, sem):
@@ -322,11 +372,18 @@
         def _():
             pass_up(slot).start()
 
+        @pl.when(slot == c)
+        def _():
+            beside.start_up()
+
         block(slot, False)
         return carry
 
+    @pl.when(c == 0)
+    def _():
+        beside.start_up()
+
     lax.fori_loop(1, c + 1, earlier, 0)
-    beside.start_up()
     for h in range(heads):
         rows = slice(h * HEAD_SIZE, (h + 1) * HEAD_SIZE)
         done = o_ref[rows, :] / tot[h]
@@ -381,19 +438,34 @@
 
 def attend_back_kernel(
     n,
+    n_seq,
     q_ref,
-    do_ref,
+    db_ref,
+    wout_ref,
     o_ref,
     lse_ref,
     kv_ref,
-    sum_ref,
+    arr_ref,
+    arr_other,
+    dg_ref,
+    dg_other,
     own_ref,
     below_ref,
     above_ref,
+    rows_line,
+    hid_line,
+    arr_line,
+    place_hbm,
+    line_hbm,
+    first_hbm,
     dq_ref,
     dkv_ref,
     summed_ref,
+    up_ref,
+    down_ref,
     all_ref,
+    rest_hbm,
+    do_ref,
     qpad,
     dopad,
     delta,
@@ -401,12 +473,27 @@
     kt,
     part,
     passing,
+    sum_ref,
     from_below,
     from_above,
+    place_buf,
+    cot_buf,
+    du_buf,
+    dy,
+    d_acc,
+    u_acc,
+    d_out,
+    d_in,
+    u_out,
+    u_in,
     send,
     recv,
     spread_sem,
     local,
+    ysem,
+    cot_local,
+    load_sem,
+    swap_sem,
 ):
     s, c, m = lax.axis_index("seq"), lax.axis_index("ctx"), lax.axis_index("mp")
     _, t, kvw2 = kv_ref.shape
@@ -414,12 +501,31 @@
     heads = q_ref.shape[0] // HEAD_SIZE
     group = heads // (kvw // HEAD_SIZE)
     ex = sum_ref.shape[0]
-    chunk_rows = sum_ref.shape[1] // n
+    half_width = sum_ref.shape[1]
+    chunk_rows = half_width // n
+    slots = arr_ref.shape[1]
+    width = db_ref.shape[1]
     up, down = (s, lax.rem(c + 1, n), m), (s, lax.rem(c + n - 1, n), m)
     spread = Spread(n, own_ref, below_ref, above_ref, all_ref, spread_sem.at[0], spread_sem.at[1], local)
+    done_blocks = first_hbm.shape[0]
+    cots = CotExchange(line_hbm, rest_hbm, done_blocks, n - done_blocks, ysem, cot_local)
     sem = pltpu.get_barrier_semaphore()
     signal_line(n, sem)
-    pl.semaphore_wait(sem, line_degree(n))
+    cots.signal(sem)
+    pl.semaphore_signal(sem, inc=1, device_id=swap_partner(), device_id_type=MESH)
+    pl.semaphore_wait(sem, line_degree(n) + 3)
+    cots.start()
+    spread.start()
+
+    def gate_part(i):
+        e, r = lax.div(i, half_width // 256), lax.rem(i, half_width // 256)
+        mine = pl.ds(pl.multiple_of(s * half_width + r * 256, 128), 256)
+        cut = pl.ds(pl.multiple_of(r * 256, 256), 256)
+        sum_ref[e, cut, :] = (
+            tn(arr_ref[e, :, mine], dg_ref[e]) + tn(arr_other[e, :, cut], dg_other[e])
+        ).astype(BF16)
+
+    loop(ex * (half_width // 256), gate_part)
 
     def remote(kind, i, src, dst, device):
         return pltpu.make_async_remote_copy(
@@ -469,7 +575,7 @@
 
     first_up(0)
     first_down(0)
-    spread.start()
+    do_ref[...] = nt(wout_ref[...], db_ref[...]).astype(BF16)
 
     def tick(i):
         first_up(i + 1)
@@ -579,9 +685,90 @@
         tick(i)
         return carry
 
-    lax.fori_loop(c, last_tick, later, 0)
+    pause = jnp.maximum(c, 2 * ex)
+    lax.fori_loop(c, pause, later, 0)
     acc = gathered(c)
     dkv_ref[...] = acc[...].astype(BF16)
+
+    cots.finish()
+
+    def load_block(b, slot, start):
+        place_copy = pltpu.make_async_copy(place_hbm.at[b], place_buf.at[slot], load_sem.at[0, slot])
+        first_copy = pltpu.make_async_copy(
+            first_hbm.at[jnp.minimum(b, done_blocks - 1)], cot_buf.at[slot], load_sem.at[1, slot]
+        )
+        rest_copy = pltpu.make_async_copy(
+            rest_hbm.at[jnp.maximum(b - done_blocks, 0)], cot_buf.at[slot], load_sem.at[1, slot]
+        )
+        if start:
+            place_copy.start()
+
+            @pl.when(b < done_blocks)
+            def _():
+                first_copy.start()
+
+            @pl.when(b >= done_blocks)
+            def _():
+                rest_copy.start()
+        else:
+            place_copy.wait()
+            first_copy.wait()
+
+    d_acc[...] = jnp.zeros_like(d_acc)
+    load_block(0, 0, True)
+    wide = 512
+
+    def down_block(b):
+        slot = lax.rem(b, 2)
+        load_block(b, slot, False)
+
+        @pl.when(b < n - 1)
+        def _():
+            load_block(b + 1, 1 - slot, True)
+
+        cols = rows_line[b].T
+        for e in range(ex):
+
+            def dys(i):
+                cut = pl.ds(pl.multiple_of(i * wide, wide), wide)
+                dy[:, cut] = (
+                    cols[:slots, e : e + 1] * nn(place_buf[slot, e * slots : (e + 1) * slots, :], cot_buf[slot, :, cut])
+                ).astype(BF16)
+
+            loop(width // wide, dys)
+            for j in range(n_seq):
+                d_acc[j, e] = d_acc[j, e] + tn(hid_line[b, j, e], dy[...])
+
+    loop(n, down_block)
+    d_out[...] = d_acc[1 - s].astype(BF16)
+    d_swap = swap(d_out, d_in, swap_sem, 0)
+    d_swap.start()
+    lax.fori_loop(pause, last_tick, later, 0)
+
+    spread.finish()
+    u_acc[...] = jnp.zeros_like(u_acc)
+
+    def load_du(b, slot):
+        return pltpu.make_async_copy(all_ref.at[b], du_buf.at[slot], load_sem.at[2, slot])
+
+    load_du(0, 0).start()
+
+    def up_block(b):
+        slot = lax.rem(b, 2)
+        load_du(b, slot).wait()
+
+        @pl.when(b < n - 1)
+        def _():
+            load_du(b + 1, 1 - slot).start()
+
+        for e in range(ex):
+            for j in range(n_seq):
+                u_acc[j, e] = u_acc[j, e] + tn(arr_line[b, j, e], du_buf[slot, e])
+
+    loop(n, up_block)
+    u_out[...] = u_acc[1 - s].astype(BF16)
+    u_swap = swap(u_out, u_in, swap_sem, 1)
+    u_swap.start()
     for e in range(ex):
         summed_ref[e] = own_unit(c, e)[...].astype(F32)
 
@@ -595,7 +782,10 @@
             sum_down(c, e).wait_recv()
             summed_ref[e] = summed_ref[e] + from_above[c, e].astype(F32)
 
-    spread.finish()
+    d_swap.wait()
+    down_ref[...] = d_acc[s] + d_in[...].astype(F32)
+    u_swap.wait()
+    up_ref[...] = u_acc[s] + u_in[...].astype(F32)
 
     def sent_kv(j, carry):
         pass_down(j).wait_send()
@@ -624,23 +814,32 @@
         lax.fori_loop(done_down, c * ex, sent, 0)
 
 
-def attend_back(n, qt, dot, o, lse, kv, sums, own, below, above):
+def attend_back(n, n_seq, qt, db, w_out, o, lse, kv, arr, arr_other, dg, dg_other, du, below, above, rows, hid, arr_line, place, line, first):
     qw, t = qt.shape
     heads = qw // HEAD_SIZE
     kvw = kv.shape[2] // 2
-    ex, rows, cols = sums.shape
-    chunk = (ex, rows // n, cols)
+    ex, slots, width = arr.shape
+    ff = dg.shape[2]
+    half_width = width // 2
+    chunk = (ex, half_width // n, ff)
+    down_chunk = (ex, hid.shape[4], width)
+    any_ = pl.BlockSpec(memory_space=pl.ANY)
+    sds = jax.ShapeDtypeStruct
     return pl.pallas_call(
-        functools.partial(attend_back_kernel, n),
+        functools.partial(attend_back_kernel, n, n_seq),
         out_shape=(
-            jax.ShapeDtypeStruct((qw, t), BF16),
-            jax.ShapeDtypeStruct((t, 2 * kvw), BF16),
-            jax.ShapeDtypeStruct(chunk, F32),
-            jax.ShapeDtypeStruct((n,) + own.shape, BF16),
+            sds((qw, t), BF16),
+            sds((t, 2 * kvw), BF16),
+            sds(chunk, F32),
+            sds(chunk, F32),
+            sds(down_chunk, F32),
+            sds((n,) + du.shape, BF16),
+            sds((n - first.shape[0],) + first.shape[1:], BF16),
         ),
-        in_specs=[VMEM] * 9,
-        out_specs=(VMEM,) * 4,
+        in_specs=[VMEM] * 16 + [any_] * 3,
+        out_specs=(VMEM,) * 5 + (any_,) * 2,
         scratch_shapes=[
+            pltpu.VMEM((qw, t), BF16),
             pltpu.VMEM((heads, kvw, t), BF16),
             pltpu.VMEM((heads, kvw, t), BF16),
             pltpu.VMEM((heads, 1, t), F32),
@@ -648,17 +847,244 @@
             pltpu.VMEM((kvw, t), BF16),
             pltpu.VMEM((2, t, 2 * kvw), F32),
             pltpu.VMEM((n, t, 2 * kvw), BF16),
+            pltpu.VMEM((ex, half_width, ff), BF16),
             pltpu.VMEM((n,) + chunk, BF16),
             pltpu.VMEM((n,) + chunk, BF16),
+            pltpu.VMEM((2,) + place.shape[1:], BF16),
+            pltpu.VMEM((2,) + first.shape[1:], BF16),
+            pltpu.VMEM((2,) + du.shape, BF16),
+            pltpu.VMEM((slots, width), BF16),
+            pltpu.VMEM((n_seq,) + down_chunk, F32),
+            pltpu.VMEM((n_seq,) + chunk, F32),
+            pltpu.VMEM(down_chunk, BF16),
+            pltpu.VMEM(down_chunk, BF16),
+            pltpu.VMEM(chunk, BF16),
+            pltpu.VMEM(chunk, BF16),
             DMA((3, n * ex)),
             DMA((3, n * ex)),
             DMA((2, n)),
             DMA((3,)),
+            DMA((2, 3)),
+            DMA((1,)),
+            DMA((3, 2)),
+            DMA((2, 2)),
         ],
-        compiler_params=params(1),
+        compiler_params=params(1, 63),
         name="attend_back",
-        cost_estimate=cost(75),
-    )(qt, dot, o, lse, kv, sums, own, below, above)
+        cost_estimate=cost(80),
+    )(qt, db, w_out, o, lse, kv, arr, arr_other, dg, dg_other, du, below, above, rows, hid, arr_line, place, line, first)
+
+
+def tn(a, b):
+    return lax.dot_general(a, b, (((0,), (0,)), ((), ())), preferred_element_type=F32)
+
+
+def loop(n, f):
+    def step(i, carry):
+        f(i)
+        return carry
+
+    lax.fori_loop(0, n, step, 0)
+
+
+def moe_kernel(
+    n,
+    n_seq,
+    experts_all,
+    h_ref,
+    cot_ref,
+    place_ref,
+    place_t_ref,
+    sel_ref,
+    router_ref,
+    wg_hbm,
+    wu_hbm,
+    wd_hbm,
+    line_hbm,
+    gates_ref,
+    rows_ref,
+    arr_ref,
+    hid_ref,
+    dg_ref,
+    du_ref,
+    back_ref,
+    comb_ref,
+    arr_line,
+    cot_first,
+    wg,
+    wu,
+    wd,
+    dout,
+    dy,
+    hid,
+    back_rows,
+    comb_rows,
+    parts,
+    cols,
+    wsem,
+    peers_sem,
+    ysem,
+    local,
+):
+    s, c, m = lax.axis_index("seq"), lax.axis_index("ctx"), lax.axis_index("mp")
+    ex, width, ff = wg.shape
+    slots = place_ref.shape[0] // ex
+    first = m * ex
+    lanes = gates_ref.shape[1]
+    peers = Peers(n, lambda p: parts.at[p], lambda i: arr_line.at[i], peers_sem.at[0], peers_sem.at[1])
+    cots = CotExchange(line_hbm, cot_first, 0, cot_first.shape[0], ysem, local)
+    sem = pltpu.get_barrier_semaphore()
+    peers.signal(sem)
+    cots.signal(sem)
+    weights = {}
+    for e in range(ex):
+        for i, (src, dst) in enumerate(((wg_hbm, wg), (wu_hbm, wu), (wd_hbm, wd))):
+            weights[i, e] = pltpu.make_async_copy(src.at[e], dst.at[e], wsem.at[i, e])
+            weights[i, e].start()
+
+    def rows_of(e):
+        return slice(e * slots, (e + 1) * slots)
+
+    def arrive(i):
+        cut = pl.ds(pl.multiple_of(i * slots, 16), slots)
+        arr_ref[i] = nn(place_ref[cut, :], h_ref[...]).astype(BF16)
+
+    loop(ex, arrive)
+    size = width // (n * n_seq)
+    for e in range(ex):
+        for i in range(n):
+            for j in range(n_seq):
+                at = (j * n + i) * size
+                parts[i, j, e] = arr_ref[e, :, at : at + size]
+    pl.semaphore_wait(sem, n - 1 + 2)
+    peers.start()
+    cots.start()
+    own = pltpu.make_async_copy(parts.at[c], arr_line.at[c], local.at[1])
+    own.start()
+
+    three = nn(h_ref[...], router_ref[...])
+    logits = three + pltpu.roll(three, lanes - experts_all, 1) + pltpu.roll(three, lanes - 2 * experts_all, 1)
+    chosen = sel_ref[...] > 0.0
+    peak = jnp.max(jnp.where(chosen, logits, -1e30), axis=1, keepdims=True)
+    raised = jnp.where(chosen, jnp.exp(jnp.where(chosen, logits - peak, 0.0)), 0.0)
+    gates = raised / jnp.sum(raised, axis=1, keepdims=True)
+    gates_ref[...] = gates
+    g1 = gates.astype(BF16)
+    rest = gates - g1.astype(F32)
+    g2 = rest.astype(BF16)
+    g3 = (rest - g2.astype(F32)).astype(BF16)
+    lane = lax.broadcasted_iota(jnp.int32, (slots, lanes), 1)
+    cols[...] = jnp.zeros_like(cols)
+    gate_col = []
+    for e in range(ex):
+        pe = place_ref[rows_of(e), :]
+        got = nn(pe, g1) + nn(pe, g2) + nn(pe, g3)
+        col = jnp.sum(jnp.where(lane == first + e, got, 0.0), axis=1, keepdims=True)
+        gate_col.append(col)
+        cols[:slots, :] = cols[:slots, :] + jnp.where(lane == e, col, 0.0)
+
+    rows_ref[...] = cols[...].T[:8, :]
+    wide = 512
+    for e in range(ex):
+        col = gate_col[e]
+
+        def douts(i):
+            cut = pl.ds(pl.multiple_of(i * wide, wide), wide)
+            d = nn(place_ref[rows_of(e), :], cot_ref[:, cut])
+            dout[e, :, cut] = d.astype(BF16)
+            dy[e, :, cut] = (col * d).astype(BF16)
+
+        loop(width // wide, douts)
+        for i in range(3):
+            weights[i, e].wait()
+
+        def hidden(i):
+            cut = pl.ds(pl.multiple_of(i * 256, 256), 256)
+            g = nn(arr_ref[e], wg[e, :, cut])
+            u = nn(arr_ref[e], wu[e, :, cut])
+            dh = nt(dy[e], wd[e, cut, :])
+            sigma = jax.nn.sigmoid(g)
+            silu = g * sigma
+            hid[:, cut] = (silu * u).astype(BF16)
+            dg_ref[e, :, cut] = (dh * u * sigma * (1.0 + g * (1.0 - sigma))).astype(BF16)
+            du_ref[e, :, cut] = (dh * silu).astype(BF16)
+
+        loop(ff // 256, hidden)
+        size = ff // (n * n_seq)
+        for i in range(n):
+            for j in range(n_seq):
+                at = (j * n + i) * size
+                hid_ref[i, j, e] = hid[:, at : at + size]
+
+        def outs(i, grads):
+            cut = pl.ds(pl.multiple_of(i * wide, wide), wide)
+            y = nn(hid[...], wd[e, :, cut]).astype(BF16).astype(F32)
+            comb_rows[rows_of(e), cut] = (col * y).astype(BF16)
+            back_rows[rows_of(e), cut] = (nt(dg_ref[e], wg[e, cut, :]) + nt(du_ref[e], wu[e, cut, :])).astype(BF16)
+            return grads + jnp.sum(dout[e, :, cut].astype(F32) * y, axis=1, keepdims=True)
+
+        grads = lax.fori_loop(0, width // wide, outs, jnp.zeros((slots, 1), F32))
+        high = grads.astype(BF16).astype(F32)
+        here = jnp.where(lane == first + e, high, jnp.where(lane == lanes // 2 + first + e, grads - high, 0.0))
+        back_rows[rows_of(e), width:] = here.astype(BF16)
+
+    def scatter(i):
+        cut = pl.ds(pl.multiple_of(i * 256, 256), 256)
+        back_ref[:, cut] = nn(place_t_ref[...], back_rows[:, cut]).astype(BF16)
+        comb_ref[:, cut] = nn(place_t_ref[...], comb_rows[:, cut]).astype(BF16)
+
+    loop(width // 256, scatter)
+    back_ref[:, width:] = nn(place_t_ref[...], back_rows[:, width:]).astype(BF16)
+    own.wait()
+    peers.finish()
+    cots.finish()
+
+
+def moe(n, n_seq, experts_all, h, cot, place, place_t, sel, router3, wg, wu, wd, line):
+    ex, width, ff = wg.shape
+    tok = h.shape[0]
+    slots = place.shape[0] // ex
+    share = line.shape[1]
+    blocks = n // 2
+    size = width // (n * n_seq)
+    any_ = pl.BlockSpec(memory_space=pl.ANY)
+    sds = jax.ShapeDtypeStruct
+    return pl.pallas_call(
+        functools.partial(moe_kernel, n, n_seq, experts_all),
+        out_shape=(
+            sds((tok, 128), F32),
+            sds((8, 256), F32),
+            sds((ex, slots, width), BF16),
+            sds((n, n_seq, ex, slots, ff // (n * n_seq)), BF16),
+            sds((ex, slots, ff), BF16),
+            sds((ex, slots, ff), BF16),
+            sds((tok, width + 128), BF16),
+            sds((tok, width), BF16),
+            sds((n, n_seq, ex, slots, size), BF16),
+            sds((blocks, tok, width), BF16),
+        ),
+        in_specs=[VMEM] * 6 + [any_] * 4,
+        out_specs=(VMEM,) * 8 + (VMEM, any_),
+        scratch_shapes=[
+            pltpu.VMEM(wg.shape, BF16),
+            pltpu.VMEM(wu.shape, BF16),
+            pltpu.VMEM(wd.shape, BF16),
+            pltpu.VMEM((ex, slots, width), BF16),
+            pltpu.VMEM((ex, slots, width), BF16),
+            pltpu.VMEM((slots, ff), BF16),
+            pltpu.VMEM((ex * slots, width + 128), BF16),
+            pltpu.VMEM((ex * slots, width), BF16),
+            pltpu.VMEM((n, n_seq, ex, slots, size), BF16),
+            pltpu.VMEM((256, 128), F32),
+            DMA((3, ex)),
+            DMA((2, n)),
+            DMA((2, 3)),
+            DMA((2,)),
+        ],
+        compiler_params=params(6, 60),
+        name="moe",
+        cost_estimate=cost(30),
+    )(h, cot, place, place_t, sel, router3, wg, wu, wd, line)
 
 
 class Mp:
@@ -822,6 +1248,8 @@
     rows_ref,
     hid_ref,
     du_ref,
+    arr_ref,
+    dg_ref,
     dresid_ref,
     db_ref,
     dlog_ref,
@@ -830,6 +1258,8 @@
     hid_line,
     below_ref,
     above_ref,
+    arr_other,
+    dg_other,
     core_in,
     y_out,
     y_in,
@@ -837,6 +1267,7 @@
     side,
     peers_sem,
     local,
+    swap_sem,
 ):
     c = lax.axis_index("ctx")
     mp = Mp(part, core_in, y_out, y_in, db_ref, sems, chunks)
@@ -848,8 +1279,18 @@
     sem = pltpu.get_barrier_semaphore()
     mp.signal(sem)
     rows_peers.signal(sem)
-    pl.semaphore_wait(sem, 2 + n - 1)
+    partner = swap_partner()
+    pl.semaphore_signal(sem, inc=1, device_id=partner, device_id_type=MESH)
+    pl.semaphore_wait(sem, 2 + n - 1 + 1)
     mp.rs_begin()
+    half_width = width // 2
+    theirs = pl.ds(pl.multiple_of((1 - lax.axis_index("seq")) * half_width, 128), half_width)
+    swaps = [
+        swap(arr_ref.at[:, :, theirs], arr_other, swap_sem, 0),
+        swap(dg_ref, dg_other, swap_sem, 1),
+    ]
+    for sw in swaps:
+        sw.start()
     beside.start_up()
     beside.start_down()
     rows_peers.start()
@@ -882,9 +1323,26 @@
     rows_peers.finish()
     hid_peers.finish()
     beside.finish()
-
-
-def mid_back(n, part, resid, gain, cot, gate, router_t, rows, hid, du, chunks=2):
+    for sw in swaps:
+        sw.wait()
+
+
+def swap_partner():
+    return (1 - lax.axis_index("seq"), lax.axis_index("ctx"), lax.axis_index("mp"))
+
+
+def swap(src, dst, sems, i):
+    return pltpu.make_async_remote_copy(
+        src_ref=src,
+        dst_ref=dst,
+        send_sem=sems.at[0, i],
+        recv_sem=sems.at[1, i],
+        device_id=swap_partner(),
+        device_id_type=MESH,
+    )
+
+
+def mid_back(n, part, resid, gain, cot, gate, router_t, rows, hid, du, arr, dg, chunks=2):
     k, share, wide = part.shape
     width = gain.shape[1]
     return pl.pallas_call(
@@ -898,14 +1356,16 @@
             jax.ShapeDtypeStruct(hid.shape, BF16),
             jax.ShapeDtypeStruct(du.shape, BF16),
             jax.ShapeDtypeStruct(du.shape, BF16),
+            jax.ShapeDtypeStruct(arr.shape[:2] + (arr.shape[2] // 2,), BF16),
+            jax.ShapeDtypeStruct(dg.shape, BF16),
         ),
-        in_specs=[VMEM] * 9,
-        out_specs=(VMEM,) * 8,
-        scratch_shapes=mp_scratch(share, wide, chunks) + [DMA((2, 2)), DMA((4, n)), DMA((2,))],
-        compiler_params=params(3, 36),
+        in_specs=[VMEM] * 11,
+        out_specs=(VMEM,) * 10,
+        scratch_shapes=mp_scratch(share, wide, chunks) + [DMA((2, 2)), DMA((4, n)), DMA((2,)), DMA((2, 2))],
+        compiler_params=params(3, 40),
         name="mid_back",
         cost_estimate=cost(32),
-    )(part, resid, gain, cot, gate, router_t, rows, hid, du)
+    )(part, resid, gain, cot, gate, router_t, rows, hid, du, arr, dg)
 
 
 class SmallSum:
@@ -952,66 +1412,117 @@
 
 
 def last_kernel(
-    chunks, sizes, part, x_ref, gain, dresid_ref, small_ref, out_ref, total_ref, core_in, y_out, y_in, sems, *rest
+    chunks,
+    sizes,
+    part,
+    x_ref,
+    gain,
+    dresid_ref,
+    small_ref,
+    wout_ref,
+    qkv_ref,
+    out_ref,
+    total_ref,
+    gout_ref,
+    gqkv_ref,
+    core_in,
+    y_out,
+    y_in,
+    sems,
+    swapped,
+    summed,
+    wout_in,
+    qkv_in,
+    swap_sem,
+    peers_sem,
+    *rest,
 ):
+    n = sizes[1]
+    s, c = lax.axis_index("seq"), lax.axis_index("ctx")
     mp = Mp(part, core_in, y_out, y_in, None, sems, chunks)
     small = SmallSum(sizes, small_ref, total_ref, rest[:3], rest[3])
+    half_rows = swapped.shape[0]
+    rows = half_rows // n
+    wout_peers = Peers(
+        n, lambda p: wout_ref.at[cut_of(p, rows)], lambda i: wout_in.at[i], peers_sem.at[0], peers_sem.at[1]
+    )
+    qkv_peers = Peers(
+        n, lambda p: summed.at[cut_of(p, rows)], lambda i: qkv_in.at[i], peers_sem.at[2], peers_sem.at[3]
+    )
     sem = pltpu.get_barrier_semaphore()
     pl.semaphore_wait(sem, small.signal(sem))
+    qkv_swap = swap(qkv_ref.at[cut_of(1 - s, half_rows)], swapped, swap_sem, 0)
+    qkv_swap.start()
     mp.rs_core(0).start()
     mp.rs_core(1).start()
     small.begin(2, small_ref[...])
+    wout_peers.start()
     mp.rs_forward()
     small.begin(0, small.end(2))
-    order = (lambda: small.begin(1, small.end(0)),)
     for i in range(chunks):
         cut = mp.cut(i)
-        if i < len(order):
-            order[i]()
+        if i == 1:
+            small.begin(1, small.end(0))
         dh = mp.rs_chunk(i)
         normed, inverse = rms_parts(x_ref[cut, :].astype(F32))
         out_ref[cut, :] = dresid_ref[cut, :] + rms_grad(dh * gain[...], normed, inverse)
+    qkv_swap.wait()
+
+    def add(i):
+        here = cut_of(i, rows)
+        summed[here, :] = (
+            qkv_ref[cut_of(s * n + i, rows), :].astype(F32) + swapped[here, :].astype(F32)
+        ).astype(BF16)
+
+    loop(n, add)
+    qkv_peers.start()
     total_ref[...] = small.end(1)
+    wout_peers.finish()
+    wout_in[c] = wout_ref[cut_of(c, rows), :]
+    total = jnp.zeros(gout_ref.shape, F32)
+    for i in range(n):
+        total = total + wout_in[i].astype(F32)
+    gout_ref[...] = total
     mp.rs_end()
-
-
-def last(sizes, part, x_mine, gain, dresid, small, chunks=2):
+    qkv_peers.finish()
+    qkv_in[c] = summed[cut_of(c, rows), :]
+    total = jnp.zeros(gqkv_ref.shape, F32)
+    for i in range(n):
+        total = total + qkv_in[i].astype(F32)
+    gqkv_ref[...] = total
+
+
+def cut_of(i, rows):
+    return pl.ds(pl.multiple_of(i * rows, 16), rows)
+
+
+def last(sizes, part, x_mine, gain, dresid, small, wout, qkv, chunks=2):
     _, share, width = part.shape
+    n = sizes[1]
+    half_rows, fo = wout.shape
+    fq = qkv.shape[1]
+    rows = half_rows // n
+    sds = jax.ShapeDtypeStruct
     return pl.pallas_call(
         functools.partial(last_kernel, chunks, sizes),
-        out_shape=(jax.ShapeDtypeStruct((share, width), F32), jax.ShapeDtypeStruct(small.shape, F32)),
-        in_specs=[VMEM] * 5,
-        out_specs=(VMEM,) * 2,
+        out_shape=(sds((share, width), F32), sds(small.shape, F32), sds((rows, fo), F32), sds((rows, fq), F32)),
+        in_specs=[VMEM] * 7,
+        out_specs=(VMEM,) * 4,
         scratch_shapes=mp_scratch(share, width, chunks)
-        + [pltpu.VMEM((n,) + small.shape, F32) for n in sizes]
+        + [
+            pltpu.VMEM((half_rows, fq), BF16),
+            pltpu.VMEM((half_rows, fq), BF16),
+            pltpu.VMEM((n, rows, fo), BF16),
+            pltpu.VMEM((n, rows, fq), BF16),
+            DMA((2, 1)),
+            DMA((4, n)),
+        ]
+        + [pltpu.VMEM((k,) + small.shape, F32) for k in sizes]
         + [DMA((2, sum(sizes)))],
-        compiler_params=params(4, 20),
+        compiler_params=params(4, 24),
         name="last",
-        cost_estimate=cost(20),
-    )(part, x_mine, gain, dresid, small)
-
-
-def line_sum(parts, n, dim):
-    c = lax.axis_index("ctx")
-    size = parts.shape[dim] // n
-
-    def chunk(k):
-        return lax.dynamic_slice_in_dim(parts, jnp.clip(k, 0, n - 1) * size, size, dim)
-
-    total = chunk(c).astype(F32)
-    for way in (1, -1):
-        moving = None
-        for t in range(1, n):
-            mine = chunk(n - t + c if way == 1 else c - n + t)
-            if moving is not None:
-                mine = (mine.astype(F32) + moving.astype(F32)).astype(BF16)
-            if way == 1:
-                pairs = [(i, i + 1) for i in range(t)]
-            else:
-                pairs = [(i, i - 1) for i in range(n - t, n)]
-            moving = lax.ppermute(mine, "ctx", pairs)
-        total = total + moving.astype(F32)
-    return total
+        cost_estimate=cost(45),
+    )(part, x_mine, gain, dresid, small, wout, qkv)
 
 
 def half(x, s, dim):
@@ -1020,13 +1531,6 @@
 
 
 SWAP = [(0, 1), (1, 0)]
-
-
-def columns(x):
-    n_seq, n_ctx = lax.axis_size("seq"), lax.axis_size("ctx")
-    size = x.shape[2] // (n_seq * n_ctx)
-    part = lambda i, j: x[:, :, (j * n_ctx + i) * size : (j * n_ctx + i + 1) * size]
-    return jnp.stack([jnp.stack([part(i, j) for j in range(n_seq)]) for i in range(n_ctx)])
 
 
 def body(
@@ -1052,7 +1556,7 @@
     exp_local = w_gate.shape[0]
     top = routes.shape[1]
     cap = share * top * 5 // (4 * experts_all)
-    slots = n_mp * cap
+    slots = -(-n_mp * cap // 16) * 16
     gain1 = norm1_gain.reshape(1, width)
     gain2 = norm2_gain.reshape(1, width)
 
@@ -1079,134 +1583,89 @@
         & chosen_line[:, :, None, :]
     ).astype(BF16)
     chosen = (routes[:, :, None] == experts[None, None, :]).any(axis=1)
+    place_line = place_line.reshape(n_ctx, exp_local * slots, tok)
     place = lax.dynamic_index_in_dim(place_line, c, 0, keepdims=False)
-    dout_rows = jnp.einsum("ert,td->erd", place, cot_all, preferred_element_type=F32)
-    dout_rows = dout_rows.astype(BF16).astype(F32)
+    place_t = place.T
+    lanes = 128
+    chosen_pad = jnp.pad(chosen.astype(F32), ((0, 0), (0, lanes - experts_all)))
     r_hi = router.astype(BF16)
     r_rest = router - r_hi.astype(F32)
     r_mid = r_rest.astype(BF16)
     r_low = (r_rest - r_mid.astype(F32)).astype(BF16)
-    router3 = jnp.concatenate([r_hi, r_mid, r_low], axis=1)
+    router3 = jnp.pad(jnp.concatenate([r_hi, r_mid, r_low], axis=1), ((0, 0), (0, lanes - 3 * experts_all)))
+    router_t = jnp.pad(router.T, ((0, lanes // 2 - experts_all), (0, 0)))
 
     part = jnp.einsum("ft,fd->td", heads_t, w_out, preferred_element_type=F32).astype(BF16)
-    resid, h_two, cot_mine = mid_forward(
+    resid, h_two, cot_line = mid_forward(
         n_ctx, part.reshape(n_mp, share, width), x_mine, gain2, cotangent, cot_below, cot_above
     )
     h_two = h_two.reshape(tok, width)
 
-    logits3 = nn(h_two, router3)
-    logits = (
-        logits3[:, :experts_all]
-        + logits3[:, experts_all : 2 * experts_all]
-        + logits3[:, 2 * experts_all :]
+    gates, gate_rows, arrived, hidden, dg, du, back, comb, arrived_line, cot_first = moe(
+        n_ctx, n_seq, experts_all, h_two, cot_all, place, place_t, chosen_pad, router3, w_gate, w_up, w_down, cot_line
     )
-    peak = jnp.max(jnp.where(chosen, logits, -jnp.inf), axis=-1, keepdims=True)
-    raised = jnp.where(chosen, jnp.exp(jnp.where(chosen, logits - peak, 0.0)), 0.0)
-    gates = raised / jnp.sum(raised, axis=-1, keepdims=True)
-    gates_mine = lax.dynamic_slice_in_dim(gates.T, first, exp_local, 0)
-    gate_rows = jnp.sum(place.astype(F32) * gates_mine[:, None, :], axis=-1)[..., None]
-    arrived = jnp.einsum("ert,td->erd", place, h_two, preferred_element_type=F32).astype(BF16)
-    gate_pre = jnp.einsum("erd,edf->erf", arrived, w_gate, preferred_element_type=F32)
-    up_pre = jnp.einsum("erd,edf->erf", arrived, w_up, preferred_element_type=F32)
-    sigma = jax.nn.sigmoid(gate_pre)
-    silu_gate = gate_pre * sigma
-    hidden = (silu_gate * up_pre).astype(BF16)
-    grad_made = (gate_rows * dout_rows).astype(BF16)
-    grad_hidden = jnp.einsum("erd,efd->erf", grad_made, w_down, preferred_element_type=F32)
-    grad_gate_pre = (grad_hidden * up_pre * sigma * (1.0 + gate_pre * (1.0 - sigma))).astype(BF16)
-    grad_up_pre = (grad_hidden * silu_gate).astype(BF16)
-    grad_arrived = jnp.einsum("erf,edf->erd", grad_gate_pre, w_gate, preferred_element_type=F32)
-    grad_arrived = grad_arrived + jnp.einsum("erf,edf->erd", grad_up_pre, w_up, preferred_element_type=F32)
-    grad_arrived = grad_arrived.astype(BF16)
-    made = jnp.einsum("erf,efd->erd", hidden, w_down, preferred_element_type=F32).astype(BF16)
-    made_f = made.astype(F32)
-    gate_grads = jnp.sum(dout_rows * made_f, axis=-1)
-    ex_pad = 64
-    local_hot = (experts[None, :] == (first + jnp.arange(exp_local, dtype=jnp.int32))[:, None]).astype(F32)
-    gate_grads = gate_grads[..., None] * local_hot[:, None, :]
-    gate_grads = jnp.pad(gate_grads, ((0, 0), (0, 0), (0, ex_pad - experts_all)))
-    gg_hi = gate_grads.astype(BF16)
-    gg_low = (gate_grads - gg_hi.astype(F32)).astype(BF16)
-    flat = place.reshape(exp_local * slots, tok)
-    back_rows = jnp.concatenate([grad_arrived, gg_hi, gg_low], axis=-1).reshape(exp_local * slots, -1)
-    back = jnp.einsum("rt,rd->td", flat, back_rows, preferred_element_type=F32).astype(BF16)
-    comb_rows = (gate_rows * made_f).astype(BF16).reshape(exp_local * slots, width)
-    comb = jnp.einsum("rt,rd->td", flat, comb_rows, preferred_element_type=F32).astype(BF16)
     output = resid + lax.psum_scatter(comb, "mp", scatter_dimension=0, tiled=True).astype(F32)
-
-    gates_pad = jnp.pad(
-        lax.dynamic_slice_in_dim(gates, m * share, share, 0), ((0, 0), (0, ex_pad - experts_all))
-    )
-    router_t = jnp.pad(router.T, ((0, ex_pad - experts_all), (0, 0)))
-    hidden_parts = columns(hidden)
-    dresid, db, dlog, gnorm2, gate_rows_line, hidden_line, du_below, du_above = mid_back(
+    gates_mine = lax.dynamic_slice_in_dim(gates, m * share, share, 0)[:, : lanes // 2]
+    dresid, db, dlog, gnorm2, gate_rows_line, hidden_line, du_below, du_above, arrived_other, dg_other = mid_back(
         n_ctx,
         back.reshape(n_mp, share, -1),
         resid,
         gain2,
         cotangent,
-        gates_pad,
+        gates_mine,
         router_t,
-        gate_rows[..., 0],
-        hidden_parts,
-        grad_up_pre,
+        gate_rows,
+        hidden,
+        du,
+        arrived,
+        dg,
     )
     db = db.reshape(tok, width)
     h_two_mine = lax.dynamic_slice_in_dim(h_two, m * share, share, 0).astype(F32)
     g_router = jnp.einsum("te,td->ed", dlog[:, :experts_all], h_two_mine, precision=lax.Precision.HIGHEST)
-
-    arrived2 = jnp.concatenate([half(arrived, s, 2), lax.ppermute(half(arrived, 1 - s, 2), "seq", SWAP)], axis=1)
-    dg2 = jnp.concatenate([grad_gate_pre, lax.ppermute(grad_gate_pre, "seq", SWAP)], axis=1)
-    g_gate = jnp.einsum("erd,erf->edf", arrived2, dg2, preferred_element_type=F32).astype(BF16)
-    arrived_line = lax.all_to_all(columns(arrived), "ctx", split_axis=0, concat_axis=0, tiled=True)
-    opp = [(i, (i + n_mp // 2) % n_mp) for i in range(n_mp)]
-    sib = [(i, i + 1 - 2 * (i % 2)) for i in range(n_mp)]
-    cot_opp = lax.ppermute(cot_mine, "mp", opp)
-    cot_sib, cot_diag = lax.ppermute(cot_mine, "mp", sib), lax.ppermute(cot_opp, "mp", sib)
-    by_mp = jnp.stack([cot_mine, cot_sib, cot_opp, cot_diag])
-    where = jnp.arange(n_mp)
-    flip = (where & 1) ^ (m & 1) | (where & 2) ^ (m & 2)
-    cot_line = by_mp[flip].transpose(1, 0, 2, 3).reshape(n_ctx, tok, width)
-    dout_line = jnp.einsum("cert,ctd->cerd", place_line, cot_line, preferred_element_type=F32)
-    dy_line = (gate_rows_line[..., None] * dout_line.astype(BF16).astype(F32)).astype(BF16)
-
-    def seq_sum(g):
-        mine = lax.dynamic_index_in_dim(g, s, 0, keepdims=False)
-        theirs = lax.dynamic_index_in_dim(g, 1 - s, 0, keepdims=False).astype(BF16)
-        return mine.astype(F32) + lax.ppermute(theirs, "seq", SWAP).astype(F32)
-
-    g_down = seq_sum(jnp.einsum("csera,cerd->sead", hidden_line, dy_line, preferred_element_type=F32))
-
-    dheads = jnp.einsum("fd,td->ft", w_out, db, preferred_element_type=F32).astype(BF16)
     g_out = jnp.einsum("td,ft->df", db, heads_t, preferred_element_type=F32).astype(BF16)
-
-    def seq_half_sum(g):
-        return (
-            half(g, s, 0).astype(F32) + lax.ppermute(half(g, 1 - s, 0), "seq", SWAP).astype(F32)
-        ).astype(BF16)
-
-    g_out = line_sum(seq_half_sum(g_out), n_ctx, 0).T
-    dq, dkv, g_gate, du_line = attend_back(
-        n_ctx, qt, dheads, o, lse, kv, g_gate, grad_up_pre, du_below, du_above
+    g_out = (
+        half(g_out, s, 0).astype(F32) + lax.ppermute(half(g_out, 1 - s, 0), "seq", SWAP).astype(F32)
+    ).astype(BF16)
+
+    dq, dkv, g_gate, g_up, g_down, _, _ = attend_back(
+        n_ctx,
+        n_seq,
+        qt,
+        db,
+        w_out,
+        o,
+        lse,
+        kv,
+        arrived,
+        arrived_other,
+        dg,
+        dg_other,
+        du,
+        du_below,
+        du_above,
+        gate_rows_line,
+        hidden_line,
+        arrived_line,
+        place_line,
+        cot_line,
+        cot_first,
     )
-    g_up = seq_sum(jnp.einsum("csera,cerf->seaf", arrived_line, du_line, preferred_element_type=F32))
     kvw = dkv.shape[1] // 2
     dk, dv = dkv[:, :kvw], dkv[:, kvw:]
+    g_q = jnp.einsum("td,ft->df", h_one, dq, preferred_element_type=F32)
+    g_kv = jnp.einsum("td,tf->df", h_one, dkv, preferred_element_type=F32)
+    g_qkv = jnp.concatenate([g_q, g_kv], axis=1).astype(BF16)
     dh = jnp.einsum("ft,df->td", dq, w_query, preferred_element_type=F32)
     dh = dh + jnp.einsum("tf,df->td", dk, key_weight_matrix, preferred_element_type=F32)
     dh = dh + jnp.einsum("tf,df->td", dv, value_weight_matrix, preferred_element_type=F32)
     gnorm1 = jnp.sum(dh * normed_one, axis=0, keepdims=True)
     rows = 2 + experts_all
     small = jnp.concatenate([gnorm1, gnorm2[:1], g_router, jnp.zeros((-rows % 8, width), F32)], axis=0)
-    grad_tokens, small = last(
-        (n_seq, n_ctx, n_mp), dh.astype(BF16).reshape(n_mp, share, width), x_mine, gain1, dresid, small
+    grad_tokens, small, g_out, g_qkv = last(
+        (n_seq, n_ctx, n_mp), dh.astype(BF16).reshape(n_mp, share, width), x_mine, gain1, dresid, small, g_out, g_qkv
     )
-    g_q = jnp.einsum("td,ft->df", h_one, dq, preferred_element_type=F32)
-    g_kv = jnp.einsum("td,tf->df", h_one, dkv, preferred_element_type=F32)
-    g_qkv = jnp.concatenate([g_q, g_kv], axis=1).astype(BF16)
-    g_qkv = line_sum(seq_half_sum(g_qkv), n_ctx, 0)
     qw = w_query.shape[1]
-
     return (
         output,
         grad_tokens,
@@ -1214,7 +1673,7 @@
         g_qkv[:, :qw],
         g_qkv[:, qw : qw + kvw],
         g_qkv[:, qw + kvw :],
-        g_out,
+        g_out.T,
         small[1],
         small[2:rows].T,
         g_gate,

time: 463 us -> 414 us (0.89); the launches traced: 454 us -> 410 us
  Pallas kernels: 219 us -> 335 us
  matrix products: 78.3 us -> 15.9 us
  starting transfers between devices: 37.8 us -> 1.65 us
  other arithmetic: 32.7 us -> 7.84 us
  local copies, waits for them, and re-layouts: 47.8 us -> 30 us
  waiting for transfers between devices: 22 us -> 5.33 us
    pallas_call x1 -> x2, Pallas kernels: 82.4 us -> 165 us  [the longest x1 117 us: attend_back(): pl.pallas_call(functools.partial(attend_back_kernel, n, n_seq), out_shape...]
    dot_general x14 -> x0, matrix products: 59.9 us -> none  [the longest x1 9.15 us: body(): jnp.einsum('csera,cerd->sead', hidden_line, dy_line, preferred_element_ty...]
    ppermute x21 -> x1, starting transfers between devices: 31.5 us -> 1.57 us  [body(): lax.ppermute(half(g_out, 1 - s, 0), 'seq', SWAP).astype(F32)]
    pallas_call x1, Pallas kernels: 27.2 us -> 56.7 us  [last(): pl.pallas_call(functools.partial(last_kernel, chunks, sizes), out_shape=(...]
    ppermute x21 -> x1, waiting for transfers between devices: 21.3 us -> 4.63 us  [body(): lax.ppermute(half(g_out, 1 - s, 0), 'seq', SWAP).astype(F32)]
    another operation x7 -> x0, other arithmetic: 9.34 us -> none  [the longest x1 7.27 us: body(): by_mp = jnp.stack([cot_mine, cot_sib, cot_opp, cot_diag])]
    gather x1 -> x0, local copies, waits for them, and re-layouts: 7.82 us -> none  [body(): cot_line = by_mp[flip].transpose(1, 0, 2, 3).reshape(n_ctx, tok, width)]
    convert_element_type x10 -> x2, other arithmetic: 8.64 us -> 0.87 us  [the longest x1 0.7 us: body(): place_line = ((rank_line[:, :, None, :] == jnp.arange(slots, dtype=jnp.in...]
  transfers between devices with their start and end apart: 24 -> 3, of which waited for: 7 -> 1; matrix products, arithmetic and copies ran while one was open for 33% -> 8% of each run, Pallas kernels for 48% -> 70%
where the time goes in v3:
time: 414 us; the launch traced here: 410 us
  Pallas kernels  335 us (81%)
  local copies, waits for them, and re-layouts  30 us (7%)
  matrix products  15.9 us (4%)
  between operations  14.6 us (4%)
  other arithmetic  7.84 us (2%)
  waiting for transfers between devices  5.33 us (1%)
    pallas_call x1, Pallas kernels, attend_back(): pl.pallas_call(functools.partial(attend_back_kernel, n, n_seq), out_shape...  117 us
    pallas_call x1, Pallas kernels, last(): pl.pallas_call(functools.partial(last_kernel, chunks, sizes), out_shape=(...  56.7 us
    pallas_call x1, Pallas kernels, moe(): pl.pallas_call(functools.partial(moe_kernel, n, n_seq, experts_all), out_...  48.3 us
    pallas_call x1, Pallas kernels, mid_back(): pl.pallas_call(functools.partial(mid_back_kernel, chunks, n), out_shape=(...  45.9 us
    pallas_call x1, Pallas kernels, attend(): pl.pallas_call(functools.partial(attend_kernel, n), out_shape=(jax.ShapeD...  38.7 us
    pallas_call x1, Pallas kernels, mid_forward(): pl.pallas_call(functools.partial(mid_forward_kernel, chunks, n), out_shap...  28.3 us
    unnamed x103, local copies, waits for them, and re-layouts  19 us
  transfers between devices with their start and end apart: 3, of which 1 were waited for; matrix products, arithmetic and copies ran while one was open for 8% of the time, Pallas kernels for 70%

profile of v3, /device:TPU:16, one launch (start us, length us, event | category | flops | bytes accessed | tf_op | source)
XLA Modules:
  0.0 410.0 jit_solution(12958215163353643317)
XLA Ops:
  11.6 2.0 fusion.6
  13.6 1.4 convolution_convert_fusion.6.k_ref
  15.0 1.4 convolution_convert_fusion.5.v_ref
  16.4 2.0 fusion.11.q_ref
  18.5 38.7 %attend.1 = (f32[384,640]{1,0:T(8,128)}, bf16[384,640]{1,0:T(8,128)(2,1)}, f32[6,1,640]{2,1,0:T(1,128)}, bf16[4,640,256]{2,1,0:T(8,128)(2,1)}, bf16[160,1536]{1,...) custom-call(bf16[384,640]{1,0:T(8,128)(2,1)} %fusion.11.q_ref, ...), custom_call_target="tpu_custom_call" | custom-call | bytes 108000000 | tf_op jit(solution)/shard_map/attend/pallas_call | solution.py:410
  59.0 1.4 copy-done.29
  63.4 1.2 convolution_convert_fusion
  64.7 28.3 %mid_forward.1 = (f32[160,1536]{1,0:T(8,128)S(1)}, bf16[4,160,1536]{2,1,0:T(8,128)(2,1)S(1)}, bf16[4,160,1536]{2,1,0:T(8,128)(2,1)S(1)}) custom-call(bf16[4,160,1536]{2,1,0:T(8,128)(2,1)S(1)} %bitcast.47, bf16[160,1536]{1,0:T(8,128)(2,1)S(1)} %constant_dynamic-slice_fusion.2.x_ref, f32[1,1536]{1,0:T(1,128)S(1)} %reshape.67.gain, ...), custom_call_target="tpu_custom_call" | custom-call | bytes 108000000 | tf_op jit(solution)/shard_map/mid_forward/pallas_call | solution.py:1223
  93.0 1.3 copy-done.2
  95.2 1.3 copy-done.9
  97.3 48.3 %moe.1 = (f32[640,128]{1,0:T(8,128)}, f32[8,256]{1,0:T(8,128)}, bf16[2,208,1536]{2,1,0:T(8,128)(2,1)}, bf16[4,2,2,208,128]{4,3,2,1,0:T(8,128)(2,1)}, bf16[2,208,...) custom-call(bf16[640,1536]{1,0:T(8,128)(2,1)} %bitcast.45, ...), custom_call_target="tpu_custom_call" | custom-call | bytes 108000000 | tf_op jit(solution)/shard_map/moe/pallas_call | solution.py:1052
  147.1 1.2 copy-done.5
  149.4 1.2 copy-done.8
  151.7 45.9 %mid_back.1 = (f32[160,1536]{1,0:T(8,128)S(1)}, bf16[4,160,1536]{2,1,0:T(8,128)(2,1)S(1)}, f32[160,64]{1,0:T(8,128)S(1)}, f32[8,1536]{1,0:T(8,128)S(1)}, f32[4,8...) custom-call(bf16[4,160,1664]{2,1,0:T(8,128)(2,1)} %bitcast.52, ...), custom_call_target="tpu_custom_call" | custom-call | bytes 115200000 | tf_op jit(solution)/shard_map/mid_back/pallas_call | solution.py:1348
  197.7 1.3 convolution_convert_fusion.2
  201.7 116.7 %attend_back.1 = (bf16[384,640]{1,0:T(8,128)(2,1)}, bf16[640,256]{1,0:T(8,128)(2,1)}, f32[2,192,1024]{2,1,0:T(8,128)}, f32[2,192,1024]{2,1,0:T(8,128)}, f32[2,12...) custom-call(bf16[384,640]{1,0:T(8,128)(2,1)} %fusion.11.q_ref, ...), custom_call_target="tpu_custom_call" | custom-call | bytes 288000000 | tf_op jit(solution)/shard_map/attend_back/pallas_call | solution.py:828
  319.2 1.6 collective-permute-start
  320.8 1.9 fusion.21
  322.7 1.2 fusion.34
  326.5 1.5 convolution_convert_fusion.1
  328.2 1.5 fusion.18
  329.8 4.6 %collective-permute-done = bf16[768,384]{1,0:T(8,128)(2,1)S(1)} collective-permute-done((bf16[768,384]{1,0:T(8,128)(2,1)}, bf16[768,384]{1,0:T(8,128)(2,1)S(1)}, u32[]{:S(2)}, u32[]{:S(2)}) %collective-permute-start) | collective-permute-done | bytes 589856 | tf_op jit(solution)/shard_map/ppermute | solution.py:1628
  334.6 56.7 %last.1 = (f32[160,1536]{1,0:T(8,128)S(1)}, f32[16,1536]{1,0:T(8,128)S(1)}, f32[192,384]{1,0:T(8,128)S(1)}, f32[192,640]{1,0:T(8,128)S(1)}) custom-call(bf16[4,160,1536]{2,1,0:T(8,128)(2,1)S(1)} %bitcast.44, bf16[160,1536]{1,0:T(8,128)(2,1)S(1)} %constant_dynamic-slice_fusion.2.x_ref, f32[1,1536]{1,0:T(1,128)S(1)} %reshape.72.gain, ...), custom_call_target="tpu_custom_call" | custom-call | bytes 162000000 | tf_op jit(solution)/shard_map/last/pallas_call | solution.py:1506
  395.0 2.2 convert_add_fusion
  (142 shorter events, 30.5 us)
Async XLA Ops:
  7.2 7.8 %copy-start = (bf16[1536,128]{1,0:T(8,128)(2,1)S(1)}, bf16[1536,128]{1,0:T(8,128)(2,1)}, u32[]{:S(2)}) copy-start(bf16[1536,128]{1,0:T(8,128)(2,1)} %param.17) | copy-start | bytes 1179652
  7.2 6.4 %copy-start.45 = (f32[1536]{0:T(1024)S(1)}, f32[1536]{0:T(1024)}, u32[]{:S(2)}) copy-start(f32[1536]{0:T(1024)} %param.14) | copy-start | bytes 18436
  7.2 6.4 %copy-start.30 = (bf16[640,1536]{1,0:T(8,128)(2,1)S(1)}, bf16[640,1536]{1,0:T(8,128)(2,1)}, u32[]{:S(2)}) copy-start(bf16[640,1536]{1,0:T(8,128)(2,1)} %param.13) | copy-start | bytes 5898244
  7.2 6.4 %copy-start.42 = (bf16[1536,128]{1,0:T(8,128)(2,1)S(1)}, bf16[1536,128]{1,0:T(8,128)(2,1)}, u32[]{:S(2)}) copy-start(bf16[1536,128]{1,0:T(8,128)(2,1)} %param.16) | copy-start | bytes 1179652
  7.2 90.0 %all-gather.2.cloned.1.call-start = ((), (), s32[]{:S(2)}) async-start(), calls=%async_computation.1 | async-start | bytes 2457600 | tf_op jit(solution)/shard_map/all_gather | solution.py:1563
  8.0 387.1 %reduce-scatter.2.cloned.1.call-start = ((), (), s32[]{:S(2)}) async-start(), calls=%async_computation.2 | async-start | bytes 2457600 | tf_op jit(solution)/shard_map/reduce_scatter | solution.py:1607
  58.3 3.3 copy-start.44
  60.5 2.8 copy-start.32
  151.7 46.0 %copy-start.48 = (bf16[384,640]{1,0:T(8,128)(2,1)S(1)}, bf16[384,640]{1,0:T(8,128)(2,1)}, u32[]{:S(2)}) copy-start(bf16[384,640]{1,0:T(8,128)(2,1)} %get-tuple-element.51) | copy-start | bytes 1474564
  197.6 2.1 copy-start.18
  197.7 2.4 copy-start.19
  197.7 2.6 copy-start.20
  197.7 2.8 copy-start.21
  197.7 2.8 copy-start.26
  197.7 2.8 copy-start.28
  319.2 15.2 %collective-permute-start = (bf16[768,384]{1,0:T(8,128)(2,1)}, bf16[768,384]{1,0:T(8,128)(2,1)S(1)}, u32[]{:S(2)}, u32[]{:S(2)}) collective-permute-start(bf16[768,384]{1,0:T(8,128)(2,1)} %constant_dynamic-slice_fusion), channel_id=1, source_target_pairs={{0,16},{16,0},{1,17},{17,1},{2,18},{18,2},{3,19},{19,3},{4,20},{20... | collective-permute-start | bytes 1769480 | tf_op jit(solution)/shard_map/ppermute | solution.py:1628
  328.0 6.5 %copy-start.38 = (bf16[1536,384]{1,0:T(8,128)(2,1)S(1)}, bf16[1536,384]{1,0:T(8,128)(2,1)}, u32[]{:S(2)}) copy-start(bf16[1536,384]{1,0:T(8,128)(2,1)} %copy-done.37) | copy-start | bytes 3538948
  328.2 6.4 %copy-start.13 = (f32[160,1536]{1,0:T(8,128)S(1)}, f32[160,1536]{1,0:T(8,128)}, u32[]{:S(2)}) copy-start(f32[160,1536]{1,0:T(8,128)} %copy-done.12) | copy-start | bytes 2949124
  334.6 60.4 %copy-start.6 = (f32[160,1536]{1,0:T(8,128)S(1)}, f32[160,1536]{1,0:T(8,128)}, u32[]{:S(2)}) copy-start(f32[160,1536]{1,0:T(8,128)} %copy-done.4) | copy-start | bytes 2949124
  392.3 2.1 copy-start.24
  392.3 4.9 %copy-start.15 = (f32[160,1536]{1,0:T(8,128)S(1)}, f32[160,1536]{1,0:T(8,128)}, u32[]{:S(2)}) copy-start(f32[160,1536]{1,0:T(8,128)} %copy-done.14) | copy-start | bytes 2949124
  395.0 3.2 copy-start.25
  395.0 3.9 copy-start.35
  400.1 2.0 copy-start.33
  (28 other events, 39.4 us)
Sparse Core Ops, SparseCore 0:
  9.6 22.9 all-gather.1
  145.8 43.1 reduce-scatter.1

commit v4 on v3

--- a/solution.py
+++ b/solution.py
@@ -13,6 +13,7 @@
 F32 = jnp.float32
 BF16 = jnp.bfloat16
 VMEM = pl.BlockSpec(memory_space=pltpu.VMEM)
+HBM = pl.BlockSpec(memory_space=pl.ANY)
 DMA = pltpu.SemaphoreType.DMA
 MIB = 2**20
 
@@ -35,10 +36,24 @@
     return jnp.dot(a, b, preferred_element_type=F32)
 
 
+class Staged:
+    def __init__(self, pairs, sems):
+        self.copies = [pltpu.make_async_copy(src, dst, sems.at[i]) for i, (src, dst) in enumerate(pairs)]
+
+    def start(self):
+        for copy in self.copies:
+            copy.start()
+
+    def wait(self, *which):
+        for i in which:
+            self.copies[i].wait()
+
+
 class Spread:
-    def __init__(self, n, own, below, above, all_ref, send, recv, local):
+    def __init__(self, n, own, below, above, all_ref, send, recv, local, short=False):
         self.n, self.own, self.below, self.above, self.all = n, own, below, above, all_ref
         self.send, self.recv, self.local = send, recv, local
+        self.top = n - 2 if short else n - 1
         s, self.c, m = lax.axis_index("seq"), lax.axis_index("ctx"), lax.axis_index("mp")
         self.lower, self.upper = lax.rem(self.c + n - 1, n), lax.rem(self.c + 1, n)
         self.up, self.down = (s, self.upper, m), (s, self.lower, m)
@@ -57,17 +72,30 @@
     def keep(self, i, src, b):
         return pltpu.make_async_copy(src, self.all.at[b], self.local.at[i])
 
+    def goes_up(self, b):
+        return jnp.logical_and(self.c < self.n - 1, self.c - b < self.top)
+
     def start(self):
+        if self.below is None:
+
+            @pl.when(self.c < self.n - 1)
+            def _():
+                self.move(self.c, self.own, self.up).start()
+        else:
+
+            @pl.when(jnp.logical_and(self.inner, self.goes_up(self.lower)))
+            def _():
+                self.move(self.lower, self.below, self.up).start()
+
+            @pl.when(self.c > 0)
+            def _():
+                self.keep(1, self.below, self.lower).start()
+
         @pl.when(self.inner)
         def _():
-            self.move(self.lower, self.below, self.up).start()
             self.move(self.upper, self.above, self.down).start()
 
         self.keep(0, self.own, self.c).start()
-
-        @pl.when(self.c > 0)
-        def _():
-            self.keep(1, self.below, self.lower).start()
 
         @pl.when(self.c < self.n - 1)
         def _():
@@ -75,13 +103,14 @@
 
     def tick(self, i):
         c, n = self.c, self.n
-
-        @pl.when(c - 1 - i >= 0)
+        off = i if self.below is None else i + 1
+
+        @pl.when(jnp.logical_and(c - off >= 0, off <= self.top))
         def _():
-            b = jnp.maximum(c - 1 - i, 0)
+            b = jnp.maximum(c - off, 0)
             self.move(b, self.all.at[b], self.up).wait_recv()
 
-            @pl.when(c < n - 1)
+            @pl.when(self.goes_up(b))
             def _():
                 self.move(b, self.all.at[b], self.up).start()
 
@@ -99,29 +128,34 @@
             self.tick(i)
             return carry
 
-        lax.fori_loop(first, self.n - 1, later, 0)
+        lax.fori_loop(first, self.n if self.below is None else self.n - 1, later, 0)
 
     def finish(self):
         self.keep(0, self.own, self.c).wait()
 
-        @pl.when(self.c > 0)
-        def _():
-            self.keep(1, self.below, self.lower).wait()
+        if self.below is not None:
+
+            @pl.when(self.c > 0)
+            def _():
+                self.keep(1, self.below, self.lower).wait()
 
         @pl.when(self.c < self.n - 1)
         def _():
             self.keep(2, self.above, self.upper).wait()
 
-        @pl.when(self.inner)
-        def _():
-            def sent(b, carry):
-                @pl.when(b != self.c)
-                def _():
-                    self.move(b, self.all.at[b], self.up).wait_send()
-
-                return carry
-
-            lax.fori_loop(0, self.n, sent, 0)
+        def sent(b, carry):
+            if self.below is None:
+                sent_up = jnp.logical_and(b <= self.c, self.goes_up(b))
+            else:
+                sent_up = jnp.logical_and(b < self.c, self.goes_up(b))
+
+            @pl.when(jnp.logical_or(sent_up, jnp.logical_and(b > self.c, self.c > 0)))
+            def _():
+                self.move(b, self.all.at[b], self.up).wait_send()
+
+            return carry
+
+        lax.fori_loop(0, self.n, sent, 0)
 
 
 class Neighbours:
@@ -150,16 +184,89 @@
         def _():
             self.move(1).start()
 
-    def finish(self):
+    def finish(self, up=True):
         @pl.when(self.c > 0)
         def _():
-            self.move(0).wait_recv()
+            if up:
+                self.move(0).wait_recv()
             self.move(1).wait_send()
 
         @pl.when(self.c < self.n - 1)
         def _():
             self.move(1).wait_recv()
-            self.move(0).wait_send()
+            if up:
+                self.move(0).wait_send()
+
+
+class LineSum:
+    ahead = 2
+
+    def __init__(self, n, parts, from_below, from_above, send, recv):
+        self.n, self.parts, self.from_below, self.from_above, self.send, self.recv = n, parts, from_below, from_above, send, recv
+        s, self.c, m = lax.axis_index("seq"), lax.axis_index("ctx"), lax.axis_index("mp")
+        self.up, self.down = (s, lax.rem(self.c + 1, n), m), (s, lax.rem(self.c + n - 1, n), m)
+        self.rows = from_below.shape[1]
+
+    def own(self, k):
+        return self.parts.at[pl.ds(pl.multiple_of(k * self.rows, 16), self.rows), :]
+
+    def move(self, way, k, first=False):
+        there = (self.from_below if way == 0 else self.from_above).at[k]
+        return pltpu.make_async_remote_copy(
+            src_ref=self.own(k) if first else there,
+            dst_ref=there,
+            send_sem=self.send.at[way, k],
+            recv_sem=self.recv.at[way, k],
+            device_id=self.up if way == 0 else self.down,
+            device_id_type=MESH,
+        )
+
+    def chunk(self, way, u):
+        return self.n - 1 - u if way == 0 else u
+
+    def first(self, u):
+        units = self.n - 1
+        for way, end in ((0, 0), (1, self.n - 1)):
+
+            @pl.when(jnp.logical_and(self.c == end, u < units))
+            def _():
+                @pl.when(u >= self.ahead)
+                def _():
+                    self.move(way, self.chunk(way, jnp.maximum(u - self.ahead, 0)), True).wait_send()
+
+                self.move(way, self.chunk(way, jnp.minimum(u, units - 1)), True).start()
+
+    def tick(self, i):
+        self.first(i + 1)
+        for way, far in ((0, self.c), (1, self.n - 1 - self.c)):
+            u = i - far
+            buf = self.from_below if way == 0 else self.from_above
+
+            @pl.when(jnp.logical_and(far > 0, jnp.logical_and(u >= 0, u < self.n - 1 - far)))
+            def _():
+                k = self.chunk(way, jnp.clip(u, 0, self.n - 2))
+                self.move(way, k).wait_recv()
+                buf[k] = (self.own(k)[...].astype(F32) + buf[k].astype(F32)).astype(BF16)
+                self.move(way, k).start()
+
+    def finish(self, out):
+        c = self.c
+        out[...] = self.own(c)[...].astype(F32)
+        for way, far in ((0, c), (1, self.n - 1 - c)):
+            buf = self.from_below if way == 0 else self.from_above
+
+            @pl.when(far > 0)
+            def _():
+                self.move(way, c).wait_recv()
+                out[...] = out[...] + buf[c].astype(F32)
+
+            done = jnp.where(far == 0, max(self.n - 1 - self.ahead, 0), 0)
+
+            def sent(u, carry):
+                self.move(way, self.chunk(way, u)).wait_send()
+                return carry
+
+            lax.fori_loop(done, self.n - 1 - far, sent, 0)
 
 
 class Peers:
@@ -194,53 +301,51 @@
 
 
 class CotExchange:
-    def __init__(self, line_ref, full, first, count, sems, local):
-        self.line, self.full, self.first, self.count, self.sems, self.local = line_ref, full, first, count, sems, local
-        s, c, m = lax.axis_index("seq"), lax.axis_index("ctx"), lax.axis_index("mp")
+    def __init__(self, n, line_ref, full, first, sems):
+        self.n, self.line, self.full, self.first, self.sems = n, line_ref, full, first, sems
+        self.count = full.shape[0]
+        s, self.c, m = lax.axis_index("seq"), lax.axis_index("ctx"), lax.axis_index("mp")
         self.m = m
         self.share = line_ref.shape[1]
         self.sib = m + 1 - 2 * lax.rem(m, 2)
         self.opp = lax.rem(m + 2, 4)
-        self.sib_id, self.opp_id = (s, c, self.sib), (s, c, self.opp)
+        self.sib_id, self.opp_id = (s, self.c, self.sib), (s, self.c, self.opp)
 
     def signal(self, sem):
         for d in (self.sib_id, self.opp_id):
             pl.semaphore_signal(sem, inc=1, device_id=d, device_id_type=MESH)
 
-    def place(self, who):
-        return self.full.at[:, pl.ds(pl.multiple_of(who * self.share, 16), self.share), :]
-
-    def move(self, i):
-        mine = self.line.at[pl.ds(self.first, self.count)]
-        src = self.place(self.opp) if i == 2 else mine
-        whose = self.opp if i == 2 else self.m
+    def place(self, i, who):
+        return self.full.at[i, pl.ds(pl.multiple_of(who * self.share, 16), self.share), :]
+
+    def mine(self, i):
+        return self.line.at[lax.rem(self.c - self.first - i + 2 * self.n, self.n)]
+
+    def move(self, kind, i):
+        whose = self.opp if kind == 2 else self.m
         return pltpu.make_async_remote_copy(
-            src_ref=src,
-            dst_ref=self.place(whose),
-            send_sem=self.sems.at[0, i],
-            recv_sem=self.sems.at[1, i],
-            device_id=self.opp_id if i == 0 else self.sib_id,
+            src_ref=self.place(i, self.opp) if kind == 2 else self.mine(i),
+            dst_ref=self.place(i, whose),
+            send_sem=self.sems.at[0, kind, i],
+            recv_sem=self.sems.at[1, kind, i],
+            device_id=self.opp_id if kind == 0 else self.sib_id,
             device_id_type=MESH,
         )
 
-    def own(self):
-        return pltpu.make_async_copy(
-            self.line.at[pl.ds(self.first, self.count)], self.place(self.m), self.local.at[0]
-        )
-
     def start(self):
-        self.move(0).start()
-        self.move(1).start()
-        self.own().start()
+        for i in range(self.count):
+            self.move(0, i).start()
+            self.move(1, i).start()
 
     def finish(self):
-        self.move(0).wait_recv()
-        self.move(2).start()
-        self.own().wait()
-        self.move(1).wait_recv()
-        self.move(2).wait_recv()
-        for i in range(3):
-            self.move(i).wait_send()
+        for i in range(self.count):
+            self.move(0, i).wait_recv()
+            self.move(2, i).start()
+        for i in range(self.count):
+            self.move(1, i).wait_recv()
+            self.move(2, i).wait_recv()
+            for kind in range(3):
+                self.move(kind, i).wait_send()
 
 
 def signal_line(n, sem):
@@ -285,7 +390,6 @@
     heads_ref,
     lse_ref,
     kv_ref,
-    below_ref,
     above_ref,
     line_ref,
     qpad,
@@ -306,7 +410,7 @@
     kv_ref[0, :, kvw:] = v_ref[...]
     line_ref[c] = routes_ref[...]
     peers = Peers(n, lambda p: routes_ref, lambda i: line_ref.at[i], peers_sem.at[0], peers_sem.at[1])
-    beside = Neighbours(n, cot_ref, below_ref, above_ref, side.at[0], side.at[1])
+    beside = Neighbours(n, cot_ref, None, above_ref, side.at[0], side.at[1])
     sem = pltpu.get_barrier_semaphore()
     peers.signal(sem)
     pl.semaphore_wait(sem, n - 1)
@@ -372,16 +476,8 @@
         def _():
             pass_up(slot).start()
 
-        @pl.when(slot == c)
-        def _():
-            beside.start_up()
-
         block(slot, False)
         return carry
-
-    @pl.when(c == 0)
-    def _():
-        beside.start_up()
 
     lax.fori_loop(1, c + 1, earlier, 0)
     for h in range(heads):
@@ -400,7 +496,7 @@
         lax.fori_loop(0, c + 1, sent, 0)
 
     peers.finish()
-    beside.finish()
+    beside.finish(up=False)
 
 
 def attend(n, qt, k, v, cot, routes):
@@ -415,11 +511,10 @@
             jax.ShapeDtypeStruct((heads, 1, t), F32),
             jax.ShapeDtypeStruct((n, t, 2 * kvw), BF16),
             jax.ShapeDtypeStruct(cot.shape, BF16),
-            jax.ShapeDtypeStruct(cot.shape, BF16),
             jax.ShapeDtypeStruct((n,) + routes.shape, jnp.int32),
         ),
-        in_specs=[VMEM] * 5,
-        out_specs=(VMEM,) * 7,
+        in_specs=[VMEM] * 3 + [HBM, VMEM],
+        out_specs=(VMEM,) * 4 + (HBM, VMEM),
         scratch_shapes=[
             pltpu.VMEM((heads, kvw, t), BF16),
             pltpu.VMEM((kvw, t), BF16),
@@ -438,7 +533,6 @@
 
 def attend_back_kernel(
     n,
-    n_seq,
     q_ref,
     db_ref,
     wout_ref,
@@ -449,21 +543,24 @@
     arr_other,
     dg_ref,
     dg_other,
+    rows_line,
     own_ref,
     below_ref,
     above_ref,
-    rows_line,
-    hid_line,
-    arr_line,
+    hid_hbm,
+    hid_own,
+    arr_hbm,
     place_hbm,
     line_hbm,
     first_hbm,
-    dq_ref,
-    dkv_ref,
-    summed_ref,
+    dqkv_ref,
+    gate_ref,
+    gate_parts,
+    down_ref,
+    down_other,
     up_ref,
-    down_ref,
-    all_ref,
+    up_other,
+    all_hbm,
     rest_hbm,
     do_ref,
     qpad,
@@ -478,138 +575,58 @@
     from_above,
     place_buf,
     cot_buf,
+    hid_buf,
+    arr_buf,
     du_buf,
     dy,
-    d_acc,
-    u_acc,
-    d_out,
-    d_in,
-    u_out,
-    u_in,
-    send,
-    recv,
+    acc_ref,
+    kv_sem,
+    sum_sem,
     spread_sem,
     local,
     ysem,
-    cot_local,
     load_sem,
-    swap_sem,
 ):
     s, c, m = lax.axis_index("seq"), lax.axis_index("ctx"), lax.axis_index("mp")
     _, t, kvw2 = kv_ref.shape
     kvw = kvw2 // 2
     heads = q_ref.shape[0] // HEAD_SIZE
     group = heads // (kvw // HEAD_SIZE)
-    ex = sum_ref.shape[0]
-    half_width = sum_ref.shape[1]
-    chunk_rows = half_width // n
-    slots = arr_ref.shape[1]
-    width = db_ref.shape[1]
-    up, down = (s, lax.rem(c + 1, n), m), (s, lax.rem(c + n - 1, n), m)
-    spread = Spread(n, own_ref, below_ref, above_ref, all_ref, spread_sem.at[0], spread_sem.at[1], local)
+    ex, slots, width = arr_ref.shape
+    half_width = width // 2
+    down = (s, lax.rem(c + n - 1, n), m)
+    spread = Spread(n, own_ref, below_ref, above_ref, all_hbm, spread_sem.at[0], spread_sem.at[1], local)
     done_blocks = first_hbm.shape[0]
-    cots = CotExchange(line_hbm, rest_hbm, done_blocks, n - done_blocks, ysem, cot_local)
+    cots = CotExchange(n, line_hbm, rest_hbm, done_blocks, ysem)
+    line = LineSum(n, sum_ref, from_below, from_above, sum_sem.at[0], sum_sem.at[1])
     sem = pltpu.get_barrier_semaphore()
     signal_line(n, sem)
     cots.signal(sem)
-    pl.semaphore_signal(sem, inc=1, device_id=swap_partner(), device_id_type=MESH)
-    pl.semaphore_wait(sem, line_degree(n) + 3)
+    pl.semaphore_wait(sem, line_degree(n) + 2)
+    spread.start()
     cots.start()
-    spread.start()
-
-    def gate_part(i):
-        e, r = lax.div(i, half_width // 256), lax.rem(i, half_width // 256)
-        mine = pl.ds(pl.multiple_of(s * half_width + r * 256, 128), 256)
-        cut = pl.ds(pl.multiple_of(r * 256, 256), 256)
-        sum_ref[e, cut, :] = (
-            tn(arr_ref[e, :, mine], dg_ref[e]) + tn(arr_other[e, :, cut], dg_other[e])
-        ).astype(BF16)
-
-    loop(ex * (half_width // 256), gate_part)
-
-    def remote(kind, i, src, dst, device):
-        return pltpu.make_async_remote_copy(
-            src_ref=src,
-            dst_ref=dst,
-            send_sem=send.at[kind, i],
-            recv_sem=recv.at[kind, i],
-            device_id=device,
-            device_id_type=MESH,
-        )
-
-    def own_unit(k, e):
-        return sum_ref.at[e, pl.ds(pl.multiple_of(k * chunk_rows, 16), chunk_rows), :]
-
-    def sum_up(k, e, first=False):
-        there = from_below.at[k, e]
-        return remote(1, k * ex + e, own_unit(k, e) if first else there, there, up)
-
-    def sum_down(k, e, first=False):
-        there = from_above.at[k, e]
-        return remote(2, k * ex + e, own_unit(k, e) if first else there, there, down)
-
-    units = (n - 1) * ex
-    ahead = 2
-
-    def first_up(u):
-        @pl.when(jnp.logical_and(c == 0, u < units))
-        def _():
-            @pl.when(u >= ahead)
-            def _():
-                v = jnp.maximum(u - ahead, 0)
-                sum_up(n - 1 - lax.div(v, ex), lax.rem(v, ex), True).wait_send()
-
-            w = jnp.minimum(u, units - 1)
-            sum_up(n - 1 - lax.div(w, ex), lax.rem(w, ex), True).start()
-
-    def first_down(u):
-        @pl.when(jnp.logical_and(c == n - 1, u < units))
-        def _():
-            @pl.when(u >= ahead)
-            def _():
-                v = jnp.maximum(u - ahead, 0)
-                sum_down(lax.div(v, ex), lax.rem(v, ex), True).wait_send()
-
-            w = jnp.minimum(u, units - 1)
-            sum_down(lax.div(w, ex), lax.rem(w, ex), True).start()
-
-    first_up(0)
-    first_down(0)
+
+    def gate_part(e, out):
+        def piece(r):
+            mine = pl.ds(pl.multiple_of(s * half_width + r * 256, 128), 256)
+            cut = pl.ds(pl.multiple_of(r * 256, 256), 256)
+            out[cut, :] = (tn(arr_ref[e, :, mine], dg_ref[e]) + tn(arr_other[e, :, cut], dg_other[e])).astype(BF16)
+
+        loop(half_width // 256, piece)
+
+    gate_part(0, sum_ref)
+    line.first(0)
     do_ref[...] = nt(wout_ref[...], db_ref[...]).astype(BF16)
 
     def tick(i):
-        first_up(i + 1)
-        first_down(i + 1)
+        line.tick(i)
         for hop in range(1, n - 1):
 
-            @pl.when(i == hop * ex)
+            @pl.when(i == 2 * hop)
             def _():
                 spread.tick(hop)
 
-        u = i - c
-        k = n - 1 - lax.div(jnp.maximum(u, 0), ex)
-        e = lax.rem(jnp.maximum(u, 0), ex)
-
-        @pl.when(jnp.logical_and(c > 0, jnp.logical_and(u >= 0, k > c)))
-        def _():
-            there = jnp.maximum(k, 0)
-            sum_up(there, e).wait_recv()
-            from_below[there, e] = (own_unit(there, e)[...].astype(F32) + from_below[there, e].astype(F32)).astype(BF16)
-            sum_up(there, e).start()
-
-        v = i - (n - 1 - c)
-        kd = lax.div(jnp.maximum(v, 0), ex)
-        ed = lax.rem(jnp.maximum(v, 0), ex)
-
-        @pl.when(jnp.logical_and(c < n - 1, jnp.logical_and(v >= 0, kd < c)))
-        def _():
-            there = jnp.minimum(kd, n - 1)
-            sum_down(there, ed).wait_recv()
-            from_above[there, ed] = (own_unit(there, ed)[...].astype(F32) + from_above[there, ed].astype(F32)).astype(BF16)
-            sum_down(there, ed).start()
-
-    last_tick = units + n
-
+    ticks = 2 * (n - 2) + 1
     pad_heads(q_ref, qpad, heads, group)
     pad_heads(do_ref, dopad, heads, group)
     for h in range(heads):
@@ -641,7 +658,14 @@
         lax.fori_loop(0, heads, head, 0)
 
     def pass_down(j):
-        return remote(0, j, passing.at[j], passing.at[j], down)
+        return pltpu.make_async_remote_copy(
+            src_ref=passing.at[j],
+            dst_ref=passing.at[j],
+            send_sem=kv_sem.at[0, j],
+            recv_sem=kv_sem.at[1, j],
+            device_id=down,
+            device_id_type=MESH,
+        )
 
     def gathered(j):
         acc = part.at[lax.rem(j, 2)]
@@ -675,117 +699,134 @@
     lax.fori_loop(0, c, step, 0)
     block(c, True)
 
-    @pl.when(spread.inner)
+    @pl.when(jnp.logical_and(c > 0, c < n - 1))
     def _():
         forward(c - 1)
 
-    dq_ref[...] = (dq[...] * 0.125).astype(BF16)
+    qw = dq.shape[0]
+    dqkv_ref[:, :qw] = (dq[...] * 0.125).astype(BF16).T
+    for e in range(1, ex):
+        gate_part(e, gate_parts.at[e - 1])
 
     def later(i, carry):
         tick(i)
         return carry
 
-    pause = jnp.maximum(c, 2 * ex)
-    lax.fori_loop(c, pause, later, 0)
-    acc = gathered(c)
-    dkv_ref[...] = acc[...].astype(BF16)
+    middle = jnp.maximum(c, min(3, ticks))
+    lax.fori_loop(c, middle, later, 0)
 
     cots.finish()
 
-    def load_block(b, slot, start):
+    def load_block(i, slot, start):
+        b = lax.rem(c - i + n, n)
+        share = line_hbm.shape[1]
         place_copy = pltpu.make_async_copy(place_hbm.at[b], place_buf.at[slot], load_sem.at[0, slot])
-        first_copy = pltpu.make_async_copy(
-            first_hbm.at[jnp.minimum(b, done_blocks - 1)], cot_buf.at[slot], load_sem.at[1, slot]
-        )
-        rest_copy = pltpu.make_async_copy(
-            rest_hbm.at[jnp.maximum(b - done_blocks, 0)], cot_buf.at[slot], load_sem.at[1, slot]
-        )
-        if start:
-            place_copy.start()
-
-            @pl.when(b < done_blocks)
-            def _():
-                first_copy.start()
-
-            @pl.when(b >= done_blocks)
-            def _():
-                rest_copy.start()
-        else:
-            place_copy.wait()
-            first_copy.wait()
-
-    d_acc[...] = jnp.zeros_like(d_acc)
+        hid_copy = pltpu.make_async_copy(hid_hbm.at[b], hid_buf.at[slot], load_sem.at[1, slot])
+        hid_mine = pltpu.make_async_copy(hid_own.at[b], hid_buf.at[slot], load_sem.at[1, slot])
+
+        def rows(who):
+            return pl.ds(pl.multiple_of(who * share, 16), share)
+
+        def piece(k, who, full, at):
+            return pltpu.make_async_copy(
+                full.at[at, rows(who), :], cot_buf.at[slot, rows(who), :], load_sem.at[2 + k, slot]
+            )
+
+        others = (cots.sib, cots.opp, lax.rem(cots.sib + 2, 4))
+        mine = pltpu.make_async_copy(line_hbm.at[b], cot_buf.at[slot, rows(m), :], load_sem.at[5, slot])
+        first = [piece(k, who, first_hbm, jnp.minimum(i, done_blocks - 1)) for k, who in enumerate(others)]
+        if not start:
+            for copy in [place_copy, hid_copy, mine] + first:
+                copy.wait()
+            return
+        rest = [piece(k, who, rest_hbm, jnp.maximum(i - done_blocks, 0)) for k, who in enumerate(others)]
+        place_copy.start()
+        mine.start()
+
+        @pl.when(b == c)
+        def _():
+            hid_mine.start()
+
+        @pl.when(b != c)
+        def _():
+            hid_copy.start()
+
+        @pl.when(i < done_blocks)
+        def _():
+            for copy in first:
+                copy.start()
+
+        @pl.when(i >= done_blocks)
+        def _():
+            for copy in rest:
+                copy.start()
+
+    fa, ua = hid_hbm.shape[3], arr_hbm.shape[3]
+    ff = dg_ref.shape[2]
+    acc_ref[...] = jnp.zeros_like(acc_ref)
     load_block(0, 0, True)
     wide = 512
 
-    def down_block(b):
-        slot = lax.rem(b, 2)
-        load_block(b, slot, False)
-
-        @pl.when(b < n - 1)
+    def down_block(i):
+        slot = lax.rem(i, 2)
+        load_block(i, slot, False)
+
+        @pl.when(i < n - 1)
         def _():
-            load_block(b + 1, 1 - slot, True)
-
-        cols = rows_line[b].T
+            load_block(i + 1, 1 - slot, True)
+
+        cols = rows_line[lax.rem(c - i + n, n)].T
         for e in range(ex):
 
-            def dys(i):
-                cut = pl.ds(pl.multiple_of(i * wide, wide), wide)
+            def dys(k):
+                cut = pl.ds(pl.multiple_of(k * wide, wide), wide)
                 dy[:, cut] = (
                     cols[:slots, e : e + 1] * nn(place_buf[slot, e * slots : (e + 1) * slots, :], cot_buf[slot, :, cut])
                 ).astype(BF16)
 
             loop(width // wide, dys)
-            for j in range(n_seq):
-                d_acc[j, e] = d_acc[j, e] + tn(hid_line[b, j, e], dy[...])
+            acc_ref[e, :fa, :] = acc_ref[e, :fa, :] + tn(hid_buf[slot, e], dy[...])
 
     loop(n, down_block)
-    d_out[...] = d_acc[1 - s].astype(BF16)
-    d_swap = swap(d_out, d_in, swap_sem, 0)
-    d_swap.start()
-    lax.fori_loop(pause, last_tick, later, 0)
+    mine, other = (pl.ds(pl.multiple_of(k * (fa // 2), 16), fa // 2) for k in (s, 1 - s))
+    down_ref[...] = acc_ref[:, mine, :]
+    down_other[...] = acc_ref[:, other, :].astype(BF16)
+
+    lax.fori_loop(middle, ticks, later, 0)
 
     spread.finish()
-    u_acc[...] = jnp.zeros_like(u_acc)
+    acc_ref[...] = jnp.zeros_like(acc_ref)
 
     def load_du(b, slot):
-        return pltpu.make_async_copy(all_ref.at[b], du_buf.at[slot], load_sem.at[2, slot])
-
-    load_du(0, 0).start()
+        return (
+            pltpu.make_async_copy(all_hbm.at[b], du_buf.at[slot], load_sem.at[6, slot]),
+            pltpu.make_async_copy(arr_hbm.at[b], arr_buf.at[slot], load_sem.at[7, slot]),
+        )
+
+    for copy in load_du(0, 0):
+        copy.start()
 
     def up_block(b):
         slot = lax.rem(b, 2)
-        load_du(b, slot).wait()
+        for copy in load_du(b, slot):
+            copy.wait()
 
         @pl.when(b < n - 1)
         def _():
-            load_du(b + 1, 1 - slot).start()
+            for copy in load_du(b + 1, 1 - slot):
+                copy.start()
 
         for e in range(ex):
-            for j in range(n_seq):
-                u_acc[j, e] = u_acc[j, e] + tn(arr_line[b, j, e], du_buf[slot, e])
+            acc_ref[e, :ua, :ff] = acc_ref[e, :ua, :ff] + tn(arr_buf[slot, e], du_buf[slot, e])
 
     loop(n, up_block)
-    u_out[...] = u_acc[1 - s].astype(BF16)
-    u_swap = swap(u_out, u_in, swap_sem, 1)
-    u_swap.start()
-    for e in range(ex):
-        summed_ref[e] = own_unit(c, e)[...].astype(F32)
-
-        @pl.when(c > 0)
-        def _():
-            sum_up(c, e).wait_recv()
-            summed_ref[e] = summed_ref[e] + from_below[c, e].astype(F32)
-
-        @pl.when(c < n - 1)
-        def _():
-            sum_down(c, e).wait_recv()
-            summed_ref[e] = summed_ref[e] + from_above[c, e].astype(F32)
-
-    d_swap.wait()
-    down_ref[...] = d_acc[s] + d_in[...].astype(F32)
-    u_swap.wait()
-    up_ref[...] = u_acc[s] + u_in[...].astype(F32)
+    mine, other = (pl.ds(pl.multiple_of(k * (ua // 2), 16), ua // 2) for k in (s, 1 - s))
+    up_ref[...] = acc_ref[:, mine, :ff]
+    up_other[...] = acc_ref[:, other, :ff].astype(BF16)
+
+    acc = gathered(c)
+    dqkv_ref[:, qw:] = acc[...].astype(BF16)
+    line.finish(gate_ref)
 
     def sent_kv(j, carry):
         pass_down(j).wait_send()
@@ -793,51 +834,33 @@
 
     lax.fori_loop(0, c, sent_kv, 0)
 
-    done = jnp.where(c == 0, units - ahead, 0)
-
-    @pl.when(c < n - 1)
-    def _():
-        def sent(u, carry):
-            sum_up(n - 1 - lax.div(u, ex), lax.rem(u, ex)).wait_send()
-            return carry
-
-        lax.fori_loop(done, (n - 1 - c) * ex, sent, 0)
-
-    done_down = jnp.where(c == n - 1, units - ahead, 0)
-
-    @pl.when(c > 0)
-    def _():
-        def sent(u, carry):
-            sum_down(lax.div(u, ex), lax.rem(u, ex)).wait_send()
-            return carry
-
-        lax.fori_loop(done_down, c * ex, sent, 0)
-
-
-def attend_back(n, n_seq, qt, db, w_out, o, lse, kv, arr, arr_other, dg, dg_other, du, below, above, rows, hid, arr_line, place, line, first):
+
+def attend_back(n, qt, db, w_out, o, lse, kv, arr, arr_other, dg, dg_other, rows, du, below, above, hid, hid_own, arr_line, place, line, first):
     qw, t = qt.shape
     heads = qw // HEAD_SIZE
     kvw = kv.shape[2] // 2
     ex, slots, width = arr.shape
     ff = dg.shape[2]
     half_width = width // 2
-    chunk = (ex, half_width // n, ff)
-    down_chunk = (ex, hid.shape[4], width)
-    any_ = pl.BlockSpec(memory_space=pl.ANY)
+    chunk = (half_width // n, ff)
+    fa, ua = hid.shape[3], arr_line.shape[3]
+    blocks = first.shape[0]
     sds = jax.ShapeDtypeStruct
     return pl.pallas_call(
-        functools.partial(attend_back_kernel, n, n_seq),
+        functools.partial(attend_back_kernel, n),
         out_shape=(
-            sds((qw, t), BF16),
-            sds((t, 2 * kvw), BF16),
+            sds((t, qw + 2 * kvw), BF16),
             sds(chunk, F32),
-            sds(chunk, F32),
-            sds(down_chunk, F32),
+            sds((ex - 1, half_width, ff), BF16),
+            sds((ex, fa // 2, width), F32),
+            sds((ex, fa // 2, width), BF16),
+            sds((ex, ua // 2, ff), F32),
+            sds((ex, ua // 2, ff), BF16),
             sds((n,) + du.shape, BF16),
-            sds((n - first.shape[0],) + first.shape[1:], BF16),
+            sds((n - blocks,) + first.shape[1:], BF16),
         ),
-        in_specs=[VMEM] * 16 + [any_] * 3,
-        out_specs=(VMEM,) * 5 + (any_,) * 2,
+        in_specs=[VMEM] * 14 + [HBM] * 6,
+        out_specs=(VMEM,) * 7 + (HBM,) * 2,
         scratch_shapes=[
             pltpu.VMEM((qw, t), BF16),
             pltpu.VMEM((heads, kvw, t), BF16),
@@ -847,32 +870,27 @@
             pltpu.VMEM((kvw, t), BF16),
             pltpu.VMEM((2, t, 2 * kvw), F32),
             pltpu.VMEM((n, t, 2 * kvw), BF16),
-            pltpu.VMEM((ex, half_width, ff), BF16),
+            pltpu.VMEM((half_width, ff), BF16),
             pltpu.VMEM((n,) + chunk, BF16),
             pltpu.VMEM((n,) + chunk, BF16),
             pltpu.VMEM((2,) + place.shape[1:], BF16),
             pltpu.VMEM((2,) + first.shape[1:], BF16),
+            pltpu.VMEM((2, ex, slots, fa), BF16),
+            pltpu.VMEM((2, ex, slots, ua), BF16),
             pltpu.VMEM((2,) + du.shape, BF16),
             pltpu.VMEM((slots, width), BF16),
-            pltpu.VMEM((n_seq,) + down_chunk, F32),
-            pltpu.VMEM((n_seq,) + chunk, F32),
-            pltpu.VMEM(down_chunk, BF16),
-            pltpu.VMEM(down_chunk, BF16),
-            pltpu.VMEM(chunk, BF16),
-            pltpu.VMEM(chunk, BF16),
-            DMA((3, n * ex)),
-            DMA((3, n * ex)),
+            pltpu.VMEM((ex, max(fa, ua), width), F32),
+            DMA((2, n)),
+            DMA((2, 2, n)),
             DMA((2, n)),
             DMA((3,)),
-            DMA((2, 3)),
-            DMA((1,)),
-            DMA((3, 2)),
-            DMA((2, 2)),
+            DMA((2, 3, n - blocks)),
+            DMA((8, 2)),
         ],
-        compiler_params=params(1, 63),
+        compiler_params=params(1, 60),
         name="attend_back",
-        cost_estimate=cost(80),
-    )(qt, db, w_out, o, lse, kv, arr, arr_other, dg, dg_other, du, below, above, rows, hid, arr_line, place, line, first)
+        cost_estimate=cost(60),
+    )(qt, db, w_out, o, lse, kv, arr, arr_other, dg, dg_other, rows, du, below, above, hid, hid_own, arr_line, place, line, first)
 
 
 def tn(a, b):
@@ -895,7 +913,7 @@
     cot_ref,
     place_ref,
     place_t_ref,
-    sel_ref,
+    routes_ref,
     router_ref,
     wg_hbm,
     wu_hbm,
@@ -911,6 +929,7 @@
     comb_ref,
     arr_line,
     cot_first,
+    line_out,
     wg,
     wu,
     wd,
@@ -925,6 +944,8 @@
     peers_sem,
     ysem,
     local,
+    far_sem,
+    router3,
 ):
     s, c, m = lax.axis_index("seq"), lax.axis_index("ctx"), lax.axis_index("mp")
     ex, width, ff = wg.shape
@@ -932,7 +953,15 @@
     first = m * ex
     lanes = gates_ref.shape[1]
     peers = Peers(n, lambda p: parts.at[p], lambda i: arr_line.at[i], peers_sem.at[0], peers_sem.at[1])
-    cots = CotExchange(line_hbm, cot_first, 0, cot_first.shape[0], ysem, local)
+    cots = CotExchange(n, line_hbm, cot_first, 0, ysem)
+    far = pltpu.make_async_remote_copy(
+        src_ref=line_hbm.at[0],
+        dst_ref=line_out.at[0],
+        send_sem=far_sem.at[0],
+        recv_sem=far_sem.at[1],
+        device_id=(s, lax.rem(c + 1, n), m),
+        device_id_type=MESH,
+    )
     sem = pltpu.get_barrier_semaphore()
     peers.signal(sem)
     cots.signal(sem)
@@ -955,16 +984,30 @@
         for i in range(n):
             for j in range(n_seq):
                 at = (j * n + i) * size
-                parts[i, j, e] = arr_ref[e, :, at : at + size]
+                parts[i, e, :, j * size : (j + 1) * size] = arr_ref[e, :, at : at + size]
     pl.semaphore_wait(sem, n - 1 + 2)
     peers.start()
     cots.start()
-    own = pltpu.make_async_copy(parts.at[c], arr_line.at[c], local.at[1])
+
+    @pl.when(c == n - 2)
+    def _():
+        far.start()
+
+    own = pltpu.make_async_copy(parts.at[c], arr_line.at[c], local.at[0])
     own.start()
 
-    three = nn(h_ref[...], router_ref[...])
+    router3[...] = jnp.zeros_like(router3)
+    left = router_ref[...]
+    for i in range(3):
+        piece = left.astype(BF16)
+        router3[:, i * experts_all : (i + 1) * experts_all] = piece
+        left = left - piece.astype(F32)
+    three = nn(h_ref[...], router3[...])
     logits = three + pltpu.roll(three, lanes - experts_all, 1) + pltpu.roll(three, lanes - 2 * experts_all, 1)
-    chosen = sel_ref[...] > 0.0
+    which = lax.broadcasted_iota(jnp.int32, three.shape, 1)
+    chosen = which == routes_ref[:, 0:1]
+    for k in range(1, routes_ref.shape[1]):
+        chosen = jnp.logical_or(chosen, which == routes_ref[:, k : k + 1])
     peak = jnp.max(jnp.where(chosen, logits, -1e30), axis=1, keepdims=True)
     raised = jnp.where(chosen, jnp.exp(jnp.where(chosen, logits - peak, 0.0)), 0.0)
     gates = raised / jnp.sum(raised, axis=1, keepdims=True)
@@ -1014,7 +1057,7 @@
         for i in range(n):
             for j in range(n_seq):
                 at = (j * n + i) * size
-                hid_ref[i, j, e] = hid[:, at : at + size]
+                hid_ref[i, e, :, j * size : (j + 1) * size] = hid[:, at : at + size]
 
         def outs(i, grads):
             cut = pl.ds(pl.multiple_of(i * wide, wide), wide)
@@ -1036,18 +1079,23 @@
     loop(width // 256, scatter)
     back_ref[:, width:] = nn(place_t_ref[...], back_rows[:, width:]).astype(BF16)
     own.wait()
+    cots.finish()
     peers.finish()
-    cots.finish()
-
-
-def moe(n, n_seq, experts_all, h, cot, place, place_t, sel, router3, wg, wu, wd, line):
+
+    @pl.when(c == n - 2)
+    def _():
+        far.wait_send()
+
+    @pl.when(c == n - 1)
+    def _():
+        far.wait_recv()
+
+
+def moe(n, n_seq, experts_all, h, cot, place, place_t, routes, router, wg, wu, wd, line):
     ex, width, ff = wg.shape
     tok = h.shape[0]
     slots = place.shape[0] // ex
-    share = line.shape[1]
     blocks = n // 2
-    size = width // (n * n_seq)
-    any_ = pl.BlockSpec(memory_space=pl.ANY)
     sds = jax.ShapeDtypeStruct
     return pl.pallas_call(
         functools.partial(moe_kernel, n, n_seq, experts_all),
@@ -1055,16 +1103,17 @@
             sds((tok, 128), F32),
             sds((8, 256), F32),
             sds((ex, slots, width), BF16),
-            sds((n, n_seq, ex, slots, ff // (n * n_seq)), BF16),
+            sds((n, ex, slots, ff // n), BF16),
             sds((ex, slots, ff), BF16),
             sds((ex, slots, ff), BF16),
             sds((tok, width + 128), BF16),
             sds((tok, width), BF16),
-            sds((n, n_seq, ex, slots, size), BF16),
+            sds((n, ex, slots, width // n), BF16),
             sds((blocks, tok, width), BF16),
+            sds(line.shape, BF16),
         ),
-        in_specs=[VMEM] * 6 + [any_] * 4,
-        out_specs=(VMEM,) * 8 + (VMEM, any_),
+        in_specs=[VMEM] * 6 + [HBM] * 4,
+        out_specs=(VMEM,) * 8 + (HBM,) * 3,
         scratch_shapes=[
             pltpu.VMEM(wg.shape, BF16),
             pltpu.VMEM(wu.shape, BF16),
@@ -1074,17 +1123,20 @@
             pltpu.VMEM((slots, ff), BF16),
             pltpu.VMEM((ex * slots, width + 128), BF16),
             pltpu.VMEM((ex * slots, width), BF16),
-            pltpu.VMEM((n, n_seq, ex, slots, size), BF16),
+            pltpu.VMEM((n, ex, slots, width // n), BF16),
             pltpu.VMEM((256, 128), F32),
             DMA((3, ex)),
             DMA((2, n)),
-            DMA((2, 3)),
+            DMA((2, 3, blocks)),
+            DMA((1,)),
             DMA((2,)),
+            pltpu.VMEM((width, 128), BF16),
         ],
+        input_output_aliases={9: 10},
         compiler_params=params(6, 60),
         name="moe",
         cost_estimate=cost(30),
-    )(h, cot, place, place_t, sel, router3, wg, wu, wd, line)
+    )(h, cot, place, place_t, routes, router, wg, wu, wd, line)
 
 
 class Mp:
@@ -1193,16 +1245,65 @@
 
 
 def mid_forward_kernel(
-    chunks, n, part, x_ref, gain, own, below, above, resid_ref, h_ref, line_ref, core_in, y_out, y_in, sems, send, recv, local
+    chunks,
+    n,
+    ex,
+    part,
+    gain,
+    own,
+    above,
+    routes_ref,
+    tok_hbm,
+    resid_ref,
+    h_ref,
+    place_ref,
+    place_t,
+    place_line,
+    line_ref,
+    core_in,
+    y_out,
+    y_in,
+    sems,
+    send,
+    recv,
+    local,
+    x_ref,
+    x_sem,
+    ranks,
 ):
+    c = lax.axis_index("ctx")
     mp = Mp(part, core_in, y_out, y_in, h_ref, sems, chunks)
-    spread = Spread(n, own, below, above, line_ref, send, recv, local)
+    spread = Spread(n, own, None, above, line_ref, send, recv, local, short=True)
+    x_copy = pltpu.make_async_copy(tok_hbm.at[mp.m], x_ref, x_sem.at[0])
+    x_copy.start()
     sem = pltpu.get_barrier_semaphore()
     mp.signal(sem)
     signal_line(n, sem)
     pl.semaphore_wait(sem, 2 + line_degree(n))
-    mp.rs_begin()
+    mp.rs_core(0).start()
+    mp.rs_core(1).start()
     spread.start()
+    mp.rs_forward()
+    tok = routes_ref.shape[2]
+    slots = place_ref.shape[0] // ex
+    before = (
+        lax.broadcasted_iota(jnp.int32, (tok, tok), 0) <= lax.broadcasted_iota(jnp.int32, (tok, tok), 1)
+    ).astype(BF16)
+
+    def places(b):
+        at = b * ex
+        ranks[...] = jnp.zeros_like(ranks)
+        for e in range(ex):
+            hit = routes_ref[b] == mp.m * ex + e
+            ranks[e : e + 1, :] = jnp.max(hit.astype(F32), axis=0, keepdims=True)
+        sel = ranks[...]
+        order = nn(sel.astype(BF16), before) - 1.0
+        rows = lax.broadcasted_iota(jnp.int32, (slots, tok), 0).astype(F32)
+        for e in range(ex):
+            one = jnp.where(rows == order[e : e + 1, :], 1.0, 0.0) * sel[e : e + 1, :]
+            place_line[b, e * slots : (e + 1) * slots, :] = one.astype(BF16)
+
+    x_copy.wait()
     for i in range(chunks):
         cut = mp.cut(i)
         resid = x_ref[cut, :].astype(F32) + mp.rs_chunk(i)
@@ -1210,30 +1311,39 @@
         normed, _ = rms_parts(resid)
         h_ref[mp.m, cut, :] = (normed * gain[...]).astype(BF16)
         mp.ag_send(i)
-    if n > 2:
-        spread.tick(1)
+    places(c)
+    place_ref[...] = place_line[c]
+    place_t[...] = place_ref[...].T
+    spread.tick(1)
+    loop(n - 1, lambda i: places(lax.rem(c + 1 + i, n)))
     mp.ag_end()
     mp.rs_end()
     spread.ticks(2)
     spread.finish()
 
 
-def mid_forward(n, part, x_mine, gain, own, below, above, chunks=2):
-    _, share, width = part.shape
+def mid_forward(n, ex, slots, part, gain, own, above, routes_line, tokens, chunks=2):
+    k, share, width = part.shape
+    tok = k * share
+    sds = jax.ShapeDtypeStruct
     return pl.pallas_call(
-        functools.partial(mid_forward_kernel, chunks, n),
+        functools.partial(mid_forward_kernel, chunks, n, ex),
         out_shape=(
-            jax.ShapeDtypeStruct((share, width), F32),
-            jax.ShapeDtypeStruct(part.shape, BF16),
-            jax.ShapeDtypeStruct((n,) + own.shape, BF16),
+            sds((share, width), F32),
+            sds(part.shape, BF16),
+            sds((ex * slots, tok), BF16),
+            sds((tok, ex * slots), BF16),
+            sds((n, ex * slots, tok), BF16),
+            sds((n,) + own.shape, BF16),
         ),
-        in_specs=[VMEM] * 6,
-        out_specs=(VMEM,) * 3,
-        scratch_shapes=mp_scratch(share, width, chunks) + [DMA((n,)), DMA((n,)), DMA((3,))],
-        compiler_params=params(2, 30),
+        in_specs=[VMEM] * 5 + [HBM],
+        out_specs=(VMEM,) * 5 + (HBM,),
+        scratch_shapes=mp_scratch(share, width, chunks)
+        + [DMA((n,)), DMA((n,)), DMA((3,)), pltpu.VMEM((share, width), BF16), DMA((1,)), pltpu.VMEM((8, tok), F32)],
+        compiler_params=params(2, 58),
         name="mid_forward",
         cost_estimate=cost(30),
-    )(part, x_mine, gain, own, below, above)
+    )(part, gain, own, above, routes_line, tokens)
 
 
 def mid_back_kernel(
@@ -1252,8 +1362,7 @@
     dg_ref,
     dresid_ref,
     db_ref,
-    dlog_ref,
-    gnorm_ref,
+    small_ref,
     rows_line,
     hid_line,
     below_ref,
@@ -1266,7 +1375,6 @@
     sems,
     side,
     peers_sem,
-    local,
     swap_sem,
 ):
     c = lax.axis_index("ctx")
@@ -1275,14 +1383,16 @@
     hid_peers = Peers(n, lambda p: hid_ref.at[p], lambda i: hid_line.at[i], peers_sem.at[2], peers_sem.at[3])
     beside = Neighbours(n, du_ref, below_ref, above_ref, side.at[0], side.at[1])
     width = gain.shape[1]
-    ex = gate_ref.shape[1]
+    ex = router_ref.shape[0]
+    lanes = gate_ref.shape[2]
     sem = pltpu.get_barrier_semaphore()
     mp.signal(sem)
     rows_peers.signal(sem)
     partner = swap_partner()
     pl.semaphore_signal(sem, inc=1, device_id=partner, device_id_type=MESH)
     pl.semaphore_wait(sem, 2 + n - 1 + 1)
-    mp.rs_begin()
+    mp.rs_core(0).start()
+    mp.rs_core(1).start()
     half_width = width // 2
     theirs = pl.ds(pl.multiple_of((1 - lax.axis_index("seq")) * half_width, 128), half_width)
     swaps = [
@@ -1295,31 +1405,30 @@
     beside.start_down()
     rows_peers.start()
     hid_peers.start()
-    own_rows = pltpu.make_async_copy(rows_ref, rows_line.at[c], local.at[0])
-    own_hid = pltpu.make_async_copy(hid_ref.at[c], hid_line.at[c], local.at[1])
-    own_rows.start()
-    own_hid.start()
-    gnorm_ref[...] = jnp.zeros_like(gnorm_ref)
+    mp.rs_forward()
+    rows_line[c] = rows_ref[...]
+    small_ref[...] = jnp.zeros_like(small_ref)
     for i in range(chunks):
         cut = mp.cut(i)
         both = mp.rs_chunk(i)
-        dgate = both[:, width : width + ex] + both[:, width + ex :]
-        gate = gate_ref[cut, :]
+        dgate = both[:, width : width + ex] + both[:, width + lanes // 2 : width + lanes // 2 + ex]
+        gate = gate_ref[mp.m, cut, :ex]
         dlog = gate * (dgate - jnp.sum(gate * dgate, axis=-1, keepdims=True))
-        dlog_ref[cut, :] = dlog
         dh = both[:, :width] + jnp.dot(
             dlog, router_ref[...], precision=lax.Precision.HIGHEST, preferred_element_type=F32
         )
         normed, inverse = rms_parts(resid_ref[cut, :])
-        gnorm_ref[0:1, :] = gnorm_ref[0:1, :] + jnp.sum(dh * normed, axis=0, keepdims=True)
+        small_ref[1:2, :] = small_ref[1:2, :] + jnp.sum(dh * normed, axis=0, keepdims=True)
+        h_two = (normed * gain[...]).astype(BF16).astype(F32)
+        small_ref[8 : 8 + ex, :] = small_ref[8 : 8 + ex, :] + lax.dot_general(
+            dlog, h_two, (((0,), (0,)), ((), ())), precision=lax.Precision.HIGHEST, preferred_element_type=F32
+        )
         dresid = cot[cut, :].astype(F32) + rms_grad(dh * gain[...], normed, inverse)
         dresid_ref[cut, :] = dresid
         db_ref[mp.m, cut, :] = dresid.astype(BF16)
         mp.ag_send(i)
     mp.ag_end()
     mp.rs_end()
-    own_rows.wait()
-    own_hid.wait()
     rows_peers.finish()
     hid_peers.finish()
     beside.finish()
@@ -1350,8 +1459,7 @@
         out_shape=(
             jax.ShapeDtypeStruct((share, width), F32),
             jax.ShapeDtypeStruct((k, share, width), BF16),
-            jax.ShapeDtypeStruct(gate.shape, F32),
-            jax.ShapeDtypeStruct((8, width), F32),
+            jax.ShapeDtypeStruct((8 + router_t.shape[0], width), F32),
             jax.ShapeDtypeStruct((n,) + rows.shape, F32),
             jax.ShapeDtypeStruct(hid.shape, BF16),
             jax.ShapeDtypeStruct(du.shape, BF16),
@@ -1359,10 +1467,10 @@
             jax.ShapeDtypeStruct(arr.shape[:2] + (arr.shape[2] // 2,), BF16),
             jax.ShapeDtypeStruct(dg.shape, BF16),
         ),
-        in_specs=[VMEM] * 11,
-        out_specs=(VMEM,) * 10,
-        scratch_shapes=mp_scratch(share, wide, chunks) + [DMA((2, 2)), DMA((4, n)), DMA((2,)), DMA((2, 2))],
-        compiler_params=params(3, 40),
+        in_specs=[VMEM] * 7 + [HBM] * 4,
+        out_specs=(VMEM,) * 4 + (HBM,) * 5,
+        scratch_shapes=mp_scratch(share, wide, chunks) + [DMA((2, 2)), DMA((4, n)), DMA((2, 2))],
+        compiler_params=params(3, 60),
         name="mid_back",
         cost_estimate=cost(32),
     )(part, resid, gain, cot, gate, router_t, rows, hid, du, arr, dg)
@@ -1414,32 +1522,86 @@
 def last_kernel(
     chunks,
     sizes,
-    part,
-    x_ref,
+    dqkv_ref,
+    h_hbm,
+    wq_hbm,
+    wk_hbm,
+    wv_hbm,
+    tok_hbm,
     gain,
-    dresid_ref,
+    dresid_hbm,
     small_ref,
     wout_ref,
-    qkv_ref,
+    gate0_hbm,
+    parts_ref,
+    down0_hbm,
+    down_other,
+    up0_hbm,
+    up_other,
+    comb_hbm,
+    resid_hbm,
     out_ref,
+    final_ref,
     total_ref,
     gout_ref,
     gqkv_ref,
+    gate_ref,
+    down_ref,
+    up_ref,
     core_in,
     y_out,
     y_in,
     sems,
+    core_in2,
+    y_out2,
+    y_in2,
+    sems2,
+    h_ref,
+    wq_ref,
+    wk_ref,
+    wv_ref,
+    tok_ref,
+    dresid_ref,
+    comb,
+    resid_ref,
+    part,
+    dh_ref,
+    qkv_ref,
     swapped,
     summed,
     wout_in,
     qkv_in,
+    down_in,
+    up_in,
+    from_below,
+    from_above,
+    load_sem,
     swap_sem,
     peers_sem,
+    sum_sem,
     *rest,
 ):
     n = sizes[1]
     s, c = lax.axis_index("seq"), lax.axis_index("ctx")
+    load = Staged(
+        (
+            (h_hbm, h_ref),
+            (wq_hbm, wq_ref),
+            (wk_hbm, wk_ref),
+            (wv_hbm, wv_ref),
+            (tok_hbm, tok_ref),
+            (comb_hbm, comb),
+            (dresid_hbm, dresid_ref),
+            (resid_hbm, resid_ref),
+            (gate0_hbm, gate_ref.at[0]),
+            (down0_hbm, down_ref),
+            (up0_hbm, up_ref),
+        ),
+        load_sem,
+    )
+    load.start()
     mp = Mp(part, core_in, y_out, y_in, None, sems, chunks)
+    mp2 = Mp(comb, core_in2, y_out2, y_in2, None, sems2, chunks)
     small = SmallSum(sizes, small_ref, total_ref, rest[:3], rest[3])
     half_rows = swapped.shape[0]
     rows = half_rows // n
@@ -1449,24 +1611,78 @@
     qkv_peers = Peers(
         n, lambda p: summed.at[cut_of(p, rows)], lambda i: qkv_in.at[i], peers_sem.at[2], peers_sem.at[3]
     )
+    ex = gate_ref.shape[0]
+    lines = [
+        LineSum(n, parts_ref.at[e], from_below.at[e], from_above.at[e], sum_sem.at[e, 0], sum_sem.at[e, 1])
+        for e in range(ex - 1)
+    ]
     sem = pltpu.get_barrier_semaphore()
     pl.semaphore_wait(sem, small.signal(sem))
+    for line in lines:
+        line.first(0)
+    wout_peers.start()
+    load.wait(0)
+
+    def weight_rows(first):
+        def piece(r):
+            at = pl.ds(pl.multiple_of(first + r * 256, 256), 256)
+            qkv_ref[at, :] = tn(h_ref[:, at], dqkv_ref[...]).astype(BF16)
+
+        loop(half_rows // 256, piece)
+
+    weight_rows((1 - s) * half_rows)
     qkv_swap = swap(qkv_ref.at[cut_of(1 - s, half_rows)], swapped, swap_sem, 0)
     qkv_swap.start()
+    load.wait(1, 2, 3)
+    share, width = out_ref.shape
+    qw, kw = wq_ref.shape[1], wk_ref.shape[1]
+
+    def token_rows(i):
+        at = pl.ds(pl.multiple_of(i * 512, 512), 512)
+        dh = nt(dqkv_ref[:, :qw], wq_ref[at, :])
+        dh = dh + nt(dqkv_ref[:, qw : qw + kw], wk_ref[at, :])
+        dh = dh + nt(dqkv_ref[:, qw + kw :], wv_ref[at, :])
+        for p in range(part.shape[0]):
+            dh_ref[p, :, at] = dh[p * share : (p + 1) * share, :]
+            part[p, :, at] = dh[p * share : (p + 1) * share, :].astype(BF16)
+
+    loop(width // 512, token_rows)
     mp.rs_core(0).start()
     mp.rs_core(1).start()
-    small.begin(2, small_ref[...])
-    wout_peers.start()
+    load.wait(5)
+    mp2.rs_core(0).start()
+    mp2.rs_core(1).start()
+    weight_rows(s * half_rows)
     mp.rs_forward()
+    load.wait(4)
+    total_ref[...] = small_ref[...]
+
+    def norm_rows(p):
+        normed, _ = rms_parts(tok_ref[p].astype(F32))
+        total_ref[0:1, :] = total_ref[0:1, :] + jnp.sum(dh_ref[p] * normed, axis=0, keepdims=True)
+
+    loop(part.shape[0], norm_rows)
+    small.begin(2, total_ref[...])
+    for line in lines:
+        line.tick(0)
+    mp2.rs_forward()
     small.begin(0, small.end(2))
+    load.wait(6)
     for i in range(chunks):
         cut = mp.cut(i)
-        if i == 1:
-            small.begin(1, small.end(0))
         dh = mp.rs_chunk(i)
-        normed, inverse = rms_parts(x_ref[cut, :].astype(F32))
-        out_ref[cut, :] = dresid_ref[cut, :] + rms_grad(dh * gain[...], normed, inverse)
+        normed, inverse = rms_parts(tok_ref[mp.m, cut, :].astype(F32))
+        final_ref[cut, :] = dresid_ref[cut, :] + rms_grad(dh * gain[...], normed, inverse)
+        for line in lines:
+            line.tick(1 + i)
+    for line in lines:
+        loop(max(2 * n - 4 - chunks, 0), lambda i: line.tick(i + 1 + chunks))
+    small.begin(1, small.end(0))
     qkv_swap.wait()
+    down_swap = swap(down_other, down_in, swap_sem, 1)
+    up_swap = swap(up_other, up_in, swap_sem, 2)
+    down_swap.start()
+    up_swap.start()
 
     def add(i):
         here = cut_of(i, rows)
@@ -1476,6 +1692,10 @@
 
     loop(n, add)
     qkv_peers.start()
+    load.wait(7)
+    for i in range(chunks):
+        cut = mp.cut(i)
+        out_ref[cut, :] = resid_ref[cut, :] + mp2.rs_chunk(i)
     total_ref[...] = small.end(1)
     wout_peers.finish()
     wout_in[c] = wout_ref[cut_of(c, rows), :]
@@ -1484,45 +1704,74 @@
         total = total + wout_in[i].astype(F32)
     gout_ref[...] = total
     mp.rs_end()
+    mp2.rs_end()
+    load.wait(8, 9, 10)
+    for e in range(1, ex):
+        lines[e - 1].finish(gate_ref.at[e])
+    down_swap.wait()
+    down_ref[...] = down_ref[...] + down_in[...].astype(F32)
     qkv_peers.finish()
     qkv_in[c] = summed[cut_of(c, rows), :]
     total = jnp.zeros(gqkv_ref.shape, F32)
     for i in range(n):
         total = total + qkv_in[i].astype(F32)
     gqkv_ref[...] = total
+    up_swap.wait()
+    up_ref[...] = up_ref[...] + up_in[...].astype(F32)
 
 
 def cut_of(i, rows):
     return pl.ds(pl.multiple_of(i * rows, 16), rows)
 
 
-def last(sizes, part, x_mine, gain, dresid, small, wout, qkv, chunks=2):
-    _, share, width = part.shape
+def last(sizes, dqkv, h, wq, wk, wv, tokens, gain, dresid, small, wout, gate0, parts, down0, down_other, up0, up_other, comb, resid, chunks=2):
+    k, share, width = comb.shape
     n = sizes[1]
     half_rows, fo = wout.shape
-    fq = qkv.shape[1]
+    fq = dqkv.shape[1]
     rows = half_rows // n
     sds = jax.ShapeDtypeStruct
+    vm = lambda x: pltpu.VMEM(x.shape, x.dtype)
     return pl.pallas_call(
         functools.partial(last_kernel, chunks, sizes),
-        out_shape=(sds((share, width), F32), sds(small.shape, F32), sds((rows, fo), F32), sds((rows, fq), F32)),
-        in_specs=[VMEM] * 7,
-        out_specs=(VMEM,) * 4,
+        out_shape=(
+            sds((share, width), F32),
+            sds((share, width), F32),
+            sds(small.shape, F32),
+            sds((rows, fo), F32),
+            sds((rows, fq), F32),
+            sds((parts.shape[0] + 1,) + gate0.shape, F32),
+            sds(down0.shape, F32),
+            sds(up0.shape, F32),
+        ),
+        in_specs=[VMEM] + [HBM] * 5 + [VMEM, HBM, VMEM, VMEM, HBM, VMEM, HBM, VMEM, HBM, VMEM, HBM, HBM],
+        out_specs=(VMEM,) * 8,
         scratch_shapes=mp_scratch(share, width, chunks)
+        + mp_scratch(share, width, chunks)
+        + [vm(h), vm(wq), vm(wk), vm(wv), vm(tokens), vm(dresid), vm(comb), vm(resid)]
         + [
+            pltpu.VMEM(comb.shape, BF16),
+            pltpu.VMEM(comb.shape, F32),
+            pltpu.VMEM((2 * half_rows, fq), BF16),
             pltpu.VMEM((half_rows, fq), BF16),
             pltpu.VMEM((half_rows, fq), BF16),
             pltpu.VMEM((n, rows, fo), BF16),
             pltpu.VMEM((n, rows, fq), BF16),
-            DMA((2, 1)),
+            pltpu.VMEM(down0.shape, BF16),
+            pltpu.VMEM(up0.shape, BF16),
+            pltpu.VMEM((parts.shape[0], n) + gate0.shape, BF16),
+            pltpu.VMEM((parts.shape[0], n) + gate0.shape, BF16),
+            DMA((11,)),
+            DMA((2, 3)),
             DMA((4, n)),
+            DMA((parts.shape[0], 2, 2, n)),
         ]
-        + [pltpu.VMEM((k,) + small.shape, F32) for k in sizes]
+        + [pltpu.VMEM((d,) + small.shape, F32) for d in sizes]
         + [DMA((2, sum(sizes)))],
-        compiler_params=params(4, 24),
+        compiler_params=params(4, 60),
         name="last",
-        cost_estimate=cost(45),
-    )(part, x_mine, gain, dresid, small, wout, qkv)
+        cost_estimate=cost(60),
+    )(dqkv, h, wq, wk, wv, tokens, gain, dresid, small, wout, gate0, parts, down0, down_other, up0, up_other, comb, resid)
 
 
 def half(x, s, dim):
@@ -1561,76 +1810,45 @@
     gain2 = norm2_gain.reshape(1, width)
 
     cot_all = lax.all_gather(cotangent, "mp", axis=0, tiled=True)
-    x_mine = lax.dynamic_slice_in_dim(tokens, m * share, share, 0)
+    by_share = tokens.reshape(n_mp, share, width)
 
     normed_one, _ = rms_parts(tokens.astype(F32))
     h_one = (normed_one * gain1).astype(BF16)
     qt = (jnp.einsum("df,td->ft", w_query, h_one, preferred_element_type=F32).astype(BF16)) * BF16(0.125)
     k = nn(h_one, key_weight_matrix).astype(BF16)
     v = nn(h_one, value_weight_matrix).astype(BF16)
-    o, heads_t, lse, kv, cot_below, cot_above, routes_line = attend(n_ctx, qt, k, v, cotangent, routes.T)
-
-    experts = jnp.arange(experts_all, dtype=jnp.int32)
-    first = m * exp_local
-    local = first + jnp.arange(exp_local, dtype=jnp.int32)
-    chosen_line = (routes_line[:, None, :, :] == local[None, :, None, None]).any(axis=2)
-    low = (jnp.arange(tok)[:, None] <= jnp.arange(tok)[None, :]).astype(BF16)
-    rank_line = (
-        jnp.einsum("cet,tu->ceu", chosen_line.astype(BF16), low, preferred_element_type=F32) - 1.0
-    ).astype(jnp.int32)
-    place_line = (
-        (rank_line[:, :, None, :] == jnp.arange(slots, dtype=jnp.int32)[None, None, :, None])
-        & chosen_line[:, :, None, :]
-    ).astype(BF16)
-    chosen = (routes[:, :, None] == experts[None, None, :]).any(axis=1)
-    place_line = place_line.reshape(n_ctx, exp_local * slots, tok)
-    place = lax.dynamic_index_in_dim(place_line, c, 0, keepdims=False)
-    place_t = place.T
-    lanes = 128
-    chosen_pad = jnp.pad(chosen.astype(F32), ((0, 0), (0, lanes - experts_all)))
-    r_hi = router.astype(BF16)
-    r_rest = router - r_hi.astype(F32)
-    r_mid = r_rest.astype(BF16)
-    r_low = (r_rest - r_mid.astype(F32)).astype(BF16)
-    router3 = jnp.pad(jnp.concatenate([r_hi, r_mid, r_low], axis=1), ((0, 0), (0, lanes - 3 * experts_all)))
-    router_t = jnp.pad(router.T, ((0, lanes // 2 - experts_all), (0, 0)))
-
+    o, heads_t, lse, kv, cot_above, routes_line = attend(n_ctx, qt, k, v, cotangent, routes.T)
     part = jnp.einsum("ft,fd->td", heads_t, w_out, preferred_element_type=F32).astype(BF16)
-    resid, h_two, cot_line = mid_forward(
-        n_ctx, part.reshape(n_mp, share, width), x_mine, gain2, cotangent, cot_below, cot_above
+    resid, h_two, place, place_t, place_line, cot_line = mid_forward(
+        n_ctx, exp_local, slots, part.reshape(n_mp, share, width), gain2, cotangent, cot_above, routes_line, by_share
     )
     h_two = h_two.reshape(tok, width)
 
-    gates, gate_rows, arrived, hidden, dg, du, back, comb, arrived_line, cot_first = moe(
-        n_ctx, n_seq, experts_all, h_two, cot_all, place, place_t, chosen_pad, router3, w_gate, w_up, w_down, cot_line
+    gates, gate_rows, arrived, hidden, dg, du, back, comb, arrived_line, cot_first, cot_line = moe(
+        n_ctx, n_seq, experts_all, h_two, cot_all, place, place_t, routes, router, w_gate, w_up, w_down, cot_line
     )
-    output = resid + lax.psum_scatter(comb, "mp", scatter_dimension=0, tiled=True).astype(F32)
-    gates_mine = lax.dynamic_slice_in_dim(gates, m * share, share, 0)[:, : lanes // 2]
-    dresid, db, dlog, gnorm2, gate_rows_line, hidden_line, du_below, du_above, arrived_other, dg_other = mid_back(
+    dresid, db, small, gate_rows_line, hidden_line, du_below, du_above, arrived_other, dg_other = mid_back(
         n_ctx,
         back.reshape(n_mp, share, -1),
         resid,
         gain2,
         cotangent,
-        gates_mine,
-        router_t,
+        gates.reshape(n_mp, share, -1),
+        router.T,
         gate_rows,
         hidden,
         du,
         arrived,
         dg,
     )
+
     db = db.reshape(tok, width)
-    h_two_mine = lax.dynamic_slice_in_dim(h_two, m * share, share, 0).astype(F32)
-    g_router = jnp.einsum("te,td->ed", dlog[:, :experts_all], h_two_mine, precision=lax.Precision.HIGHEST)
     g_out = jnp.einsum("td,ft->df", db, heads_t, preferred_element_type=F32).astype(BF16)
     g_out = (
         half(g_out, s, 0).astype(F32) + lax.ppermute(half(g_out, 1 - s, 0), "seq", SWAP).astype(F32)
     ).astype(BF16)
-
-    dq, dkv, g_gate, g_up, g_down, _, _ = attend_back(
+    dqkv, gate0, gate_parts, down0, down_other, up0, up_other, _, _ = attend_back(
         n_ctx,
-        n_seq,
         qt,
         db,
         w_out,
@@ -1641,31 +1859,39 @@
         arrived_other,
         dg,
         dg_other,
+        gate_rows_line,
         du,
         du_below,
         du_above,
-        gate_rows_line,
         hidden_line,
+        hidden,
         arrived_line,
         place_line,
         cot_line,
         cot_first,
     )
-    kvw = dkv.shape[1] // 2
-    dk, dv = dkv[:, :kvw], dkv[:, kvw:]
-    g_q = jnp.einsum("td,ft->df", h_one, dq, preferred_element_type=F32)
-    g_kv = jnp.einsum("td,tf->df", h_one, dkv, preferred_element_type=F32)
-    g_qkv = jnp.concatenate([g_q, g_kv], axis=1).astype(BF16)
-    dh = jnp.einsum("ft,df->td", dq, w_query, preferred_element_type=F32)
-    dh = dh + jnp.einsum("tf,df->td", dk, key_weight_matrix, preferred_element_type=F32)
-    dh = dh + jnp.einsum("tf,df->td", dv, value_weight_matrix, preferred_element_type=F32)
-    gnorm1 = jnp.sum(dh * normed_one, axis=0, keepdims=True)
-    rows = 2 + experts_all
-    small = jnp.concatenate([gnorm1, gnorm2[:1], g_router, jnp.zeros((-rows % 8, width), F32)], axis=0)
-    grad_tokens, small, g_out, g_qkv = last(
-        (n_seq, n_ctx, n_mp), dh.astype(BF16).reshape(n_mp, share, width), x_mine, gain1, dresid, small, g_out, g_qkv
+    output, grad_tokens, small, g_out, g_qkv, g_gate, g_down, g_up = last(
+        (n_seq, n_ctx, n_mp),
+        dqkv,
+        h_one,
+        w_query,
+        key_weight_matrix,
+        value_weight_matrix,
+        by_share,
+        gain1,
+        dresid,
+        small,
+        g_out,
+        gate0,
+        gate_parts,
+        down0,
+        down_other,
+        up0,
+        up_other,
+        comb.reshape(n_mp, share, width),
+        resid,
     )
-    qw = w_query.shape[1]
+    qw, kvw = w_query.shape[1], key_weight_matrix.shape[1]
     return (
         output,
         grad_tokens,
@@ -1675,7 +1901,7 @@
         g_qkv[:, qw + kvw :],
         g_out.T,
         small[1],
-        small[2:rows].T,
+        small[8 : 8 + experts_all].T,
         g_gate,
         g_up,
         g_down,

time: 414 us -> 363 us (0.88)
  Pallas kernels: 335 us -> 308 us
  local copies, waits for them, and re-layouts: 30 us -> 20.6 us
  matrix products: 15.9 us -> 11 us
  waiting for transfers between devices: 5.33 us -> 0.7 us
  other arithmetic: 7.84 us -> 3.63 us
    pallas_call x2, Pallas kernels: 145 us -> 118 us  [the longest x1 80.1 us: attend_back(): pl.pallas_call(functools.partial(attend_back_kernel, n), out_shape=(sds((...]
    pallas_call x1, Pallas kernels: 56.7 us -> 78.4 us  [last(): pl.pallas_call(functools.partial(last_kernel, chunks, sizes), out_shape=(...]
    pallas_call x1, Pallas kernels: 38.7 us -> 27.5 us  [attend(): pl.pallas_call(functools.partial(attend_kernel, n), out_shape=(jax.ShapeD...]
    dot_general x7 -> x0, matrix products: 8.52 us -> none  [the longest x1 1.87 us: body(): jnp.einsum('tf,df->td', dk, key_weight_matrix, preferred_element_type=F32)]
    pallas_call x1, Pallas kernels: 48.3 us -> 39.9 us  [moe(): pl.pallas_call(functools.partial(moe_kernel, n, n_seq, experts_all), out_...]
    unnamed x103 -> x34, local copies, waits for them, and re-layouts: 19 us -> 12.3 us
    ppermute x1, waiting for transfers between devices: 4.63 us -> 0.01 us  [body(): lax.ppermute(half(g_out, 1 - s, 0), 'seq', SWAP).astype(F32)]
  transfers between devices with their start and end apart: 3 -> 2, of which waited for: 1 -> 0; matrix products, arithmetic and copies ran while one was open for 8% -> 5% of each run, Pallas kernels for 70% -> 40%
where the time goes in v4:
time: 363 us; the launch traced here: 360 us
  Pallas kernels  308 us (85%)
  local copies, waits for them, and re-layouts  20.6 us (6%)
  between operations  14.2 us (4%)
  matrix products  11 us (3%)
  other arithmetic  3.63 us (1%)
    pallas_call x1, Pallas kernels, attend_back(): pl.pallas_call(functools.partial(attend_back_kernel, n), out_shape=(sds((...  80.1 us
    pallas_call x1, Pallas kernels, last(): pl.pallas_call(functools.partial(last_kernel, chunks, sizes), out_shape=(...  78.4 us
    pallas_call x1, Pallas kernels, mid_back(): pl.pallas_call(functools.partial(mid_back_kernel, chunks, n), out_shape=(...  44.1 us
    pallas_call x1, Pallas kernels, moe(): pl.pallas_call(functools.partial(moe_kernel, n, n_seq, experts_all), out_...  39.9 us
    pallas_call x1, Pallas kernels, mid_forward(): pl.pallas_call(functools.partial(mid_forward_kernel, chunks, n, ex), out_...  38 us
    pallas_call x1, Pallas kernels, attend(): pl.pallas_call(functools.partial(attend_kernel, n), out_shape=(jax.ShapeD...  27.5 us
    unnamed x34, local copies, waits for them, and re-layouts  12.3 us
  transfers between devices with their start and end apart: 2, of which 0 were waited for; matrix products, arithmetic and copies ran while one was open for 5% of the time, Pallas kernels for 40%

profile of v4, /device:TPU:16, one launch (start us, length us, event | category | flops | bytes accessed | tf_op | source)
XLA Modules:
  0.0 359.9 jit_solution(547662337713061084)
XLA Ops:
  7.9 1.3 reshape.61.gain
  9.2 1.6 copy.27.routes_ref
  10.8 1.9 copy.28.router_ref
  12.8 2.1 fusion
  15.9 1.3 convolution_convert_fusion.4.k_ref
  17.3 1.3 convolution_convert_fusion.3.v_ref
  18.6 1.9 fusion.4.q_ref
  20.6 27.5 %attend.1 = (f32[384,640]{1,0:T(8,128)}, bf16[384,640]{1,0:T(8,128)(2,1)}, f32[6,1,640]{2,1,0:T(1,128)}, bf16[4,640,256]{2,1,0:T(8,128)(2,1)}, bf16[160,1536]{1,0:T(8,128)(2,1)}, /*index=5*/s32[4,2,640]{2,1,0:T(2,128)}) custom-call(bf16[384,640]{1,0:T(8,128)(2,1)} %fusion.4.q_ref, bf16[640,128]{1,0:T(8,128)(2,1)} %convolution_convert_fusion.4.k_ref, ...), custom_call_target="tpu_custom_call" | custom-call | bytes 108000000 | tf_op jit(solution)/shard_map/attend/pallas_call | solution.py:506
  48.1 3.5 convolution_convert_fusion
  51.6 38.0 %mid_forward.1 = (f32[160,1536]{1,0:T(8,128)}, bf16[4,160,1536]{2,1,0:T(8,128)(2,1)}, bf16[416,640]{1,0:T(8,128)(2,1)}, bf16[640,416]{1,0:T(8,128)(2,1)}, bf16[4...) custom-call(bf16[4,160,1536]{2,1,0:T(8,128)(2,1)} %bitcast.28, f32[1,1536]{1,0:T(1,128)} %reshape.61.gain, ...), custom_call_target="tpu_custom_call" | custom-call | bytes 108000000 | tf_op jit(solution)/shard_map/mid_forward/pallas_call | solution.py:1329
  89.6 39.9 %moe.1 = (f32[640,128]{1,0:T(8,128)}, f32[8,256]{1,0:T(8,128)}, bf16[2,208,1536]{2,1,0:T(8,128)(2,1)}, bf16[4,2,208,256]{3,2,1,0:T(8,128)(2,1)}, bf16[2,208,1024...) custom-call(bf16[640,1536]{1,0:T(8,128)(2,1)} %bitcast.27, ...), custom_call_target="tpu_custom_call", output_to_operand_aliasing={{10}: (9, {})} | custom-call | bytes 108000000 | tf_op jit(solution)/shard_map/moe/pallas_call | solution.py:1100
  129.5 44.1 %mid_back.1 = (f32[160,1536]{1,0:T(8,128)}, bf16[4,160,1536]{2,1,0:T(8,128)(2,1)}, f32[16,1536]{1,0:T(8,128)}, f32[4,8,256]{2,1,0:T(8,128)}, bf16[4,2,208,256]{3...) custom-call(bf16[4,160,1664]{2,1,0:T(8,128)(2,1)} %bitcast.26, ...), custom_call_target="tpu_custom_call" | custom-call | bytes 115200000 | tf_op jit(solution)/shard_map/mid_back/pallas_call | solution.py:1457
  173.7 2.9 convolution_convert_fusion.1
  176.7 1.6 collective-permute-start
  178.8 80.1 %attend_back.1 = (bf16[640,640]{1,0:T(8,128)(2,1)}, f32[192,1024]{1,0:T(8,128)}, bf16[1,768,1024]{2,1,0:T(8,128)(2,1)}, f32[2,128,1536]{2,1,0:T(8,128)}, bf16[2,...) custom-call(bf16[384,640]{1,0:T(8,128)(2,1)} %fusion.4.q_ref, ...), custom_call_target="tpu_custom_call" | custom-call | bytes 216000000 | tf_op jit(solution)/shard_map/attend_back/pallas_call | solution.py:849
  259.9 78.4 %last.1 = (f32[160,1536]{1,0:T(8,128)}, f32[160,1536]{1,0:T(8,128)}, f32[16,1536]{1,0:T(8,128)}, f32[192,384]{1,0:T(8,128)}, f32[192,640]{1,0:T(8,128)}, /*index...) custom-call(bf16[640,640]{1,0:T(8,128)(2,1)} %get-tuple-element.88.dqkv_ref, ...), custom_call_target="tpu_custom_call" | custom-call | bytes 216000000 | tf_op jit(solution)/shard_map/last/pallas_call | solution.py:1735
  338.4 1.8 slice.19
  340.2 1.6 fusion.5
  341.8 1.5 slice_reduce_fusion
  343.3 1.4 slice_bitcast_fusion
  344.7 2.3 copy.37
  348.7 1.1 copy.40
  349.9 1.1 copy.41
  351.9 1.1 copy.42
  (37 shorter events, 5.9 us)
Async XLA Ops:
  7.2 7.7 %copy-start.11 = (f32[1536]{0:T(1024)S(1)}, f32[1536]{0:T(1024)}, u32[]{:S(2)}) copy-start(f32[1536]{0:T(1024)} %param.14) | copy-start | bytes 18436
  7.2 82.4 %all-gather.2.cloned.1.call-start = ((), (), s32[]{:S(2)}) async-start(), calls=%async_computation | async-start | bytes 2457600 | tf_op jit(solution)/shard_map/all_gather | solution.py:1812
  12.8 2.2 copy-start.1
  14.9 1.0 copy-start.5
  15.9 2.7 copy-start
  15.9 1.3 copy-start.6
  15.9 2.7 copy-start.8
  18.6 29.5 %copy-start.7 = (bf16[384,1536]{1,0:T(8,128)(2,1)S(1)}, bf16[384,1536]{1,0:T(8,128)(2,1)}, u32[]{:S(2)}) copy-start(bf16[384,1536]{1,0:T(8,128)(2,1)} %wout_ref.1) | copy-start | bytes 3538948
  129.5 44.1 %copy-start.12 = (bf16[384,640]{1,0:T(8,128)(2,1)S(1)}, bf16[384,640]{1,0:T(8,128)(2,1)}, u32[]{:S(2)}) copy-start(bf16[384,640]{1,0:T(8,128)(2,1)} %get-tuple-element.59) | copy-start | bytes 1474564
  176.7 82.3 %collective-permute-start = (bf16[768,384]{1,0:T(8,128)(2,1)S(1)}, bf16[768,384]{1,0:T(8,128)(2,1)S(1)}, u32[]{:S(2)}, u32[]{:S(2)}) collective-permute-start(bf16[768,384]{1,0:T(8,128)(2,1)S(1)} %constant_dynamic-slice_fusion), channel_id=1, source_target_pairs={{0,16},{16,0},{1,17},{17,1},{2,18},{18,2},{3,19},{19,3},{4,20},{20... | collective-permute-start | bytes 1769480 | tf_op jit(solution)/shard_map/ppermute | solution.py:1848
  338.4 8.7 %copy-start.9 = (f32[160,1536]{1,0:T(8,128)S(1)}, f32[160,1536]{1,0:T(8,128)}, u32[]{:S(2)}) copy-start(f32[160,1536]{1,0:T(8,128)} %get-tuple-element.123) | copy-start | bytes 2949124
  344.7 3.3 copy-start.10
  344.7 4.0 %copy-start.4 = (f32[2,192,1024]{2,1,0:T(8,128)S(1)}, f32[2,192,1024]{2,1,0:T(8,128)}, u32[]{:S(2)}) copy-start(f32[2,192,1024]{2,1,0:T(8,128)} %get-tuple-element.131) | copy-start | bytes 4718596
  348.0 1.9 copy-start.3
  349.9 2.0 copy-start.2
Sparse Core Ops, SparseCore 0:
  9.6 22.9 all-gather.1

commit v5 on v4

--- a/solution.py
+++ b/solution.py
@@ -202,71 +202,75 @@
     ahead = 2
 
     def __init__(self, n, parts, from_below, from_above, send, recv):
-        self.n, self.parts, self.from_below, self.from_above, self.send, self.recv = n, parts, from_below, from_above, send, recv
+        self.n, self.parts, self.bufs, self.send, self.recv = n, parts, (from_below, from_above), send, recv
         s, self.c, m = lax.axis_index("seq"), lax.axis_index("ctx"), lax.axis_index("mp")
         self.up, self.down = (s, lax.rem(self.c + 1, n), m), (s, lax.rem(self.c + n - 1, n), m)
-        self.rows = from_below.shape[1]
-
-    def own(self, k):
-        return self.parts.at[pl.ds(pl.multiple_of(k * self.rows, 16), self.rows), :]
-
-    def move(self, way, k, first=False):
-        there = (self.from_below if way == 0 else self.from_above).at[k]
+        self.ex, self.rows = from_below.shape[1], from_below.shape[2]
+        self.units = (n - 1) * self.ex
+        self.ticks = self.units + n - 3
+
+    def own(self, k, e):
+        return self.parts.at[e, pl.ds(pl.multiple_of(k * self.rows, 16), self.rows), :]
+
+    def move(self, way, k, e, first=False):
+        there = self.bufs[way].at[k, e]
         return pltpu.make_async_remote_copy(
-            src_ref=self.own(k) if first else there,
+            src_ref=self.own(k, e) if first else there,
             dst_ref=there,
-            send_sem=self.send.at[way, k],
-            recv_sem=self.recv.at[way, k],
+            send_sem=self.send.at[way, k, e],
+            recv_sem=self.recv.at[way, k, e],
             device_id=self.up if way == 0 else self.down,
             device_id_type=MESH,
         )
 
-    def chunk(self, way, u):
-        return self.n - 1 - u if way == 0 else u
+    def unit(self, way, u):
+        k = lax.div(u, self.ex)
+        return (self.n - 1 - k if way == 0 else k), lax.rem(u, self.ex)
 
     def first(self, u):
-        units = self.n - 1
         for way, end in ((0, 0), (1, self.n - 1)):
 
-            @pl.when(jnp.logical_and(self.c == end, u < units))
+            @pl.when(jnp.logical_and(self.c == end, u < self.units))
             def _():
                 @pl.when(u >= self.ahead)
                 def _():
-                    self.move(way, self.chunk(way, jnp.maximum(u - self.ahead, 0)), True).wait_send()
-
-                self.move(way, self.chunk(way, jnp.minimum(u, units - 1)), True).start()
+                    self.move(way, *self.unit(way, jnp.maximum(u - self.ahead, 0)), True).wait_send()
+
+                self.move(way, *self.unit(way, jnp.minimum(u, self.units - 1)), True).start()
 
     def tick(self, i):
         self.first(i + 1)
         for way, far in ((0, self.c), (1, self.n - 1 - self.c)):
             u = i - far
-            buf = self.from_below if way == 0 else self.from_above
-
-            @pl.when(jnp.logical_and(far > 0, jnp.logical_and(u >= 0, u < self.n - 1 - far)))
+
+            @pl.when(jnp.logical_and(far > 0, jnp.logical_and(u >= 0, u < (self.n - 1 - far) * self.ex)))
             def _():
-                k = self.chunk(way, jnp.clip(u, 0, self.n - 2))
-                self.move(way, k).wait_recv()
-                buf[k] = (self.own(k)[...].astype(F32) + buf[k].astype(F32)).astype(BF16)
-                self.move(way, k).start()
+                k, e = self.unit(way, jnp.clip(u, 0, self.units - 1))
+                self.move(way, k, e).wait_recv()
+                self.bufs[way][k, e] = (
+                    self.own(k, e)[...].astype(F32) + self.bufs[way][k, e].astype(F32)
+                ).astype(BF16)
+                self.move(way, k, e).start()
 
     def finish(self, out):
         c = self.c
-        out[...] = self.own(c)[...].astype(F32)
+        for e in range(self.ex):
+            out[e] = self.own(c, e)[...].astype(F32)
         for way, far in ((0, c), (1, self.n - 1 - c)):
-            buf = self.from_below if way == 0 else self.from_above
 
             @pl.when(far > 0)
             def _():
-                self.move(way, c).wait_recv()
-                out[...] = out[...] + buf[c].astype(F32)
-
-            done = jnp.where(far == 0, max(self.n - 1 - self.ahead, 0), 0)
+                for e in range(self.ex):
+                    self.move(way, c, e).wait_recv()
+                    out[e] = out[e] + self.bufs[way][c, e].astype(F32)
+
+            done = jnp.where(far == 0, max(self.units - self.ahead, 0), 0)
 
             def sent(u, carry):
-                self.move(way, self.chunk(way, u)).wait_send()
+                self.move(way, *self.unit(way, u)).wait_send()
                 return carry
 
-            lax.fori_loop(done, self.n - 1 - far, sent, 0)
+            lax.fori_loop(done, (self.n - 1 - far) * self.ex, sent, 0)
 
 
 class Peers:
@@ -549,17 +553,17 @@
     above_ref,
     hid_hbm,
     hid_own,
+    heads_ref,
     arr_hbm,
     place_hbm,
     line_hbm,
     first_hbm,
     dqkv_ref,
     gate_ref,
-    gate_parts,
     down_ref,
-    down_other,
     up_ref,
     up_other,
+    wsum_ref,
     all_hbm,
     rest_hbm,
     do_ref,
@@ -586,6 +590,11 @@
     local,
     ysem,
     load_sem,
+    swap_sem,
+    wout_part,
+    wout_in,
+    down_out,
+    down_in,
 ):
     s, c, m = lax.axis_index("seq"), lax.axis_index("ctx"), lax.axis_index("mp")
     _, t, kvw2 = kv_ref.shape
@@ -602,7 +611,8 @@
     sem = pltpu.get_barrier_semaphore()
     signal_line(n, sem)
     cots.signal(sem)
-    pl.semaphore_wait(sem, line_degree(n) + 2)
+    pl.semaphore_signal(sem, inc=1, device_id=swap_partner(), device_id_type=MESH)
+    pl.semaphore_wait(sem, line_degree(n) + 3)
     spread.start()
     cots.start()
 
@@ -614,19 +624,30 @@
 
         loop(half_width // 256, piece)
 
-    gate_part(0, sum_ref)
-    line.first(0)
+    for e in range(ex):
+        gate_part(e, sum_ref.at[e])
+        if e == 0:
+            line.first(0)
     do_ref[...] = nt(wout_ref[...], db_ref[...]).astype(BF16)
+
+    def wout_piece(r):
+        at = pl.ds(pl.multiple_of(r * 512, 512), 512)
+        wout_part[:, at] = nn(heads_ref[...], db_ref[:, at]).astype(BF16)
+
+    loop(width // 512, wout_piece)
+    own_half, other_half = (pl.ds(pl.multiple_of(k * half_width, 128), half_width) for k in (s, 1 - s))
+    wout_swap = swap(wout_part.at[:, other_half], wout_in, swap_sem, 0)
+    wout_swap.start()
 
     def tick(i):
         line.tick(i)
         for hop in range(1, n - 1):
 
-            @pl.when(i == 2 * hop)
+            @pl.when(i == 2 * hop - 1)
             def _():
                 spread.tick(hop)
 
-    ticks = 2 * (n - 2) + 1
+    ticks = max(line.ticks, 2 * (n - 2)) + 1
     pad_heads(q_ref, qpad, heads, group)
     pad_heads(do_ref, dopad, heads, group)
     for h in range(heads):
@@ -697,22 +718,11 @@
         return carry
 
     lax.fori_loop(0, c, step, 0)
-    block(c, True)
-
-    @pl.when(jnp.logical_and(c > 0, c < n - 1))
-    def _():
-        forward(c - 1)
-
-    qw = dq.shape[0]
-    dqkv_ref[:, :qw] = (dq[...] * 0.125).astype(BF16).T
-    for e in range(1, ex):
-        gate_part(e, gate_parts.at[e - 1])
-
     def later(i, carry):
         tick(i)
         return carry
 
-    middle = jnp.maximum(c, min(3, ticks))
+    middle = jnp.maximum(c, min(2, ticks))
     lax.fori_loop(c, middle, later, 0)
 
     cots.finish()
@@ -790,9 +800,23 @@
     loop(n, down_block)
     mine, other = (pl.ds(pl.multiple_of(k * (fa // 2), 16), fa // 2) for k in (s, 1 - s))
     down_ref[...] = acc_ref[:, mine, :]
-    down_other[...] = acc_ref[:, other, :].astype(BF16)
-
-    lax.fori_loop(middle, ticks, later, 0)
+    down_out[...] = acc_ref[:, other, :].astype(BF16)
+    wout_swap.wait()
+    down_swap = swap(down_out, down_in, swap_sem, 1)
+    down_swap.start()
+    wsum_ref[...] = (wout_part[:, own_half].astype(F32) + wout_in[...].astype(F32)).astype(BF16).T
+
+    after = jnp.minimum(middle + 1, ticks)
+    lax.fori_loop(middle, after, later, 0)
+    block(c, True)
+
+    @pl.when(jnp.logical_and(c > 0, c < n - 1))
+    def _():
+        forward(c - 1)
+
+    qw = dq.shape[0]
+    dqkv_ref[:, :qw] = (dq[...] * 0.125).astype(BF16).T
+    lax.fori_loop(after, ticks, later, 0)
 
     spread.finish()
     acc_ref[...] = jnp.zeros_like(acc_ref)
@@ -827,6 +851,8 @@
     acc = gathered(c)
     dqkv_ref[:, qw:] = acc[...].astype(BF16)
     line.finish(gate_ref)
+    down_swap.wait()
+    down_ref[...] = down_ref[...] + down_in[...].astype(F32)
 
     def sent_kv(j, carry):
         pass_down(j).wait_send()
@@ -835,14 +861,14 @@
     lax.fori_loop(0, c, sent_kv, 0)
 
 
-def attend_back(n, qt, db, w_out, o, lse, kv, arr, arr_other, dg, dg_other, rows, du, below, above, hid, hid_own, arr_line, place, line, first):
+def attend_back(n, qt, db, w_out, o, lse, kv, arr, arr_other, dg, dg_other, rows, du, below, above, hid, hid_own, heads_t, arr_line, place, line, first):
     qw, t = qt.shape
     heads = qw // HEAD_SIZE
     kvw = kv.shape[2] // 2
     ex, slots, width = arr.shape
     ff = dg.shape[2]
     half_width = width // 2
-    chunk = (half_width // n, ff)
+    chunk = (ex, half_width // n, ff)
     fa, ua = hid.shape[3], arr_line.shape[3]
     blocks = first.shape[0]
     sds = jax.ShapeDtypeStruct
@@ -851,16 +877,15 @@
         out_shape=(
             sds((t, qw + 2 * kvw), BF16),
             sds(chunk, F32),
-            sds((ex - 1, half_width, ff), BF16),
             sds((ex, fa // 2, width), F32),
-            sds((ex, fa // 2, width), BF16),
             sds((ex, ua // 2, ff), F32),
             sds((ex, ua // 2, ff), BF16),
+            sds((half_width, qw), BF16),
             sds((n,) + du.shape, BF16),
             sds((n - blocks,) + first.shape[1:], BF16),
         ),
-        in_specs=[VMEM] * 14 + [HBM] * 6,
-        out_specs=(VMEM,) * 7 + (HBM,) * 2,
+        in_specs=[VMEM] * 14 + [HBM] * 2 + [VMEM] + [HBM] * 4,
+        out_specs=(VMEM,) * 6 + (HBM,) * 2,
         scratch_shapes=[
             pltpu.VMEM((qw, t), BF16),
             pltpu.VMEM((heads, kvw, t), BF16),
@@ -870,7 +895,7 @@
             pltpu.VMEM((kvw, t), BF16),
             pltpu.VMEM((2, t, 2 * kvw), F32),
             pltpu.VMEM((n, t, 2 * kvw), BF16),
-            pltpu.VMEM((half_width, ff), BF16),
+            pltpu.VMEM((ex, half_width, ff), BF16),
             pltpu.VMEM((n,) + chunk, BF16),
             pltpu.VMEM((n,) + chunk, BF16),
             pltpu.VMEM((2,) + place.shape[1:], BF16),
@@ -881,16 +906,21 @@
             pltpu.VMEM((slots, width), BF16),
             pltpu.VMEM((ex, max(fa, ua), width), F32),
             DMA((2, n)),
-            DMA((2, 2, n)),
+            DMA((2, 2, n, ex)),
             DMA((2, n)),
             DMA((3,)),
             DMA((2, 3, n - blocks)),
             DMA((8, 2)),
+            DMA((2, 2)),
+            pltpu.VMEM((qw, width), BF16),
+            pltpu.VMEM((qw, half_width), BF16),
+            pltpu.VMEM((ex, fa // 2, width), BF16),
+            pltpu.VMEM((ex, fa // 2, width), BF16),
         ],
-        compiler_params=params(1, 60),
+        compiler_params=params(1, 62),
         name="attend_back",
         cost_estimate=cost(60),
-    )(qt, db, w_out, o, lse, kv, arr, arr_other, dg, dg_other, rows, du, below, above, hid, hid_own, arr_line, place, line, first)
+    )(qt, db, w_out, o, lse, kv, arr, arr_other, dg, dg_other, rows, du, below, above, hid, hid_own, heads_t, arr_line, place, line, first)
 
 
 def tn(a, b):
@@ -946,6 +976,7 @@
     local,
     far_sem,
     router3,
+    named,
 ):
     s, c, m = lax.axis_index("seq"), lax.axis_index("ctx"), lax.axis_index("mp")
     ex, width, ff = wg.shape
@@ -971,6 +1002,13 @@
             weights[i, e] = pltpu.make_async_copy(src.at[e], dst.at[e], wsem.at[i, e])
             weights[i, e].start()
 
+    pl.semaphore_wait(sem, n - 1 + 2)
+    cots.start()
+
+    @pl.when(c == n - 2)
+    def _():
+        far.start()
+
     def rows_of(e):
         return slice(e * slots, (e + 1) * slots)
 
@@ -985,14 +1023,7 @@
             for j in range(n_seq):
                 at = (j * n + i) * size
                 parts[i, e, :, j * size : (j + 1) * size] = arr_ref[e, :, at : at + size]
-    pl.semaphore_wait(sem, n - 1 + 2)
     peers.start()
-    cots.start()
-
-    @pl.when(c == n - 2)
-    def _():
-        far.start()
-
     own = pltpu.make_async_copy(parts.at[c], arr_line.at[c], local.at[0])
     own.start()
 
@@ -1000,14 +1031,19 @@
     left = router_ref[...]
     for i in range(3):
         piece = left.astype(BF16)
-        router3[:, i * experts_all : (i + 1) * experts_all] = piece
+        router3[i * experts_all : (i + 1) * experts_all, :] = piece
         left = left - piece.astype(F32)
-    three = nn(h_ref[...], router3[...])
+    three = nt(h_ref[...], router3[...])
     logits = three + pltpu.roll(three, lanes - experts_all, 1) + pltpu.roll(three, lanes - 2 * experts_all, 1)
     which = lax.broadcasted_iota(jnp.int32, three.shape, 1)
-    chosen = which == routes_ref[:, 0:1]
-    for k in range(1, routes_ref.shape[1]):
-        chosen = jnp.logical_or(chosen, which == routes_ref[:, k : k + 1])
+    top = routes_ref.shape[0]
+    named[...] = jnp.zeros_like(named)
+    named[:top, :] = routes_ref[...].astype(F32)
+    columns = named[...].T
+    which = which.astype(F32)
+    chosen = which == columns[:, 0:1]
+    for k in range(1, top):
+        chosen = jnp.logical_or(chosen, which == columns[:, k : k + 1])
     peak = jnp.max(jnp.where(chosen, logits, -1e30), axis=1, keepdims=True)
     raised = jnp.where(chosen, jnp.exp(jnp.where(chosen, logits - peak, 0.0)), 0.0)
     gates = raised / jnp.sum(raised, axis=1, keepdims=True)
@@ -1130,7 +1166,8 @@
             DMA((2, 3, blocks)),
             DMA((1,)),
             DMA((2,)),
-            pltpu.VMEM((width, 128), BF16),
+            pltpu.VMEM((128, width), BF16),
+            pltpu.VMEM((8, tok), F32),
         ],
         input_output_aliases={9: 10},
         compiler_params=params(6, 60),
@@ -1248,7 +1285,8 @@
     chunks,
     n,
     ex,
-    part,
+    heads_ref,
+    wout_ref,
     gain,
     own,
     above,
@@ -1270,6 +1308,7 @@
     x_ref,
     x_sem,
     ranks,
+    part,
 ):
     c = lax.axis_index("ctx")
     mp = Mp(part, core_in, y_out, y_in, h_ref, sems, chunks)
@@ -1279,6 +1318,15 @@
     sem = pltpu.get_barrier_semaphore()
     mp.signal(sem)
     signal_line(n, sem)
+    share, width = x_ref.shape
+
+    def outs(i):
+        at = pl.ds(pl.multiple_of(i * 512, 512), 512)
+        rows = tn(heads_ref[...], wout_ref[:, at]).astype(BF16)
+        for p in range(part.shape[0]):
+            part[p, :, at] = rows[p * share : (p + 1) * share, :]
+
+    loop(width // 512, outs)
     pl.semaphore_wait(sem, 2 + line_degree(n))
     mp.rs_core(0).start()
     mp.rs_core(1).start()
@@ -1303,17 +1351,17 @@
             one = jnp.where(rows == order[e : e + 1, :], 1.0, 0.0) * sel[e : e + 1, :]
             place_line[b, e * slots : (e + 1) * slots, :] = one.astype(BF16)
 
+    places(c)
+    place_ref[...] = place_line[c]
+    place_t[...] = place_ref[...].T
     x_copy.wait()
     for i in range(chunks):
         cut = mp.cut(i)
         resid = x_ref[cut, :].astype(F32) + mp.rs_chunk(i)
         resid_ref[cut, :] = resid
         normed, _ = rms_parts(resid)
-        h_ref[mp.m, cut, :] = (normed * gain[...]).astype(BF16)
+        h_ref[mp.m, cut, :] = (normed * gain[...].reshape(1, -1)).astype(BF16)
         mp.ag_send(i)
-    places(c)
-    place_ref[...] = place_line[c]
-    place_t[...] = place_ref[...].T
     spread.tick(1)
     loop(n - 1, lambda i: places(lax.rem(c + 1 + i, n)))
     mp.ag_end()
@@ -1322,28 +1370,29 @@
     spread.finish()
 
 
-def mid_forward(n, ex, slots, part, gain, own, above, routes_line, tokens, chunks=2):
-    k, share, width = part.shape
+def mid_forward(n, ex, slots, heads_t, w_out, gain, own, above, routes_line, tokens, chunks=2):
+    k, share, width = tokens.shape
     tok = k * share
     sds = jax.ShapeDtypeStruct
     return pl.pallas_call(
         functools.partial(mid_forward_kernel, chunks, n, ex),
         out_shape=(
             sds((share, width), F32),
-            sds(part.shape, BF16),
+            sds(tokens.shape, BF16),
             sds((ex * slots, tok), BF16),
             sds((tok, ex * slots), BF16),
             sds((n, ex * slots, tok), BF16),
             sds((n,) + own.shape, BF16),
         ),
-        in_specs=[VMEM] * 5 + [HBM],
+        in_specs=[VMEM] * 6 + [HBM],
         out_specs=(VMEM,) * 5 + (HBM,),
         scratch_shapes=mp_scratch(share, width, chunks)
-        + [DMA((n,)), DMA((n,)), DMA((3,)), pltpu.VMEM((share, width), BF16), DMA((1,)), pltpu.VMEM((8, tok), F32)],
+        + [DMA((n,)), DMA((n,)), DMA((3,)), pltpu.VMEM((share, width), BF16), DMA((1,)), pltpu.VMEM((8, tok), F32)]
+        + [pltpu.VMEM(tokens.shape, BF16)],
         compiler_params=params(2, 58),
         name="mid_forward",
         cost_estimate=cost(30),
-    )(part, gain, own, above, routes_line, tokens)
+    )(heads_t, w_out, gain, own, above, routes_line, tokens)
 
 
 def mid_back_kernel(
@@ -1382,7 +1431,7 @@
     rows_peers = Peers(n, lambda p: rows_ref, lambda i: rows_line.at[i], peers_sem.at[0], peers_sem.at[1])
     hid_peers = Peers(n, lambda p: hid_ref.at[p], lambda i: hid_line.at[i], peers_sem.at[2], peers_sem.at[3])
     beside = Neighbours(n, du_ref, below_ref, above_ref, side.at[0], side.at[1])
-    width = gain.shape[1]
+    width = gain.shape[0]
     ex = router_ref.shape[0]
     lanes = gate_ref.shape[2]
     sem = pltpu.get_barrier_semaphore()
@@ -1419,11 +1468,11 @@
         )
         normed, inverse = rms_parts(resid_ref[cut, :])
         small_ref[1:2, :] = small_ref[1:2, :] + jnp.sum(dh * normed, axis=0, keepdims=True)
-        h_two = (normed * gain[...]).astype(BF16).astype(F32)
+        h_two = (normed * gain[...].reshape(1, -1)).astype(BF16).astype(F32)
         small_ref[8 : 8 + ex, :] = small_ref[8 : 8 + ex, :] + lax.dot_general(
             dlog, h_two, (((0,), (0,)), ((), ())), precision=lax.Precision.HIGHEST, preferred_element_type=F32
         )
-        dresid = cot[cut, :].astype(F32) + rms_grad(dh * gain[...], normed, inverse)
+        dresid = cot[cut, :].astype(F32) + rms_grad(dh * gain[...].reshape(1, -1), normed, inverse)
         dresid_ref[cut, :] = dresid
         db_ref[mp.m, cut, :] = dresid.astype(BF16)
         mp.ag_send(i)
@@ -1453,7 +1502,7 @@
 
 def mid_back(n, part, resid, gain, cot, gate, router_t, rows, hid, du, arr, dg, chunks=2):
     k, share, wide = part.shape
-    width = gain.shape[1]
+    width = gain.shape[0]
     return pl.pallas_call(
         functools.partial(mid_back_kernel, chunks, n),
         out_shape=(
@@ -1532,10 +1581,6 @@
     dresid_hbm,
     small_ref,
     wout_ref,
-    gate0_hbm,
-    parts_ref,
-    down0_hbm,
-    down_other,
     up0_hbm,
     up_other,
     comb_hbm,
@@ -1545,8 +1590,6 @@
     total_ref,
     gout_ref,
     gqkv_ref,
-    gate_ref,
-    down_ref,
     up_ref,
     core_in,
     y_out,
@@ -1571,14 +1614,10 @@
     summed,
     wout_in,
     qkv_in,
-    down_in,
     up_in,
-    from_below,
-    from_above,
     load_sem,
     swap_sem,
     peers_sem,
-    sum_sem,
     *rest,
 ):
     n = sizes[1]
@@ -1593,8 +1632,6 @@
             (comb_hbm, comb),
             (dresid_hbm, dresid_ref),
             (resid_hbm, resid_ref),
-            (gate0_hbm, gate_ref.at[0]),
-            (down0_hbm, down_ref),
             (up0_hbm, up_ref),
         ),
         load_sem,
@@ -1611,15 +1648,8 @@
     qkv_peers = Peers(
         n, lambda p: summed.at[cut_of(p, rows)], lambda i: qkv_in.at[i], peers_sem.at[2], peers_sem.at[3]
     )
-    ex = gate_ref.shape[0]
-    lines = [
-        LineSum(n, parts_ref.at[e], from_below.at[e], from_above.at[e], sum_sem.at[e, 0], sum_sem.at[e, 1])
-        for e in range(ex - 1)
-    ]
     sem = pltpu.get_barrier_semaphore()
     pl.semaphore_wait(sem, small.signal(sem))
-    for line in lines:
-        line.first(0)
     wout_peers.start()
     load.wait(0)
 
@@ -1631,8 +1661,29 @@
         loop(half_rows // 256, piece)
 
     weight_rows((1 - s) * half_rows)
-    qkv_swap = swap(qkv_ref.at[cut_of(1 - s, half_rows)], swapped, swap_sem, 0)
-    qkv_swap.start()
+
+    def chunk_swap(k):
+        p = lax.rem(c + 1 + k, n)
+        return swap(qkv_ref.at[cut_of((1 - s) * n + p, rows)], swapped.at[cut_of(p, rows)], swap_sem, k)
+
+    up_swap = swap(up_other, up_in, swap_sem, n)
+
+    def chunk_arrived(k):
+        chunk_swap(k).wait_recv()
+        if k + 2 < n:
+            chunk_swap(k + 2).start()
+        if k + 2 == n:
+            up_swap.start()
+        p = lax.rem(c + 1 + k, n)
+        here = cut_of(p, rows)
+        summed[here, :] = (
+            qkv_ref[cut_of(s * n + p, rows), :].astype(F32) + swapped[here, :].astype(F32)
+        ).astype(BF16)
+        if k < n - 1:
+            qkv_peers.move(k + 1).start()
+
+    for k in range(min(2, n)):
+        chunk_swap(k).start()
     load.wait(1, 2, 3)
     share, width = out_ref.shape
     qw, kw = wq_ref.shape[1], wk_ref.shape[1]
@@ -1662,41 +1713,28 @@
         total_ref[0:1, :] = total_ref[0:1, :] + jnp.sum(dh_ref[p] * normed, axis=0, keepdims=True)
 
     loop(part.shape[0], norm_rows)
-    small.begin(2, total_ref[...])
-    for line in lines:
-        line.tick(0)
+    small.begin(1, total_ref[...])
+    chunk_arrived(0)
     mp2.rs_forward()
-    small.begin(0, small.end(2))
+    chunk_arrived(1)
     load.wait(6)
     for i in range(chunks):
         cut = mp.cut(i)
         dh = mp.rs_chunk(i)
         normed, inverse = rms_parts(tok_ref[mp.m, cut, :].astype(F32))
-        final_ref[cut, :] = dresid_ref[cut, :] + rms_grad(dh * gain[...], normed, inverse)
-        for line in lines:
-            line.tick(1 + i)
-    for line in lines:
-        loop(max(2 * n - 4 - chunks, 0), lambda i: line.tick(i + 1 + chunks))
-    small.begin(1, small.end(0))
-    qkv_swap.wait()
-    down_swap = swap(down_other, down_in, swap_sem, 1)
-    up_swap = swap(up_other, up_in, swap_sem, 2)
-    down_swap.start()
-    up_swap.start()
-
-    def add(i):
-        here = cut_of(i, rows)
-        summed[here, :] = (
-            qkv_ref[cut_of(s * n + i, rows), :].astype(F32) + swapped[here, :].astype(F32)
-        ).astype(BF16)
-
-    loop(n, add)
-    qkv_peers.start()
+        final_ref[cut, :] = dresid_ref[cut, :] + rms_grad(dh * gain[...].reshape(1, -1), normed, inverse)
+        if i + 2 < n:
+            chunk_arrived(i + 2)
+        if i == 0:
+            small.begin(0, small.end(1))
+    for k in range(chunks + 2, n):
+        chunk_arrived(k)
+    small.begin(2, small.end(0))
     load.wait(7)
     for i in range(chunks):
         cut = mp.cut(i)
         out_ref[cut, :] = resid_ref[cut, :] + mp2.rs_chunk(i)
-    total_ref[...] = small.end(1)
+    total_ref[...] = small.end(2)
     wout_peers.finish()
     wout_in[c] = wout_ref[cut_of(c, rows), :]
     total = jnp.zeros(gout_ref.shape, F32)
@@ -1705,11 +1743,9 @@
     gout_ref[...] = total
     mp.rs_end()
     mp2.rs_end()
-    load.wait(8, 9, 10)
-    for e in range(1, ex):
-        lines[e - 1].finish(gate_ref.at[e])
-    down_swap.wait()
-    down_ref[...] = down_ref[...] + down_in[...].astype(F32)
+    load.wait(8)
+    for k in range(n):
+        chunk_swap(k).wait_send()
     qkv_peers.finish()
     qkv_in[c] = summed[cut_of(c, rows), :]
     total = jnp.zeros(gqkv_ref.shape, F32)
@@ -1724,7 +1760,7 @@
     return pl.ds(pl.multiple_of(i * rows, 16), rows)
 
 
-def last(sizes, dqkv, h, wq, wk, wv, tokens, gain, dresid, small, wout, gate0, parts, down0, down_other, up0, up_other, comb, resid, chunks=2):
+def last(sizes, dqkv, h, wq, wk, wv, tokens, gain, dresid, small, wout, up0, up_other, comb, resid, chunks=2):
     k, share, width = comb.shape
     n = sizes[1]
     half_rows, fo = wout.shape
@@ -1740,12 +1776,10 @@
             sds(small.shape, F32),
             sds((rows, fo), F32),
             sds((rows, fq), F32),
-            sds((parts.shape[0] + 1,) + gate0.shape, F32),
-            sds(down0.shape, F32),
             sds(up0.shape, F32),
         ),
-        in_specs=[VMEM] + [HBM] * 5 + [VMEM, HBM, VMEM, VMEM, HBM, VMEM, HBM, VMEM, HBM, VMEM, HBM, HBM],
-        out_specs=(VMEM,) * 8,
+        in_specs=[VMEM] + [HBM] * 5 + [VMEM, HBM, VMEM, VMEM, HBM, VMEM, HBM, HBM],
+        out_specs=(VMEM,) * 6,
         scratch_shapes=mp_scratch(share, width, chunks)
         + mp_scratch(share, width, chunks)
         + [vm(h), vm(wq), vm(wk), vm(wv), vm(tokens), vm(dresid), vm(comb), vm(resid)]
@@ -1757,29 +1791,67 @@
             pltpu.VMEM((half_rows, fq), BF16),
             pltpu.VMEM((n, rows, fo), BF16),
             pltpu.VMEM((n, rows, fq), BF16),
-            pltpu.VMEM(down0.shape, BF16),
             pltpu.VMEM(up0.shape, BF16),
-            pltpu.VMEM((parts.shape[0], n) + gate0.shape, BF16),
-            pltpu.VMEM((parts.shape[0], n) + gate0.shape, BF16),
-            DMA((11,)),
-            DMA((2, 3)),
+            DMA((9,)),
+            DMA((2, n + 1)),
             DMA((4, n)),
-            DMA((parts.shape[0], 2, 2, n)),
         ]
         + [pltpu.VMEM((d,) + small.shape, F32) for d in sizes]
         + [DMA((2, sum(sizes)))],
         compiler_params=params(4, 60),
         name="last",
         cost_estimate=cost(60),
-    )(dqkv, h, wq, wk, wv, tokens, gain, dresid, small, wout, gate0, parts, down0, down_other, up0, up_other, comb, resid)
-
-
-def half(x, s, dim):
-    size = x.shape[dim] // 2
-    return lax.dynamic_slice_in_dim(x, s * size, size, dim)
-
-
-SWAP = [(0, 1), (1, 0)]
+    )(dqkv, h, wq, wk, wv, tokens, gain, dresid, small, wout, up0, up_other, comb, resid)
+
+
+def finish_kernel(*refs):
+    n_in = 8
+    total, gout, gqkv = refs[5:n_in]
+    outs = refs[n_in : n_in + 12]
+    sems = refs[n_in + 12]
+    output, tokens, norm1, gq, gk, gv, go, norm2, router, gate, up, down = outs
+    large = Staged(tuple(zip(refs[:5], (output, tokens, gate, up, down))), sems)
+    large.start()
+    norm1[...] = total[0, :]
+    norm2[...] = total[1, :]
+    router[...] = total[8 : 8 + router.shape[0], :]
+    qw, kw = gq.shape[1], gk.shape[1]
+    gq[...] = gqkv[:, :qw]
+    gk[...] = gqkv[:, qw : qw + kw]
+    gv[...] = gqkv[:, qw + kw :]
+    go[...] = gout[...].T
+    large.wait(0, 1, 2, 3, 4)
+
+
+def finish(experts_all, qw, output, tokens, gate, up, down, total, gout, gqkv):
+    sds = jax.ShapeDtypeStruct
+    width = total.shape[1]
+    rows = gqkv.shape[0]
+    kw = (gqkv.shape[1] - qw) // 2
+    shapes = (
+        output.shape,
+        tokens.shape,
+        (width,),
+        (rows, qw),
+        (rows, kw),
+        (rows, kw),
+        gout.shape[::-1],
+        (width,),
+        (experts_all, width),
+        gate.shape,
+        up.shape,
+        down.shape,
+    )
+    return pl.pallas_call(
+        finish_kernel,
+        out_shape=tuple(sds(x, F32) for x in shapes),
+        in_specs=[HBM] * 5 + [VMEM] * 3,
+        out_specs=(VMEM,) * 12,
+        scratch_shapes=[DMA((5,))],
+        compiler_params=pltpu.CompilerParams(vmem_limit_bytes=60 * MIB),
+        name="finish",
+        cost_estimate=cost(6),
+    )(output, tokens, gate, up, down, total, gout, gqkv)
 
 
 def body(
@@ -1806,32 +1878,29 @@
     top = routes.shape[1]
     cap = share * top * 5 // (4 * experts_all)
     slots = -(-n_mp * cap // 16) * 16
-    gain1 = norm1_gain.reshape(1, width)
-    gain2 = norm2_gain.reshape(1, width)
 
     cot_all = lax.all_gather(cotangent, "mp", axis=0, tiled=True)
     by_share = tokens.reshape(n_mp, share, width)
 
     normed_one, _ = rms_parts(tokens.astype(F32))
-    h_one = (normed_one * gain1).astype(BF16)
+    h_one = (normed_one * norm1_gain[None, :]).astype(BF16)
     qt = (jnp.einsum("df,td->ft", w_query, h_one, preferred_element_type=F32).astype(BF16)) * BF16(0.125)
     k = nn(h_one, key_weight_matrix).astype(BF16)
     v = nn(h_one, value_weight_matrix).astype(BF16)
     o, heads_t, lse, kv, cot_above, routes_line = attend(n_ctx, qt, k, v, cotangent, routes.T)
-    part = jnp.einsum("ft,fd->td", heads_t, w_out, preferred_element_type=F32).astype(BF16)
     resid, h_two, place, place_t, place_line, cot_line = mid_forward(
-        n_ctx, exp_local, slots, part.reshape(n_mp, share, width), gain2, cotangent, cot_above, routes_line, by_share
+        n_ctx, exp_local, slots, heads_t, w_out, norm2_gain, cotangent, cot_above, routes_line, by_share
     )
     h_two = h_two.reshape(tok, width)
 
     gates, gate_rows, arrived, hidden, dg, du, back, comb, arrived_line, cot_first, cot_line = moe(
-        n_ctx, n_seq, experts_all, h_two, cot_all, place, place_t, routes, router, w_gate, w_up, w_down, cot_line
+        n_ctx, n_seq, experts_all, h_two, cot_all, place, place_t, routes.T, router.T, w_gate, w_up, w_down, cot_line
     )
     dresid, db, small, gate_rows_line, hidden_line, du_below, du_above, arrived_other, dg_other = mid_back(
         n_ctx,
         back.reshape(n_mp, share, -1),
         resid,
-        gain2,
+        norm2_gain,
         cotangent,
         gates.reshape(n_mp, share, -1),
         router.T,
@@ -1843,11 +1912,7 @@
     )
 
     db = db.reshape(tok, width)
-    g_out = jnp.einsum("td,ft->df", db, heads_t, preferred_element_type=F32).astype(BF16)
-    g_out = (
-        half(g_out, s, 0).astype(F32) + lax.ppermute(half(g_out, 1 - s, 0), "seq", SWAP).astype(F32)
-    ).astype(BF16)
-    dqkv, gate0, gate_parts, down0, down_other, up0, up_other, _, _ = attend_back(
+    dqkv, g_gate, g_down, up0, up_other, g_out, _, _ = attend_back(
         n_ctx,
         qt,
         db,
@@ -1865,12 +1930,13 @@
         du_above,
         hidden_line,
         hidden,
+        heads_t,
         arrived_line,
         place_line,
         cot_line,
         cot_first,
     )
-    output, grad_tokens, small, g_out, g_qkv, g_gate, g_down, g_up = last(
+    output, grad_tokens, small, g_out, g_qkv, g_up = last(
         (n_seq, n_ctx, n_mp),
         dqkv,
         h_one,
@@ -1878,34 +1944,17 @@
         key_weight_matrix,
         value_weight_matrix,
         by_share,
-        gain1,
+        norm1_gain,
         dresid,
         small,
         g_out,
-        gate0,
-        gate_parts,
-        down0,
-        down_other,
         up0,
         up_other,
         comb.reshape(n_mp, share, width),
         resid,
     )
-    qw, kvw = w_query.shape[1], key_weight_matrix.shape[1]
-    return (
-        output,
-        grad_tokens,
-        small[0],
-        g_qkv[:, :qw],
-        g_qkv[:, qw : qw + kvw],
-        g_qkv[:, qw + kvw :],
-        g_out.T,
-        small[1],
-        small[8 : 8 + experts_all].T,
-        g_gate,
-        g_up,
-        g_down,
-    )
+    outs = finish(experts_all, w_query.shape[1], output, grad_tokens, g_gate, g_up, g_down, small, g_out, g_qkv)
+    return outs[:8] + (outs[8].T,) + outs[9:]
 
 
 def solution(mesh):

time: 363 us -> 326 us (0.90)
  local copies, waits for them, and re-layouts: 20.6 us -> 2.36 us
  Pallas kernels: 308 us -> 300 us
  matrix products: 11 us -> 4.61 us
    pallas_call x1, Pallas kernels: 78.4 us -> 54.6 us  [last(): pl.pallas_call(functools.partial(last_kernel, chunks, sizes), out_shape=(...]
    unnamed x34 -> x13, local copies, waits for them, and re-layouts: 12.3 us -> 2.36 us
    pallas_call x1, Pallas kernels: 80.1 us -> 89.8 us  [attend_back(): pl.pallas_call(functools.partial(attend_back_kernel, n), out_shape=(sds((...]
    pallas_call x0 -> x1, Pallas kernels: none -> 7.28 us  [finish(): pl.pallas_call(finish_kernel, out_shape=tuple((sds(x, F32) for x in shape...]
    dot_general x2 -> x0, matrix products: 6.39 us -> none  [the longest x1 3.5 us: body(): jnp.einsum('ft,fd->td', heads_t, w_out, preferred_element_type=F32)]
    slice x3 -> x0, local copies, waits for them, and re-layouts: 4.91 us -> none  [the longest x1 1.78 us: body(): g_qkv[:, :qw]]
  transfers between devices with their start and end apart: 2 -> 1, of which waited for: 0 -> 0; matrix products, arithmetic and copies ran while one was open for 5% -> 2% of each run, Pallas kernels for 40% -> 20%
where the time goes in v5:
time: 326 us; the launch traced here: 325 us
  Pallas kernels  300 us (92%)
  between operations  14.2 us (4%)
  matrix products  4.61 us (1%)
    pallas_call x1, Pallas kernels, attend_back(): pl.pallas_call(functools.partial(attend_back_kernel, n), out_shape=(sds((...  89.8 us
    pallas_call x1, Pallas kernels, last(): pl.pallas_call(functools.partial(last_kernel, chunks, sizes), out_shape=(...  54.6 us
    pallas_call x1, Pallas kernels, mid_back(): pl.pallas_call(functools.partial(mid_back_kernel, chunks, n), out_shape=(...  43.8 us
    pallas_call x1, Pallas kernels, moe(): pl.pallas_call(functools.partial(moe_kernel, n, n_seq, experts_all), out_...  39.3 us
    pallas_call x1, Pallas kernels, mid_forward(): pl.pallas_call(functools.partial(mid_forward_kernel, chunks, n, ex), out_...  37.9 us
    pallas_call x1, Pallas kernels, attend(): pl.pallas_call(functools.partial(attend_kernel, n), out_shape=(jax.ShapeD...  27.5 us
    pallas_call x1, Pallas kernels, finish(): pl.pallas_call(finish_kernel, out_shape=tuple((sds(x, F32) for x in shape...  7.28 us
  transfers between devices with their start and end apart: 1, of which 0 were waited for; matrix products, arithmetic and copies ran while one was open for 2% of the time, Pallas kernels for 20%

profile of v5, /device:TPU:16, one launch (start us, length us, event | category | flops | bytes accessed | tf_op | source)
XLA Modules:
  0.0 324.7 jit_solution(3305068710406499440)
XLA Ops:
  7.2 0.0 copy-start.5
  7.2 0.0 all-gather.2.cloned.1.call-start
  7.2 0.7 all-gather.2.cloned.1.call-update
  7.9 0.0 copy-start.1
  7.9 2.1 fusion
  10.1 0.0 copy-done.5
  10.1 0.0 copy-done.1
  10.1 0.0 copy-start.3
  10.1 0.5 fusion.2.h_hbm
  10.6 0.5 copy-done.3
  11.1 1.3 convolution_convert_fusion.1.v_ref
  12.5 0.0 copy-done.2
  12.5 1.3 convolution_convert_fusion.2.k_ref
  13.8 0.0 copy-done
  13.8 1.9 fusion.4.q_ref
  15.7 27.5 %attend.1 = (f32[384,640]{1,0:T(8,128)}, bf16[384,640]{1,0:T(8,128)(2,1)}, f32[6,1,640]{2,1,0:T(1,128)}, bf16[4,640,256]{2,1,0:T(8,128)(2,1)}, bf16[160,1536]{1,0:T(8,128)(2,1)}, /*index=5*/s32[4,2,640]{2,1,0:T(2,128)}) custom-call(bf16[384,640]{1,0:T(8,128)(2,1)} %fusion.4.q_ref, bf16[640,128]{1,0:T(8,128)(2,1)} %convolution_convert_fusion.2.k_ref, ...), custom_call_target="tpu_custom_call" | custom-call | bytes 108000000 | tf_op jit(solution)/shard_map/attend/pallas_call | solution.py:510
  43.2 37.9 %mid_forward.1 = (f32[160,1536]{1,0:T(8,128)}, bf16[4,160,1536]{2,1,0:T(8,128)(2,1)}, bf16[416,640]{1,0:T(8,128)(2,1)}, bf16[640,416]{1,0:T(8,128)(2,1)}, bf16[4...) custom-call(bf16[384,640]{1,0:T(8,128)(2,1)} %get-tuple-element.68.heads_ref, bf16[384,1536]{1,0:T(8,128)(2,1)} %wout_ref.3, ...), custom_call_target="tpu_custom_call" | custom-call | bytes 108000000 | tf_op jit(solution)/shard_map/mid_forward/pallas_call | solution.py:1377
  81.1 0.0 all-gather.2.cloned.1.call-done.cot_ref
  81.1 39.3 %moe.1 = (f32[640,128]{1,0:T(8,128)}, f32[8,256]{1,0:T(8,128)}, bf16[2,208,1536]{2,1,0:T(8,128)(2,1)}, bf16[4,2,208,256]{3,2,1,0:T(8,128)(2,1)}, bf16[2,208,1024...) custom-call(bf16[640,1536]{1,0:T(8,128)(2,1)} %bitcast.21, ...), custom_call_target="tpu_custom_call", output_to_operand_aliasing={{10}: (9, {})} | custom-call | bytes 108000000 | tf_op jit(solution)/shard_map/moe/pallas_call | solution.py:1136
  120.4 43.8 %mid_back.1 = (f32[160,1536]{1,0:T(8,128)}, bf16[4,160,1536]{2,1,0:T(8,128)(2,1)}, f32[16,1536]{1,0:T(8,128)}, f32[4,8,256]{2,1,0:T(8,128)}, bf16[4,2,208,256]{3...) custom-call(bf16[4,160,1664]{2,1,0:T(8,128)(2,1)} %bitcast.19, ...), custom_call_target="tpu_custom_call" | custom-call | bytes 115200000 | tf_op jit(solution)/shard_map/mid_back/pallas_call | solution.py:1506
  164.3 89.8 %attend_back.1 = (bf16[640,640]{1,0:T(8,128)(2,1)}, f32[2,192,1024]{2,1,0:T(8,128)}, f32[2,128,1536]{2,1,0:T(8,128)}, f32[2,192,1024]{2,1,0:T(8,128)}, bf16[2,19...) custom-call(bf16[384,640]{1,0:T(8,128)(2,1)} %fusion.4.q_ref, ...), custom_call_target="tpu_custom_call" | custom-call | bytes 216000000 | tf_op jit(solution)/shard_map/attend_back/pallas_call | solution.py:875
  254.1 54.6 %last.1 = (f32[160,1536]{1,0:T(8,128)}, f32[160,1536]{1,0:T(8,128)}, f32[16,1536]{1,0:T(8,128)}, f32[192,384]{1,0:T(8,128)}, f32[192,640]{1,0:T(8,128)}, /*index=5*/f32[2,192,1024]{2,1,0:T(8,128)}) custom-call(bf16[640,640]{1,0:T(8,128)(2,1)} %get-tuple-element.97.dqkv_ref, bf16[640,1536]{1,0:T(8,128)(2,1)} %copy-done, bf16[1536,384]{1,0:T(8,128)(2,1)} %wq_hbm.1, ...), custom_call_target="tpu_custom_call" | custom-call | bytes 216000000 | tf_op jit(solution)/shard_map/last/pallas_call | solution.py:1771
  308.7 7.3 %finish.1 = (f32[160,1536]{1,0:T(8,128)}, f32[160,1536]{1,0:T(8,128)}, f32[1536]{0:T(1024)}, f32[192,384]{1,0:T(8,128)}, f32[192,128]{1,0:T(8,128)}, /*index=5*/...) custom-call(f32[160,1536]{1,0:T(8,128)} %get-tuple-element.104.refs_, ...), custom_call_target="tpu_custom_call" | custom-call | bytes 21600000 | tf_op jit(solution)/shard_map/finish/pallas_call | solution.py:1845
  316.0 1.9 copy.27
  (5 shorter events, 0.0 us)
Async XLA Ops:
  7.2 2.9 copy-start.5
  7.2 73.9 %all-gather.2.cloned.1.call-start = ((), (), s32[]{:S(2)}) async-start(), calls=%async_computation | async-start | bytes 2457600 | tf_op jit(solution)/shard_map/all_gather | solution.py:1882
  7.9 2.2 copy-start.1
  10.1 1.0 copy-start.3
  11.1 2.7 copy-start
  11.1 1.3 copy-start.2
  11.1 2.7 copy-start.4
Sparse Core Ops, SparseCore 0:
  9.6 22.9 all-gather.1

commit v6 on v5

--- a/solution.py
+++ b/solution.py
@@ -385,11 +385,15 @@
 
 def attend_kernel(
     n,
-    q_ref,
-    k_ref,
-    v_ref,
+    tok_ref,
+    gain,
+    wq_ref,
+    wk_ref,
+    wv_ref,
     cot_ref,
     routes_ref,
+    q_ref,
+    h_ref,
     o_ref,
     heads_ref,
     lse_ref,
@@ -406,12 +410,19 @@
     peers_sem,
 ):
     s, c, m = lax.axis_index("seq"), lax.axis_index("ctx"), lax.axis_index("mp")
-    t, kvw = k_ref.shape
+    t, kvw = tok_ref.shape[0], wk_ref.shape[1]
     heads = q_ref.shape[0] // HEAD_SIZE
     group = heads // (kvw // HEAD_SIZE)
     up, down = (s, lax.rem(c + 1, n), m), (s, lax.rem(c + n - 1, n), m)
-    kv_ref[0, :, :kvw] = k_ref[...]
-    kv_ref[0, :, kvw:] = v_ref[...]
+
+    def norm_rows(i):
+        rows = pl.ds(pl.multiple_of(i * 128, 128), 128)
+        normed, _ = rms_parts(tok_ref[rows, :].astype(F32))
+        h_ref[rows, :] = (normed * gain[...].reshape(1, -1)).astype(BF16)
+
+    loop(t // 128, norm_rows)
+    kv_ref[0, :, :kvw] = nn(h_ref[...], wk_ref[...]).astype(BF16)
+    kv_ref[0, :, kvw:] = nn(h_ref[...], wv_ref[...]).astype(BF16)
     line_ref[c] = routes_ref[...]
     peers = Peers(n, lambda p: routes_ref, lambda i: line_ref.at[i], peers_sem.at[0], peers_sem.at[1])
     beside = Neighbours(n, cot_ref, None, above_ref, side.at[0], side.at[1])
@@ -445,6 +456,7 @@
 
     peers.start()
     beside.start_down()
+    q_ref[...] = (nn(h_ref[...], wq_ref[...]) * 0.125).astype(BF16).T
     pad_heads(q_ref, qpad, heads, group)
     top[...] = jnp.full_like(top, -1e30)
     tot[...] = jnp.zeros_like(tot)
@@ -503,13 +515,15 @@
     beside.finish(up=False)
 
 
-def attend(n, qt, k, v, cot, routes):
-    t, kvw = k.shape
-    qw = qt.shape[0]
+def attend(n, tokens, gain, wq, wk, wv, cot, routes):
+    t, kvw = tokens.shape[0], wk.shape[1]
+    qw = wq.shape[1]
     heads = qw // HEAD_SIZE
     return pl.pallas_call(
         functools.partial(attend_kernel, n),
         out_shape=(
+            jax.ShapeDtypeStruct((qw, t), BF16),
+            jax.ShapeDtypeStruct(tokens.shape, BF16),
             jax.ShapeDtypeStruct((qw, t), F32),
             jax.ShapeDtypeStruct((qw, t), BF16),
             jax.ShapeDtypeStruct((heads, 1, t), F32),
@@ -517,8 +531,8 @@
             jax.ShapeDtypeStruct(cot.shape, BF16),
             jax.ShapeDtypeStruct((n,) + routes.shape, jnp.int32),
         ),
-        in_specs=[VMEM] * 3 + [HBM, VMEM],
-        out_specs=(VMEM,) * 4 + (HBM, VMEM),
+        in_specs=[VMEM] * 5 + [HBM, VMEM],
+        out_specs=(VMEM,) * 6 + (HBM, VMEM),
         scratch_shapes=[
             pltpu.VMEM((heads, kvw, t), BF16),
             pltpu.VMEM((kvw, t), BF16),
@@ -532,7 +546,7 @@
         compiler_params=params(0),
         name="attend",
         cost_estimate=cost(30),
-    )(qt, k, v, cot, routes)
+    )(tokens, gain, wq, wk, wv, cot, routes)
 
 
 def attend_back_kernel(
@@ -1882,12 +1896,9 @@
     cot_all = lax.all_gather(cotangent, "mp", axis=0, tiled=True)
     by_share = tokens.reshape(n_mp, share, width)
 
-    normed_one, _ = rms_parts(tokens.astype(F32))
-    h_one = (normed_one * norm1_gain[None, :]).astype(BF16)
-    qt = (jnp.einsum("df,td->ft", w_query, h_one, preferred_element_type=F32).astype(BF16)) * BF16(0.125)
-    k = nn(h_one, key_weight_matrix).astype(BF16)
-    v = nn(h_one, value_weight_matrix).astype(BF16)
-    o, heads_t, lse, kv, cot_above, routes_line = attend(n_ctx, qt, k, v, cotangent, routes.T)
+    qt, h_one, o, heads_t, lse, kv, cot_above, routes_line = attend(
+        n_ctx, tokens, norm1_gain, w_query, key_weight_matrix, value_weight_matrix, cotangent, routes.T
+    )
     resid, h_two, place, place_t, place_line, cot_line = mid_forward(
         n_ctx, exp_local, slots, heads_t, w_out, norm2_gain, cotangent, cot_above, routes_line, by_share
     )

time: 326 us -> 322 us (0.988)
  matrix products: 4.61 us -> 0 us
  Pallas kernels: 300 us -> 304 us
    dot_general x3 -> x0, matrix products: 4.61 us -> none  [the longest x2 2.68 us: nn(): return jnp.dot(a, b, preferred_element_type=F32)]
    pallas_call x1, Pallas kernels: 27.5 us -> 31.4 us  [attend(): pl.pallas_call(functools.partial(attend_kernel, n), out_shape=(jax.ShapeD...]
  transfers between devices with their start and end apart: 1 -> 1, of which waited for: 0 -> 0; matrix products, arithmetic and copies ran while one was open for 2% -> 0% of each run, Pallas kernels for 20% -> 22%
where the time goes in v6:
time: 322 us; the launch traced here: 321 us
  Pallas kernels  304 us (94%)
  between operations  14.1 us (4%)
    pallas_call x1, Pallas kernels, attend_back(): pl.pallas_call(functools.partial(attend_back_kernel, n), out_shape=(sds((...  89.8 us
    pallas_call x1, Pallas kernels, last(): pl.pallas_call(functools.partial(last_kernel, chunks, sizes), out_shape=(...  54.6 us
    pallas_call x1, Pallas kernels, mid_back(): pl.pallas_call(functools.partial(mid_back_kernel, chunks, n), out_shape=(...  43.8 us
    pallas_call x1, Pallas kernels, moe(): pl.pallas_call(functools.partial(moe_kernel, n, n_seq, experts_all), out_...  39.3 us
    pallas_call x1, Pallas kernels, mid_forward(): pl.pallas_call(functools.partial(mid_forward_kernel, chunks, n, ex), out_...  38 us
    pallas_call x1, Pallas kernels, attend(): pl.pallas_call(functools.partial(attend_kernel, n), out_shape=(jax.ShapeD...  31.4 us
    pallas_call x1, Pallas kernels, finish(): pl.pallas_call(finish_kernel, out_shape=tuple((sds(x, F32) for x in shape...  7.28 us
  transfers between devices with their start and end apart: 1, of which 0 were waited for; matrix products, arithmetic and copies ran while one was open for 0% of the time, Pallas kernels for 22%

profile of v6, /device:TPU:16, one launch (start us, length us, event | category | flops | bytes accessed | tf_op | source)
XLA Modules:
  0.0 320.9 jit_solution(15358056230869678998)
XLA Ops:
  7.2 0.0 all-gather.2.cloned.1.call-start
  7.2 0.7 all-gather.2.cloned.1.call-update
  7.9 31.4 %attend.1 = (bf16[384,640]{1,0:T(8,128)(2,1)}, bf16[640,1536]{1,0:T(8,128)(2,1)}, f32[384,640]{1,0:T(8,128)}, bf16[384,640]{1,0:T(8,128)(2,1)}, f32[6,1,640]{2,1...) custom-call(bf16[640,1536]{1,0:T(8,128)(2,1)} %tok_ref.1, f32[1536]{0:T(1024)} %gain.7, ...), custom_call_target="tpu_custom_call" | custom-call | bytes 108000000 | tf_op jit(solution)/shard_map/attend/pallas_call | solution.py:522
  39.3 38.0 %mid_forward.1 = (f32[160,1536]{1,0:T(8,128)}, bf16[4,160,1536]{2,1,0:T(8,128)(2,1)}, bf16[416,640]{1,0:T(8,128)(2,1)}, bf16[640,416]{1,0:T(8,128)(2,1)}, bf16[4...) custom-call(bf16[384,640]{1,0:T(8,128)(2,1)} %get-tuple-element.71.heads_ref, bf16[384,1536]{1,0:T(8,128)(2,1)} %wout_ref.3, ...), custom_call_target="tpu_custom_call" | custom-call | bytes 108000000 | tf_op jit(solution)/shard_map/mid_forward/pallas_call | solution.py:1391
  77.3 0.0 all-gather.2.cloned.1.call-done.cot_ref
  77.4 39.3 %moe.1 = (f32[640,128]{1,0:T(8,128)}, f32[8,256]{1,0:T(8,128)}, bf16[2,208,1536]{2,1,0:T(8,128)(2,1)}, bf16[4,2,208,256]{3,2,1,0:T(8,128)(2,1)}, bf16[2,208,1024...) custom-call(bf16[640,1536]{1,0:T(8,128)(2,1)} %bitcast.13, ...), custom_call_target="tpu_custom_call", output_to_operand_aliasing={{10}: (9, {})} | custom-call | bytes 108000000 | tf_op jit(solution)/shard_map/moe/pallas_call | solution.py:1150
  116.7 43.8 %mid_back.1 = (f32[160,1536]{1,0:T(8,128)}, bf16[4,160,1536]{2,1,0:T(8,128)(2,1)}, f32[16,1536]{1,0:T(8,128)}, f32[4,8,256]{2,1,0:T(8,128)}, bf16[4,2,208,256]{3...) custom-call(bf16[4,160,1664]{2,1,0:T(8,128)(2,1)} %bitcast.11, ...), custom_call_target="tpu_custom_call" | custom-call | bytes 115200000 | tf_op jit(solution)/shard_map/mid_back/pallas_call | solution.py:1520
  160.5 89.8 %attend_back.1 = (bf16[640,640]{1,0:T(8,128)(2,1)}, f32[2,192,1024]{2,1,0:T(8,128)}, f32[2,128,1536]{2,1,0:T(8,128)}, f32[2,192,1024]{2,1,0:T(8,128)}, bf16[2,19...) custom-call(bf16[384,640]{1,0:T(8,128)(2,1)} %get-tuple-element.70.q, ...), custom_call_target="tpu_custom_call" | custom-call | bytes 216000000 | tf_op jit(solution)/shard_map/attend_back/pallas_call | solution.py:889
  250.3 54.6 %last.1 = (f32[160,1536]{1,0:T(8,128)}, f32[160,1536]{1,0:T(8,128)}, f32[16,1536]{1,0:T(8,128)}, f32[192,384]{1,0:T(8,128)}, f32[192,640]{1,0:T(8,128)}, /*index=5*/f32[2,192,1024]{2,1,0:T(8,128)}) custom-call(bf16[640,640]{1,0:T(8,128)(2,1)} %get-tuple-element.100.dqkv_ref, bf16[640,1536]{1,0:T(8,128)(2,1)} %get-tuple-element.101.h_hbm, ...), custom_call_target="tpu_custom_call" | custom-call | bytes 216000000 | tf_op jit(solution)/shard_map/last/pallas_call | solution.py:1785
  304.9 7.3 %finish.1 = (f32[160,1536]{1,0:T(8,128)}, f32[160,1536]{1,0:T(8,128)}, f32[1536]{0:T(1024)}, f32[192,384]{1,0:T(8,128)}, f32[192,128]{1,0:T(8,128)}, /*index=5*/...) custom-call(f32[160,1536]{1,0:T(8,128)} %get-tuple-element.108.refs_, ...), custom_call_target="tpu_custom_call" | custom-call | bytes 21600000 | tf_op jit(solution)/shard_map/finish/pallas_call | solution.py:1859
  312.2 1.9 copy.26
Async XLA Ops:
  7.2 70.2 %all-gather.2.cloned.1.call-start = ((), (), s32[]{:S(2)}) async-start(), calls=%async_computation | async-start | bytes 2457600 | tf_op jit(solution)/shard_map/all_gather | solution.py:1896
Sparse Core Ops, SparseCore 0:
  9.6 22.9 all-gather.1

commit v7 on v6

--- a/solution.py
+++ b/solution.py
@@ -551,23 +551,23 @@
 
 def attend_back_kernel(
     n,
-    q_ref,
-    db_ref,
-    wout_ref,
-    o_ref,
+    q_hbm,
+    db_hbm,
+    wout_hbm,
+    o_hbm,
     lse_ref,
-    kv_ref,
+    kv_hbm,
     arr_ref,
     arr_other,
     dg_ref,
     dg_other,
     rows_line,
-    own_ref,
-    below_ref,
-    above_ref,
+    own_hbm,
+    below_hbm,
+    above_hbm,
     hid_hbm,
     hid_own,
-    heads_ref,
+    heads_hbm,
     arr_hbm,
     place_hbm,
     line_hbm,
@@ -609,8 +609,33 @@
     wout_in,
     down_out,
     down_in,
+    stage_sem,
+    db_ref,
+    wout_ref,
+    own_ref,
+    below_ref,
+    above_ref,
+    heads_ref,
+    q_ref,
+    o_ref,
+    kv_ref,
 ):
     s, c, m = lax.axis_index("seq"), lax.axis_index("ctx"), lax.axis_index("mp")
+    load = Staged(
+        (
+            (db_hbm, db_ref),
+            (wout_hbm, wout_ref),
+            (own_hbm, own_ref),
+            (below_hbm, below_ref),
+            (above_hbm, above_ref),
+            (heads_hbm, heads_ref),
+            (q_hbm, q_ref),
+            (o_hbm, o_ref),
+            (kv_hbm, kv_ref),
+        ),
+        stage_sem,
+    )
+    load.start()
     _, t, kvw2 = kv_ref.shape
     kvw = kvw2 // 2
     heads = q_ref.shape[0] // HEAD_SIZE
@@ -627,7 +652,6 @@
     cots.signal(sem)
     pl.semaphore_signal(sem, inc=1, device_id=swap_partner(), device_id_type=MESH)
     pl.semaphore_wait(sem, line_degree(n) + 3)
-    spread.start()
     cots.start()
 
     def gate_part(e, out):
@@ -642,7 +666,11 @@
         gate_part(e, sum_ref.at[e])
         if e == 0:
             line.first(0)
+            load.wait(0, 1, 2, 3, 4)
+            spread.start()
     do_ref[...] = nt(wout_ref[...], db_ref[...]).astype(BF16)
+
+    load.wait(5)
 
     def wout_piece(r):
         at = pl.ds(pl.multiple_of(r * 512, 512), 512)
@@ -662,6 +690,7 @@
                 spread.tick(hop)
 
     ticks = max(line.ticks, 2 * (n - 2)) + 1
+    load.wait(6, 7, 8)
     pad_heads(q_ref, qpad, heads, group)
     pad_heads(do_ref, dopad, heads, group)
     for h in range(heads):
@@ -898,7 +927,7 @@
             sds((n,) + du.shape, BF16),
             sds((n - blocks,) + first.shape[1:], BF16),
         ),
-        in_specs=[VMEM] * 14 + [HBM] * 2 + [VMEM] + [HBM] * 4,
+        in_specs=[HBM] * 4 + [VMEM, HBM] + [VMEM] * 5 + [HBM] * 10,
         out_specs=(VMEM,) * 6 + (HBM,) * 2,
         scratch_shapes=[
             pltpu.VMEM((qw, t), BF16),
@@ -930,7 +959,9 @@
             pltpu.VMEM((qw, half_width), BF16),
             pltpu.VMEM((ex, fa // 2, width), BF16),
             pltpu.VMEM((ex, fa // 2, width), BF16),
-        ],
+            DMA((9,)),
+        ]
+        + [pltpu.VMEM(x.shape, x.dtype) for x in (db, w_out, du, below, above, heads_t, qt, o, kv)],
         compiler_params=params(1, 62),
         name="attend_back",
         cost_estimate=cost(60),

time: 322 us -> 320 us (level)
  no operation moved by 1% of the time
where the time goes in v7:
time: 320 us; the launch traced here: 318 us
  Pallas kernels  302 us (94%)
  between operations  14.1 us (4%)
    pallas_call x1, Pallas kernels, attend_back(): pl.pallas_call(functools.partial(attend_back_kernel, n), out_shape=(sds((...  87.4 us
    pallas_call x1, Pallas kernels, last(): pl.pallas_call(functools.partial(last_kernel, chunks, sizes), out_shape=(...  54.5 us
    pallas_call x1, Pallas kernels, mid_back(): pl.pallas_call(functools.partial(mid_back_kernel, chunks, n), out_shape=(...  43.8 us
    pallas_call x1, Pallas kernels, moe(): pl.pallas_call(functools.partial(moe_kernel, n, n_seq, experts_all), out_...  39.3 us
    pallas_call x1, Pallas kernels, mid_forward(): pl.pallas_call(functools.partial(mid_forward_kernel, chunks, n, ex), out_...  38 us
    pallas_call x1, Pallas kernels, attend(): pl.pallas_call(functools.partial(attend_kernel, n), out_shape=(jax.ShapeD...  31.4 us
    pallas_call x1, Pallas kernels, finish(): pl.pallas_call(finish_kernel, out_shape=tuple((sds(x, F32) for x in shape...  7.28 us
  transfers between devices with their start and end apart: 1, of which 0 were waited for; matrix products, arithmetic and copies ran while one was open for 0% of the time, Pallas kernels for 22%

profile of v7, /device:TPU:16, one launch (start us, length us, event | category | flops | bytes accessed | tf_op | source)
XLA Modules:
  0.0 318.4 jit_solution(17632121257653319026)
XLA Ops:
  7.2 0.0 all-gather.2.cloned.1.call-start
  7.2 0.7 all-gather.2.cloned.1.call-update
  7.9 31.4 %attend.1 = (bf16[384,640]{1,0:T(8,128)(2,1)}, bf16[640,1536]{1,0:T(8,128)(2,1)}, f32[384,640]{1,0:T(8,128)}, bf16[384,640]{1,0:T(8,128)(2,1)}, f32[6,1,640]{2,1...) custom-call(bf16[640,1536]{1,0:T(8,128)(2,1)} %tok_ref.1, f32[1536]{0:T(1024)} %gain.7, ...), custom_call_target="tpu_custom_call" | custom-call | bytes 108000000 | tf_op jit(solution)/shard_map/attend/pallas_call | solution.py:522
  39.3 38.0 %mid_forward.1 = (f32[160,1536]{1,0:T(8,128)}, bf16[4,160,1536]{2,1,0:T(8,128)(2,1)}, bf16[416,640]{1,0:T(8,128)(2,1)}, bf16[640,416]{1,0:T(8,128)(2,1)}, bf16[4...) custom-call(bf16[384,640]{1,0:T(8,128)(2,1)} %get-tuple-element.71.heads_ref.heads_hbm, bf16[384,1536]{1,0:T(8,128)(2,1)} %wout_hbm.1, ...), custom_call_target="tpu_custom_call" | custom-call | bytes 108000000 | tf_op jit(solution)/shard_map/mid_forward/pallas_call | solution.py:1422
  77.3 0.0 all-gather.2.cloned.1.call-done.cot_ref
  77.4 39.3 %moe.1 = (f32[640,128]{1,0:T(8,128)}, f32[8,256]{1,0:T(8,128)}, bf16[2,208,1536]{2,1,0:T(8,128)(2,1)}, bf16[4,2,208,256]{3,2,1,0:T(8,128)(2,1)}, bf16[2,208,1024...) custom-call(bf16[640,1536]{1,0:T(8,128)(2,1)} %bitcast.13, ...), custom_call_target="tpu_custom_call", output_to_operand_aliasing={{10}: (9, {})} | custom-call | bytes 108000000 | tf_op jit(solution)/shard_map/moe/pallas_call | solution.py:1181
  116.7 43.8 %mid_back.1 = (f32[160,1536]{1,0:T(8,128)}, bf16[4,160,1536]{2,1,0:T(8,128)(2,1)}, f32[16,1536]{1,0:T(8,128)}, f32[4,8,256]{2,1,0:T(8,128)}, bf16[4,2,208,256]{3...) custom-call(bf16[4,160,1664]{2,1,0:T(8,128)(2,1)} %bitcast.11, ...), custom_call_target="tpu_custom_call" | custom-call | bytes 115200000 | tf_op jit(solution)/shard_map/mid_back/pallas_call | solution.py:1551
  160.5 87.4 %attend_back.1 = (bf16[640,640]{1,0:T(8,128)(2,1)}, f32[2,192,1024]{2,1,0:T(8,128)}, f32[2,128,1536]{2,1,0:T(8,128)}, f32[2,192,1024]{2,1,0:T(8,128)}, bf16[2,19...) custom-call(bf16[384,640]{1,0:T(8,128)(2,1)} %get-tuple-element.70.q, ...), custom_call_target="tpu_custom_call" | custom-call | bytes 216000000 | tf_op jit(solution)/shard_map/attend_back/pallas_call | solution.py:918
  247.9 54.5 %last.1 = (f32[160,1536]{1,0:T(8,128)}, f32[160,1536]{1,0:T(8,128)}, f32[16,1536]{1,0:T(8,128)}, f32[192,384]{1,0:T(8,128)}, f32[192,640]{1,0:T(8,128)}, /*index=5*/f32[2,192,1024]{2,1,0:T(8,128)}) custom-call(bf16[640,640]{1,0:T(8,128)(2,1)} %get-tuple-element.100.dqkv_ref, bf16[640,1536]{1,0:T(8,128)(2,1)} %get-tuple-element.101.h_hbm, ...), custom_call_target="tpu_custom_call" | custom-call | bytes 216000000 | tf_op jit(solution)/shard_map/last/pallas_call | solution.py:1816
  302.4 7.3 %finish.1 = (f32[160,1536]{1,0:T(8,128)}, f32[160,1536]{1,0:T(8,128)}, f32[1536]{0:T(1024)}, f32[192,384]{1,0:T(8,128)}, f32[192,128]{1,0:T(8,128)}, /*index=5*/...) custom-call(f32[160,1536]{1,0:T(8,128)} %get-tuple-element.108.refs_, ...), custom_call_target="tpu_custom_call" | custom-call | bytes 21600000 | tf_op jit(solution)/shard_map/finish/pallas_call | solution.py:1890
  309.7 1.9 copy.26
Async XLA Ops:
  7.2 70.2 %all-gather.2.cloned.1.call-start = ((), (), s32[]{:S(2)}) async-start(), calls=%async_computation | async-start | bytes 2457600 | tf_op jit(solution)/shard_map/all_gather | solution.py:1927
Sparse Core Ops, SparseCore 0:
  9.6 22.9 all-gather.1

commit v8 on v7

--- a/solution.py
+++ b/solution.py
@@ -985,9 +985,9 @@
     n_seq,
     experts_all,
     h_ref,
-    cot_ref,
+    cot_hbm,
     place_ref,
-    place_t_ref,
+    place_t_hbm,
     routes_ref,
     router_ref,
     wg_hbm,
@@ -1022,8 +1022,13 @@
     far_sem,
     router3,
     named,
+    stage_sem,
+    cot_ref,
+    place_t_ref,
 ):
     s, c, m = lax.axis_index("seq"), lax.axis_index("ctx"), lax.axis_index("mp")
+    load = Staged(((cot_hbm, cot_ref), (place_t_hbm, place_t_ref)), stage_sem)
+    load.start()
     ex, width, ff = wg.shape
     slots = place_ref.shape[0] // ex
     first = m * ex
@@ -1109,6 +1114,7 @@
 
     rows_ref[...] = cols[...].T[:8, :]
     wide = 512
+    load.wait(0)
     for e in range(ex):
         col = gate_col[e]
 
@@ -1151,6 +1157,8 @@
         high = grads.astype(BF16).astype(F32)
         here = jnp.where(lane == first + e, high, jnp.where(lane == lanes // 2 + first + e, grads - high, 0.0))
         back_rows[rows_of(e), width:] = here.astype(BF16)
+
+    load.wait(1)
 
     def scatter(i):
         cut = pl.ds(pl.multiple_of(i * 256, 256), 256)
@@ -1193,7 +1201,7 @@
             sds((blocks, tok, width), BF16),
             sds(line.shape, BF16),
         ),
-        in_specs=[VMEM] * 6 + [HBM] * 4,
+        in_specs=[VMEM, HBM, VMEM, HBM, VMEM, VMEM] + [HBM] * 4,
         out_specs=(VMEM,) * 8 + (HBM,) * 3,
         scratch_shapes=[
             pltpu.VMEM(wg.shape, BF16),
@@ -1213,6 +1221,9 @@
             DMA((2,)),
             pltpu.VMEM((128, width), BF16),
             pltpu.VMEM((8, tok), F32),
+            DMA((2,)),
+            pltpu.VMEM(cot.shape, BF16),
+            pltpu.VMEM(place_t.shape, BF16),
         ],
         input_output_aliases={9: 10},
         compiler_params=params(6, 60),
@@ -1444,10 +1455,10 @@
     chunks,
     n,
     part,
-    resid_ref,
+    resid_hbm,
     gain,
-    cot,
-    gate_ref,
+    cot_hbm,
+    gate_hbm,
     router_ref,
     rows_ref,
     hid_ref,
@@ -1470,8 +1481,14 @@
     side,
     peers_sem,
     swap_sem,
+    stage_sem,
+    resid_ref,
+    cot,
+    gate_ref,
 ):
     c = lax.axis_index("ctx")
+    load = Staged(((resid_hbm, resid_ref), (cot_hbm, cot), (gate_hbm, gate_ref)), stage_sem)
+    load.start()
     mp = Mp(part, core_in, y_out, y_in, db_ref, sems, chunks)
     rows_peers = Peers(n, lambda p: rows_ref, lambda i: rows_line.at[i], peers_sem.at[0], peers_sem.at[1])
     hid_peers = Peers(n, lambda p: hid_ref.at[p], lambda i: hid_line.at[i], peers_sem.at[2], peers_sem.at[3])
@@ -1502,6 +1519,7 @@
     mp.rs_forward()
     rows_line[c] = rows_ref[...]
     small_ref[...] = jnp.zeros_like(small_ref)
+    load.wait(0, 1, 2)
     for i in range(chunks):
         cut = mp.cut(i)
         both = mp.rs_chunk(i)
@@ -1561,9 +1579,10 @@
             jax.ShapeDtypeStruct(arr.shape[:2] + (arr.shape[2] // 2,), BF16),
             jax.ShapeDtypeStruct(dg.shape, BF16),
         ),
-        in_specs=[VMEM] * 7 + [HBM] * 4,
+        in_specs=[VMEM, HBM, VMEM, HBM, HBM, VMEM, VMEM] + [HBM] * 4,
         out_specs=(VMEM,) * 4 + (HBM,) * 5,
-        scratch_shapes=mp_scratch(share, wide, chunks) + [DMA((2, 2)), DMA((4, n)), DMA((2, 2))],
+        scratch_shapes=mp_scratch(share, wide, chunks) + [DMA((2, 2)), DMA((4, n)), DMA((2, 2)), DMA((3,))]
+        + [pltpu.VMEM(x.shape, x.dtype) for x in (resid, cot, gate)],
         compiler_params=params(3, 60),
         name="mid_back",
         cost_estimate=cost(32),

time: 320 us -> 319 us (level)
  no operation moved by 1% of the time
where the time goes in v8:
time: 319 us; the launch traced here: 317 us
  Pallas kernels  301 us (94%)
  between operations  14.1 us (4%)
    pallas_call x1, Pallas kernels, attend_back(): pl.pallas_call(functools.partial(attend_back_kernel, n), out_shape=(sds((...  87.4 us
    pallas_call x1, Pallas kernels, last(): pl.pallas_call(functools.partial(last_kernel, chunks, sizes), out_shape=(...  54.5 us
    pallas_call x1, Pallas kernels, mid_back(): pl.pallas_call(functools.partial(mid_back_kernel, chunks, n), out_shape=(...  43.3 us
    pallas_call x1, Pallas kernels, moe(): pl.pallas_call(functools.partial(moe_kernel, n, n_seq, experts_all), out_...  38.6 us
    pallas_call x1, Pallas kernels, mid_forward(): pl.pallas_call(functools.partial(mid_forward_kernel, chunks, n, ex), out_...  38 us
    pallas_call x1, Pallas kernels, attend(): pl.pallas_call(functools.partial(attend_kernel, n), out_shape=(jax.ShapeD...  31.4 us
    pallas_call x1, Pallas kernels, finish(): pl.pallas_call(finish_kernel, out_shape=tuple((sds(x, F32) for x in shape...  7.28 us
  transfers between devices with their start and end apart: 1, of which 0 were waited for; matrix products, arithmetic and copies ran while one was open for 0% of the time, Pallas kernels for 22%

profile of v8, /device:TPU:16, one launch (start us, length us, event | category | flops | bytes accessed | tf_op | source)
XLA Modules:
  0.0 317.2 jit_solution(11602093958604152178)
XLA Ops:
  7.2 0.0 all-gather.2.cloned.1.call-start
  7.2 0.7 all-gather.2.cloned.1.call-update
  7.9 31.4 %attend.1 = (bf16[384,640]{1,0:T(8,128)(2,1)}, bf16[640,1536]{1,0:T(8,128)(2,1)}, f32[384,640]{1,0:T(8,128)}, bf16[384,640]{1,0:T(8,128)(2,1)}, f32[6,1,640]{2,1...) custom-call(bf16[640,1536]{1,0:T(8,128)(2,1)} %tok_ref.1, f32[1536]{0:T(1024)} %gain.7, ...), custom_call_target="tpu_custom_call" | custom-call | bytes 108000000 | tf_op jit(solution)/shard_map/attend/pallas_call | solution.py:522
  39.3 38.0 %mid_forward.1 = (f32[160,1536]{1,0:T(8,128)}, bf16[4,160,1536]{2,1,0:T(8,128)(2,1)}, bf16[416,640]{1,0:T(8,128)(2,1)}, bf16[640,416]{1,0:T(8,128)(2,1)}, bf16[4...) custom-call(bf16[384,640]{1,0:T(8,128)(2,1)} %get-tuple-element.71.heads_ref.heads_hbm, bf16[384,1536]{1,0:T(8,128)(2,1)} %wout_hbm.1, ...), custom_call_target="tpu_custom_call" | custom-call | bytes 108000000 | tf_op jit(solution)/shard_map/mid_forward/pallas_call | solution.py:1433
  77.3 0.0 all-gather.2.cloned.1.call-done.cot_hbm
  77.4 38.6 %moe.1 = (f32[640,128]{1,0:T(8,128)}, f32[8,256]{1,0:T(8,128)}, bf16[2,208,1536]{2,1,0:T(8,128)(2,1)}, bf16[4,2,208,256]{3,2,1,0:T(8,128)(2,1)}, bf16[2,208,1024...) custom-call(bf16[640,1536]{1,0:T(8,128)(2,1)} %bitcast.13, ...), custom_call_target="tpu_custom_call", output_to_operand_aliasing={{10}: (9, {})} | custom-call | bytes 108000000 | tf_op jit(solution)/shard_map/moe/pallas_call | solution.py:1189
  116.0 43.3 %mid_back.1 = (f32[160,1536]{1,0:T(8,128)}, bf16[4,160,1536]{2,1,0:T(8,128)(2,1)}, f32[16,1536]{1,0:T(8,128)}, f32[4,8,256]{2,1,0:T(8,128)}, bf16[4,2,208,256]{3...) custom-call(bf16[4,160,1664]{2,1,0:T(8,128)(2,1)} %bitcast.11, ...), custom_call_target="tpu_custom_call" | custom-call | bytes 115200000 | tf_op jit(solution)/shard_map/mid_back/pallas_call | solution.py:1569
  159.3 87.4 %attend_back.1 = (bf16[640,640]{1,0:T(8,128)(2,1)}, f32[2,192,1024]{2,1,0:T(8,128)}, f32[2,128,1536]{2,1,0:T(8,128)}, f32[2,192,1024]{2,1,0:T(8,128)}, bf16[2,19...) custom-call(bf16[384,640]{1,0:T(8,128)(2,1)} %get-tuple-element.70.q, ...), custom_call_target="tpu_custom_call" | custom-call | bytes 216000000 | tf_op jit(solution)/shard_map/attend_back/pallas_call | solution.py:918
  246.7 54.5 %last.1 = (f32[160,1536]{1,0:T(8,128)}, f32[160,1536]{1,0:T(8,128)}, f32[16,1536]{1,0:T(8,128)}, f32[192,384]{1,0:T(8,128)}, f32[192,640]{1,0:T(8,128)}, /*index=5*/f32[2,192,1024]{2,1,0:T(8,128)}) custom-call(bf16[640,640]{1,0:T(8,128)(2,1)} %get-tuple-element.100.dqkv_ref, bf16[640,1536]{1,0:T(8,128)(2,1)} %get-tuple-element.101.h_hbm, ...), custom_call_target="tpu_custom_call" | custom-call | bytes 216000000 | tf_op jit(solution)/shard_map/last/pallas_call | solution.py:1835
  301.2 7.3 %finish.1 = (f32[160,1536]{1,0:T(8,128)}, f32[160,1536]{1,0:T(8,128)}, f32[1536]{0:T(1024)}, f32[192,384]{1,0:T(8,128)}, f32[192,128]{1,0:T(8,128)}, /*index=5*/...) custom-call(f32[160,1536]{1,0:T(8,128)} %get-tuple-element.108.refs_, ...), custom_call_target="tpu_custom_call" | custom-call | bytes 21600000 | tf_op jit(solution)/shard_map/finish/pallas_call | solution.py:1909
  308.5 1.9 copy.26
Async XLA Ops:
  7.2 70.2 %all-gather.2.cloned.1.call-start = ((), (), s32[]{:S(2)}) async-start(), calls=%async_computation | async-start | bytes 2457600 | tf_op jit(solution)/shard_map/all_gather | solution.py:1946
Sparse Core Ops, SparseCore 0:
  9.6 22.9 all-gather.1
